TPU v7x, 256 devices: a whole 4x4x8 slice. The times are simulated.
256 devices in a mesh: lat: 32 (over x_lo, z, core), lev: 8 (over y, x_hi).
Axes of the slice: x: 4 (x_hi: 2, x_lo: 2; x = x_hi * 2 + x_lo), y: 4, z: 8, core: 2. Of those that a mesh axis runs over, the one named last changes fastest.
Arguments:
- adjoint_in: float32 [64, 512, 1440], P('lev', 'lat'), may hold values from -6 to 6
- courant_lon: float32 [64, 512, 1440], P('lev', 'lat'), may hold values from -0.9 to 0.9
- codes_lon: int32 [64, 512, 1440], P('lev', 'lat'), may hold values from 0 to 3
- courant_lat: float32 [64, 512, 1440], P('lev', 'lat'), may hold values from -0.9 to 0.9
- codes_lat: int32 [64, 512, 1440], P('lev', 'lat'), may hold values from 0 to 3
- courant_lev: float32 [64, 512, 1440], P(None, 'lat', 'lev'), may hold values from -0.9 to 0.9
- codes_lev: int32 [64, 512, 1440], P(None, 'lat', 'lev'), may hold values from 0 to 3
- block_inverse: float32 [512, 4, 16, 16], P('lat'), may hold values from -1 to 1.5
- block_lower: float32 [512, 3, 16, 16], P('lat'), may hold values from -0.6 to 0.6
- block_upper: float32 [512, 3, 16, 16], P('lat'), may hold values from -0.6 to 0.6
- region_ids: int32 [512, 1440], P('lat'), may hold values from 0 to 1999
- owner: int32 [2000], replicated, may hold values from 0 to 255, as said below
Outputs:
- adjoint_out: float32 [64, 512, 1440], P('lev', 'lat')
- region_sens: float32 [4096, 64], P(('lat', 'lev'))
Inputs may be any that keep to these rules, and one draw needn't show every extreme that they name: owner is a device index along lat+lev (lat slowest); no device owns more than 16 regions, and some device owns exactly 16.
All inputs are finite; a program needn't handle non-finite values.
Results may differ from a plain program's by a relative error of at most 0.0003.
Values sent between devices are 32-bit elements; how exact they have to be, the bound alone decides.
No kernel may reach another device: no remote copies, remote signals or barrier semaphores. Data moves between devices by JAX's collectives and lax.ppermute only.
A program may use at most 64 MiB of HBM per device.

v0:
```python
import jax
import jax.numpy as jnp
from jax import lax
from jax.sharding import PartitionSpec as P

SUB = 2
NREG = 2000


def padded(block, sides, width):
    for axis, dim in sides:
        count = lax.axis_size(axis)
        forward = [(i, i + 1) for i in range(count - 1)]
        backward = [(target, source) for source, target in forward]
        low = lax.ppermute(
            lax.slice_in_dim(block, block.shape[dim] - width, None, axis=dim), axis, forward
        )
        high = lax.ppermute(lax.slice_in_dim(block, 0, width, axis=dim), axis, backward)
        block = jnp.concatenate([low, block, high], axis=dim)
    return block


def pad_along(array, before_cells, after_cells, along, pad_mode):
    widths = [(0, 0)] * array.ndim
    widths[along] = (before_cells, after_cells)
    return jnp.pad(array, widths, mode=pad_mode)


def sweep_core(tracer, courant, codes, along):
    length = tracer.shape[along]

    def window(array, first_cell, end_cell):
        return lax.slice_in_dim(array, first_cell, end_cell, axis=along)

    centre = window(tracer, 1, length - 1)
    next_cell = window(tracer, 2, length)
    behind = window(tracer, 0, length - 2)
    slopes = jnp.where(
        codes == 1,
        next_cell - centre,
        jnp.where(
            codes == 2, centre - behind, jnp.where(codes == 3, 0.5 * (next_cell - behind), 0.0)
        ),
    )
    low_cell = window(tracer, 1, length - 2)
    up_cell = window(tracer, 2, length - 1)
    low_slope = window(slopes, 0, length - 3)
    up_slope = window(slopes, 1, length - 2)
    fluxes = jnp.maximum(courant, 0.0) * (
        low_cell + 0.5 * (1.0 - courant) * low_slope
    ) + jnp.minimum(courant, 0.0) * (up_cell - 0.5 * (1.0 + courant) * up_slope)
    return window(tracer, 2, length - 2) - (
        window(fluxes, 1, length - 3) - window(fluxes, 0, length - 4)
    )


def wall_forward(tracer, courant, codes, along):
    length = tracer.shape[along]
    inside = lax.broadcasted_iota(jnp.int32, courant.shape, along) < length - 1
    walled = jnp.where(inside, courant, 0.0)
    return sweep_core(
        pad_along(tracer, 2, 2, along, "constant"),
        pad_along(walled, 1, 0, along, "constant"),
        pad_along(codes, 1, 1, along, "constant"),
        along,
    )


def cycle_forward(tracer, courant, codes, along):
    return sweep_core(
        pad_along(tracer, 2, 2, along, "wrap"),
        pad_along(courant, 1, 0, along, "wrap"),
        pad_along(codes, 1, 1, along, "wrap"),
        along,
    )


def block_forward(source, inverses, lower_maps, upper_maps):
    size_block = inverses.shape[-1]
    block_total = inverses.shape[1]

    def apply_matrix(matrix, vector):
        return jnp.einsum("aij,jab->iab", matrix, vector, precision=lax.Precision.HIGHEST)

    solved = []
    for index in range(block_total):
        block_rhs = source[index * size_block : (index + 1) * size_block]
        if index > 0:
            block_rhs = block_rhs - apply_matrix(lower_maps[:, index - 1], solved[-1])
        solved.append(apply_matrix(inverses[:, index], block_rhs))
    result_blocks = [solved[-1]]
    for index in range(block_total - 2, -1, -1):
        result_blocks.insert(
            0, solved[index] - apply_matrix(upper_maps[:, index], result_blocks[0])
        )
    return jnp.concatenate(result_blocks, 0)


def transpose_of(forward, cotangent):
    return jax.vjp(forward, jnp.zeros_like(cotangent))[1](cotangent)[0]


def rows_adjoint(extended, courant_rows, code_rows):
    inner_rows = extended.shape[1] - 4
    zeros_field = jnp.zeros((extended.shape[0], inner_rows + 8, extended.shape[2]), extended.dtype)

    def forward(tracer):
        return sweep_core(tracer, courant_rows[:, :-1], code_rows, 1)

    gradient = jax.vjp(forward, zeros_field)[1](extended)[0]
    return gradient[:, 4 : inner_rows + 4]


def cycle_adjoint(adjoint, courant, codes):
    return transpose_of(lambda tracer: cycle_forward(tracer, courant, codes, 2), adjoint)


def slot_rows(owner, capacity):
    count = owner.shape[0]
    same_owner = owner[:, None] == owner[None, :]
    earlier = jnp.arange(count)[None, :] < jnp.arange(count)[:, None]
    slot_rank = jnp.sum((same_owner & earlier).astype(jnp.int32), axis=1)
    return owner * capacity + slot_rank


def region_totals(field, region_ids, region_count):
    levels_here = field.shape[0]
    band_major = jnp.transpose(field, (1, 0, 2))
    region_iota = lax.broadcasted_iota(jnp.int32, (1, region_count), 1)

    def add_band(total, inputs):
        band_field, band_ids = inputs
        matches = (band_ids[:, None] == region_iota).astype(jnp.float32)
        return (
            total
            + jnp.dot(
                band_field,
                matches,
                precision=lax.Precision.HIGHEST,
                preferred_element_type=jnp.float32,
            ),
            None,
        )

    start = jnp.zeros((levels_here, region_count), jnp.float32)
    total, unused = lax.scan(add_band, start, (band_major, region_ids))
    return total.T


def local(
    adjoint_in,
    courant_lon,
    codes_lon,
    courant_lat,
    codes_lat,
    courant_lev,
    codes_lev,
    block_inverse,
    block_lower,
    block_upper,
    region_ids,
    owner,
):
    levels_here, bands_here, lon_cells = adjoint_in.shape
    band_count = lax.axis_size("lat")
    group_count = lax.axis_size("lev")
    first_row = lax.axis_index("lat") * bands_here
    rows_here = first_row + lax.broadcasted_iota(jnp.int32, courant_lat.shape, 1)
    wall_courant = jnp.where(rows_here < bands_here * band_count - 1, courant_lat, 0.0)
    lat_codes = codes_lat.astype(jnp.float32)
    adjoint = adjoint_in
    for substep in range(SUB):
        if substep == 0:
            stacked = jnp.stack([adjoint, wall_courant, lat_codes])
            widened = padded(stacked, (("lat", 2),), 3)
            courant_rows = widened[1]
            code_rows = widened[2]
            extended = widened[0][:, 1:-1]
        else:
            extended = padded(adjoint, (("lat", 1),), 2)
        adjoint = rows_adjoint(extended, courant_rows, code_rows)
        adjoint = cycle_adjoint(adjoint, courant_lon, codes_lon)
    columns_view = lax.all_to_all(adjoint, "lev", split_axis=2, concat_axis=0, tiled=True)
    columns_view = transpose_of(
        lambda tracer: block_forward(tracer, block_inverse, block_lower, block_upper), columns_view
    )
    columns_view = transpose_of(
        lambda tracer: wall_forward(tracer, courant_lev, codes_lev, 0), columns_view
    )
    adjoint_out = lax.all_to_all(columns_view, "lev", split_axis=0, concat_axis=2, tiled=True)
    devices = band_count * group_count
    capacity = (2 * NREG + devices - 1) // devices
    weight_scale = (NREG / (bands_here * band_count * lon_cells)) ** 0.5
    region_sums = region_totals(adjoint_out, region_ids, NREG) * weight_scale
    row_index = slot_rows(owner, capacity)
    placed = jnp.zeros((NREG, levels_here * group_count), jnp.float32)
    placed = lax.dynamic_update_slice_in_dim(
        placed, region_sums, lax.axis_index("lev") * levels_here, 1
    )
    region_terms = (
        jnp.zeros((devices * capacity, levels_here * group_count), jnp.float32)
        .at[row_index]
        .set(placed)
    )
    region_sens = lax.psum_scatter(region_terms, ("lat", "lev"), scatter_dimension=0, tiled=True)
    return (adjoint_out, region_sens)


def solution(mesh):
    placed = (
        P("lev", "lat", None),
        P("lev", "lat", None),
        P("lev", "lat", None),
        P("lev", "lat", None),
        P("lev", "lat", None),
        P(None, "lat", "lev"),
        P(None, "lat", "lev"),
        P("lat", None, None, None),
        P("lat", None, None, None),
        P("lat", None, None, None),
        P("lat", None),
        P(),
    )
    return jax.shard_map(
        local,
        mesh=mesh,
        in_specs=placed,
        out_specs=(P("lev", "lat", None), P(("lat", "lev"), None)),
        check_vma=False,
    )
```

profile of v0, /device:TPU:128, one launch (start us, length us, event | category | flops | bytes accessed | tf_op | source)
XLA Modules:
  0.0 1525.6 jit_solution(8351296290861719215)
XLA Ops:
  13.0 4.9 collective-permute-start.1
  33.7 5.4 collective-permute-start.3
  45.7 4.0 copy.73
  49.7 5.3 reshape.30
  55.0 7.1 all-to-all-start
  64.6 10.3 all-to-all-done
  79.8 4.5 reshape.31
  84.3 5.1 copy.74
  103.0 13.7 all-to-all-done.1
  118.2 75.3 %while.11 = (s32[]{:T(128)}, f32[8,2000]{1,0:T(8,128)S(1)}, f32[16,8,1440]{2,0,1:T(8,128)S(1)}, s32[16,1440]{1,0:T(8,128)}, s32[]{:T(128)}, /*index=5*/s32[]{:T(128)}) while((s32[]{:T(128)}, f32[8,2000]{1,0:T(8,128)S(1)}, f32[16,8,1440]{2,0,1:T(8,128)S(1)}, s32[16,1440]{1,0:T(8,128)}, s32[]{:T(128)}, /*index=5*/s32[]{:T(128)}) %tuple.95), condition=%wide.region_2.3_spmd.clone, body=%wide.region_1.2_spmd.clone.sunk | while | flops 279392000 | bytes 283607 | solution.py:146
  119.3 3.8 fusion.73
  133.3 3.8 fusion.73
  138.0 3.8 fusion.73
  142.7 3.8 fusion.73
  147.4 3.8 fusion.73
  152.1 3.8 fusion.73
  156.8 3.8 fusion.73
  161.5 3.8 fusion.73
  166.2 3.8 fusion.73
  180.3 3.8 fusion.73
  185.0 3.8 fusion.73
  193.9 7.6 dynamic_update_slice.3
  201.5 9.5 scatter_custom_fusion
  211.0 1307.5 %reduce-scatter.2.cloned.1.call-done = f32[16,64]{1,0:T(8,128)} async-done(((f32[4096,64]{1,0:T(8,128)}), f32[16,64]{1,0:T(8,128)}) %reduce-scatter.2.cloned.1.call-update) | async-done | bytes 4112 | tf_op jit(solution)/shard_map/reduce_scatter | solution.py:205
  (134 shorter events, 83.8 us)
Async XLA Ops:
  7.2 1.7 copy-start.7
  7.2 1.7 copy-start.8
  9.9 7.9 copy-start.5
  10.9 7.5 copy-start.6
  10.9 11.3 collective-permute-start
  13.0 11.0 collective-permute-start.1
  18.8 0.9 copy-start
  27.8 1.1 copy-start.1
  31.7 7.4 collective-permute-start.2
  33.7 7.2 collective-permute-start.3
  55.0 7.1 copy-start.4
  55.0 19.9 %all-to-all-start = ((f32[8,1,23040]{2,1,0:T(1,128)}), f32[8,1,23040]{2,1,0:T(1,128)S(1)}, u32[]{:S(2)}, u32[]{:S(2)}) async-start(f32[8,1,23040]{2,1,0:T(1,128)} %reshape.30), calls=%async_computation | async-start | bytes 1474560 | tf_op jit(solution)/shard_map/all_to_all | solution.py:183
  74.9 0.9 copy-start.2
  84.3 5.1 copy-start.10
  89.4 1.4 copy-start.9
  89.9 1.4 copy-start.11
  97.8 3.7 copy-start.13
  97.8 18.9 %all-to-all-start.1 = ((f32[64,16,180]{2,1,0:T(8,128)}), f32[64,16,180]{2,1,0:T(8,128)S(1)}, u32[]{:S(2)}, u32[]{:S(2)}) async-start(f32[64,16,180]{2,1,0:T(8,128)} %copy.87), calls=%async_computation.1 | async-start | bytes 2097152 | tf_op jit(solution)/shard_map/all_to_all | solution.py:190
  101.5 1417.0 %reduce-scatter.2.cloned.1.call-start = ((), (), s32[]{:S(2)}) async-start(), calls=%async_computation.3 | async-start | bytes 2105344 | tf_op jit(solution)/shard_map/reduce_scatter | solution.py:205
  117.3 0.8 copy-start.12
  193.5 8.0 copy-start.3
Sparse Core Ops, SparseCore 0:
  211.1 1307.3 reduce-scatter.1
where the time goes:
time: 1530 us
  waiting for transfers between devices  1340 us (88%)
  matrix products  65.3 us (4%)
  local copies, waits for them, and re-layouts  60.4 us (4%)
  starting transfers between devices  25.1 us (2%)
  other arithmetic  24.6 us (2%)
    reduce_scatter x1, waiting for transfers between devices, local(): lax.psum_scatter(region_terms, ('lat', 'lev'), scatter_dimension=0, tiled...  1310 us
    dot_general x16, matrix products, add_band(): jnp.dot(band_field, matches, precision=lax.Precision.HIGHEST, preferred_e...  60.9 us
  transfers between devices with their start and end apart: 7, of which 5 were waited for; matrix products, arithmetic and copies ran while one was open for 0% of the time, Pallas kernels for 0%

commit v1 on v0

v1 whole, which is shorter than its diff:
```python
import functools

import jax
import jax.numpy as jnp
from jax import lax
from jax.experimental import pallas as pl
from jax.experimental.pallas import tpu as pltpu
from jax.sharding import PartitionSpec as P

SUB = 2
SLOTS = 16
LANES = 128
F32 = jnp.float32
BF16 = jnp.bfloat16
VMEM = pl.BlockSpec(memory_space=pltpu.VMEM)
SMEM = pl.BlockSpec(memory_space=pltpu.SMEM)
NT = (((1,), (1,)), ((), ()))


def params():
    return pltpu.CompilerParams(vmem_limit_bytes=40 * 2**20)


def flux_parts(courant):
    up = jnp.maximum(courant, 0.0)
    down = jnp.minimum(courant, 0.0)
    half = 0.5 * courant
    return up, down, up * (0.5 - half), down * (0.5 + half)


def slope_parts(codes):
    centred = jnp.where(codes == 3, 0.5, 0.0)
    ahead = jnp.where(codes == 1, 1.0, centred)
    behind = jnp.where(codes == 2, 1.0, centred)
    return ahead, behind


def split(value):
    high = value.astype(BF16)
    low = (value - high.astype(F32)).astype(BF16)
    return high, low


def roll(value, shift, axis):
    return pltpu.roll(value, shift % value.shape[axis], axis)


def wrapped(value, width):
    length = value.shape[1]
    spare = width - length
    first = spare // 2
    return jnp.concatenate([value, value[:, :first], value[:, length - spare + first :]], axis=1)


def horizontal_kernel(
    last_ref, a_ref, clat_ref, klat_ref, clon_ref, klon_ref, below_ref, above_ref, bcoef_ref, acoef_ref, *refs, final
):
    if final:
        send_ref, edge_w, edge_q, edge_a, edge_r, rows_ref = refs
    else:
        out_ref, up_ref, down_ref, edge_w, edge_q, edge_a, edge_r, rows_ref = refs
    levels, rows, lons = a_ref.shape
    width = rows_ref.shape[2]
    last = last_ref[0]
    a0 = a_ref[:, 0, :]
    am1, am2 = below_ref[0], below_ref[1]
    up1, down1, uph1, downh1 = flux_parts(bcoef_ref[0])
    _, _, _, downh2 = flux_parts(bcoef_ref[1])
    ahead1, _ = slope_parts(bcoef_ref[2])
    f1 = a0 - am1
    f2 = am1 - am2
    s1 = uph1 * f1 - downh2 * f2
    edge_w[...] = downh1 * f1
    edge_q[...] = down1 * f1 + ahead1 * s1
    a_in = a_ref[:, rows - 1, :]
    a16, a17 = above_ref[0], above_ref[1]
    c15 = jnp.where(last == 1, 0.0, clat_ref[:, rows - 1, :])
    _, _, _, downh15 = flux_parts(c15)
    _, _, uph16, _ = flux_parts(acoef_ref[0])
    _, behind16 = slope_parts(acoef_ref[1])
    edge_a[...] = a16
    edge_r[...] = behind16 * (uph16 * (a17 - a16) - downh15 * (a16 - a_in))

    step = 4 * LANES
    chunks = [(start, min(step, lons - start)) for start in range(0, lons, step)]
    tile = 8

    def level(l, carry):
        for start, size in chunks:
            cols = slice(start, start + size)
            row = lax.broadcasted_iota(jnp.int32, (rows, size), 0)
            lowest, highest = row == 0, row == rows - 1
            a = a_ref[l, :, cols]
            courant = jnp.where(highest & (last == 1), 0.0, clat_ref[l, :, cols])
            up, down, uph, downh = flux_parts(courant)
            ahead, behind = slope_parts(klat_ref[l, :, cols])

            def edge(ref):
                return ref[pl.ds(l, 1), cols]

            f = jnp.where(highest, edge(edge_a), roll(a, -1, 0)) - a
            s = uph * f - jnp.where(lowest, edge(edge_w), roll(downh * f, 1, 0))
            q = jnp.where(lowest, edge(edge_q), roll(down * f + ahead * s, 1, 0))
            r = jnp.where(highest, edge(edge_r), roll(behind * s, -1, 0))
            rows_ref[0, :, cols] = a + up * f + (behind - ahead) * s + q - r
        for low in range(0, rows, tile):
            band = slice(low, low + tile)
            a = wrapped(rows_ref[0, band, :lons], width)
            up, down, uph, downh = flux_parts(wrapped(clon_ref[l, band, :], width))
            ahead, behind = slope_parts(wrapped(klon_ref[l, band, :], width))
            f = roll(a, -1, 1) - a
            s = uph * f - roll(downh * f, 1, 1)
            q = roll(down * f + ahead * s, 1, 1)
            r = roll(behind * s, -1, 1)
            value = a + up * f + (behind - ahead) * s + q - r
            if final:
                parts = send_ref.shape[0]
                share = lons // parts
                for part in range(parts):
                    send_ref[part, l, band, :] = value[:, part * share : (part + 1) * share]
            else:
                out_ref[l, band, :] = value[:, :lons]
        return carry

    lax.fori_loop(0, levels, level, 0)
    if not final:
        up_ref[0] = out_ref[:, rows - 1, :]
        up_ref[1] = out_ref[:, rows - 2, :]
        down_ref[0] = out_ref[:, 0, :]
        down_ref[1] = out_ref[:, 1, :]


def horizontal(last, a, clat, klat, clon, klon, below, above, bcoef, acoef, parts):
    levels, rows, lons = a.shape
    width = -(-lons // LANES) * LANES
    final = parts > 0
    if final:
        out_shape = jax.ShapeDtypeStruct((parts, levels, rows, lons // parts), F32)
    else:
        edge = jax.ShapeDtypeStruct((2, levels, lons), F32)
        out_shape = (jax.ShapeDtypeStruct(a.shape, F32), edge, edge)
    return pl.pallas_call(
        functools.partial(horizontal_kernel, final=final),
        out_shape=out_shape,
        in_specs=[SMEM] + [VMEM] * 9,
        out_specs=VMEM if final else (VMEM, VMEM, VMEM),
        scratch_shapes=[pltpu.VMEM((levels, lons), F32)] * 4 + [pltpu.VMEM((1, rows, width), F32)],
        compiler_params=params(),
        name="horizontal",
    )(last, a, clat, klat, clon, klon, below, above, bcoef, acoef)


def prep_kernel(inverse_ref, lower_ref, upper_ref, owner_ref, matrix_ref, slot_ref, *, devices):
    lats, blocks, size, _ = inverse_ref.shape
    group = LANES // size
    levels = blocks * size
    row = lax.broadcasted_iota(jnp.int32, (LANES, LANES), 0)
    col = lax.broadcasted_iota(jnp.int32, (LANES, LANES), 1)
    diagonal = (row // size) == (col // size)
    row_l = lax.broadcasted_iota(jnp.int32, (LANES, levels), 0)
    col_l = lax.broadcasted_iota(jnp.int32, (LANES, levels), 1)

    def times(matrix, vector):
        wide = jnp.concatenate([matrix.reshape(LANES, size)] * group, axis=1)
        wide = jnp.where(diagonal, wide, 0.0)
        return jnp.dot(wide, vector, precision=lax.Precision.HIGHEST, preferred_element_type=F32)

    for first in range(0, lats, group):
        lat = slice(first, first + group)
        solved = []
        for k in range(blocks):
            rhs = jnp.where(col_l == row_l % size + size * k, 1.0, 0.0)
            if k > 0:
                rhs = rhs - times(lower_ref[lat, k - 1], solved[-1])
            solved.append(times(inverse_ref[lat, k], rhs))
        result = [solved[-1]]
        for k in range(blocks - 2, -1, -1):
            result.insert(0, solved[k] - times(upper_ref[lat, k], result[0]))
        for g in range(group):
            dense = jnp.concatenate([block[g * size : (g + 1) * size] for block in result], axis=0)
            high, low = split(dense.T)
            matrix_ref[first + g] = jnp.concatenate([high, low, high], axis=1)

    tiles = owner_ref.shape[0]
    device = lax.broadcasted_iota(jnp.int32, (devices, LANES), 0)
    earlier = jnp.where(row < col, 1.0, 0.0).astype(BF16)
    running = jnp.zeros((devices, 1), F32)
    for t in range(tiles):
        owned = jnp.where(owner_ref[pl.ds(t, 1), :] == device, 1.0, 0.0)
        before = jnp.dot(owned.astype(BF16), earlier, preferred_element_type=F32) + running
        slot_ref[pl.ds(t, 1), :] = jnp.sum(owned * before, axis=0, keepdims=True).astype(jnp.int32)
        running = running + jnp.sum(owned, axis=1, keepdims=True)


def prep(inverse, lower, upper, owner_tiles, devices):
    lats, blocks, size, _ = inverse.shape
    levels = blocks * size
    return pl.pallas_call(
        functools.partial(prep_kernel, devices=devices),
        out_shape=(
            jax.ShapeDtypeStruct((lats, levels, 3 * levels), BF16),
            jax.ShapeDtypeStruct(owner_tiles.shape, jnp.int32),
        ),
        in_specs=[VMEM] * 4,
        out_specs=(VMEM, VMEM),
        compiler_params=params(),
        name="prep",
    )(inverse, lower, upper, owner_tiles)


def vertical_kernel(x_ref, matrix_ref, c_ref, k_ref, out_ref, y_ref):
    levels, rows, _ = x_ref.shape
    for lat in range(rows):
        high, low = split(x_ref[:, lat, :])
        stacked = jnp.concatenate([high, high, low], axis=0)
        y_ref[:, lat, :] = jnp.dot(matrix_ref[lat], stacked, preferred_element_type=F32)
    zero = jnp.zeros(x_ref.shape[1:], F32)
    y = y_ref[0]
    prior_w, prior_q, pending = zero, zero, None
    for i in range(levels):
        ahead, behind = slope_parts(k_ref[i])
        if i < levels - 1:
            up, down, uph, downh = flux_parts(c_ref[i])
            y_next = y_ref[i + 1]
            f = y_next - y
            s = uph * f - prior_w
            here = y + up * f + prior_q
            prior_w = downh * f
            prior_q = down * f + ahead * s
        else:
            y_next = None
            s = -prior_w
            here = y + prior_q
        here = here + (behind - ahead) * s
        if i > 0:
            out_ref[i - 1] = pending - behind * s
        pending = here
        y = y_next
    out_ref[levels - 1] = pending


def vertical(x, matrix, courant, codes):
    return pl.pallas_call(
        vertical_kernel,
        out_shape=jax.ShapeDtypeStruct(x.shape, F32),
        in_specs=[VMEM] * 4,
        out_specs=VMEM,
        scratch_shapes=[pltpu.VMEM(x.shape, F32)],
        compiler_params=params(),
        name="vertical",
    )(x, matrix, courant, codes)


def region_kernel(field_ref, ids_ref, owner_ref, slot_ref, out_ref, send_ref, high_ref, low_ref, acc_ref, table_ref, *, scale):
    parts, levels, rows, share = field_ref.shape
    tiles = owner_ref.shape[0]
    devices = send_ref.shape[0]
    lons = parts * share
    for l in range(levels):
        whole = jnp.concatenate([field_ref[part, l] for part in range(parts)], axis=1)
        out_ref[l] = whole
        high = whole.astype(BF16).astype(F32)
        high_ref[l] = high
        low_ref[l] = whole - high
    acc_ref[...] = jnp.zeros_like(acc_ref)
    coarse = lax.broadcasted_iota(jnp.int32, (tiles, lons), 0)
    fine = lax.broadcasted_iota(jnp.int32, (LANES, lons), 0)

    def band(lat, carry):
        ids = ids_ref[pl.ds(lat, 1), :]
        mask = (ids // LANES) == coarse
        onehot = jnp.where((ids % LANES) == fine, 1.0, 0.0).astype(BF16)
        pieces = []
        for ref in (high_ref, low_ref):
            for l in range(levels):
                pieces.append(jnp.where(mask, ref[l, pl.ds(lat, 1), :], 0.0).astype(BF16))
        stacked = jnp.concatenate(pieces, axis=0)
        acc_ref[...] += lax.dot_general(stacked, onehot, NT, preferred_element_type=F32)
        return carry

    lax.fori_loop(0, rows, band, 0)
    half = levels * tiles
    table_ref[...] = acc_ref[pl.ds(0, half), :] + acc_ref[pl.ds(half, half), :]
    device = lax.broadcasted_iota(jnp.int32, (devices, LANES), 0)
    place = lax.broadcasted_iota(jnp.int32, (SLOTS * levels, LANES), 0) // levels
    total = jnp.zeros((devices, SLOTS * levels), F32)
    for t in range(tiles):
        owned = jnp.where(owner_ref[pl.ds(t, 1), :] == device, 1.0, 0.0).astype(BF16)
        sums = table_ref[pl.ds(t, levels, stride=tiles), :]
        spread = jnp.where(slot_ref[pl.ds(t, 1), :] == place, jnp.concatenate([sums] * SLOTS, axis=0), 0.0)
        for piece in split(spread):
            total += lax.dot_general(owned, piece, NT, preferred_element_type=F32)
    send_ref[...] = total * scale


def regions(field, ids, owner_tiles, slot_tiles, devices, scale):
    parts, levels, rows, share = field.shape
    tiles = owner_tiles.shape[0]
    lons = parts * share
    return pl.pallas_call(
        functools.partial(region_kernel, scale=scale),
        out_shape=(
            jax.ShapeDtypeStruct((levels, rows, lons), F32),
            jax.ShapeDtypeStruct((devices, SLOTS * levels), F32),
        ),
        in_specs=[VMEM] * 4,
        out_specs=(VMEM, VMEM),
        scratch_shapes=[
            pltpu.VMEM((levels, rows, lons), F32),
            pltpu.VMEM((levels, rows, lons), F32),
            pltpu.VMEM((2 * levels * tiles, LANES), F32),
            pltpu.VMEM((levels * tiles, LANES), F32),
        ],
        compiler_params=params(),
        name="regions",
    )(field, ids, owner_tiles, slot_tiles)


def neighbours(up, down):
    count = lax.axis_size("lat")
    forward = [(i, i + 1) for i in range(count - 1)]
    backward = [(target, source) for source, target in forward]
    return lax.ppermute(up, "lat", forward), lax.ppermute(down, "lat", backward)


def local(
    adjoint_in,
    courant_lon,
    codes_lon,
    courant_lat,
    codes_lat,
    courant_lev,
    codes_lev,
    block_inverse,
    block_lower,
    block_upper,
    region_ids,
    owner,
):
    levels_here, bands_here, lon_cells = adjoint_in.shape
    band_count = lax.axis_size("lat")
    group_count = lax.axis_size("lev")
    devices = band_count * group_count
    region_count = owner.shape[0]
    tiles = -(-region_count // LANES)
    tiles = -(-tiles // 8) * 8
    owner_tiles = jnp.pad(owner, (0, tiles * LANES - region_count), constant_values=-1).reshape(tiles, LANES)
    matrix, slot_tiles = prep(block_inverse, block_lower, block_upper, owner_tiles, devices)
    last = (lax.axis_index("lat") == band_count - 1).astype(jnp.int32).reshape(1)
    edge = bands_here - 1
    up = jnp.stack(
        [
            adjoint_in[:, edge],
            adjoint_in[:, edge - 1],
            courant_lat[:, edge],
            courant_lat[:, edge - 1],
            codes_lat[:, edge].astype(F32),
        ]
    )
    down = jnp.stack([adjoint_in[:, 0], adjoint_in[:, 1], courant_lat[:, 0], codes_lat[:, 0].astype(F32)])
    below, above = neighbours(up, down)
    coefficients = (courant_lat, codes_lat, courant_lon, codes_lon)
    adjoint, up, down = horizontal(
        last, adjoint_in, *coefficients, below[:2], above[:2], below[2:], above[2:], 0
    )
    below_next, above_next = neighbours(up, down)
    sent = horizontal(
        last, adjoint, *coefficients, below_next, above_next, below[2:], above[2:], group_count
    )
    columns = lax.all_to_all(sent, "lev", split_axis=0, concat_axis=0, tiled=True)
    columns = columns.reshape(group_count * levels_here, bands_here, lon_cells // group_count)
    columns = vertical(columns, matrix, courant_lev, codes_lev)
    columns = columns.reshape(group_count, levels_here, bands_here, lon_cells // group_count)
    field = lax.all_to_all(columns, "lev", split_axis=0, concat_axis=0, tiled=True)
    scale = (region_count / (bands_here * band_count * lon_cells)) ** 0.5
    adjoint_out, rows = regions(field, region_ids, owner_tiles, slot_tiles, devices, scale)
    rows = lax.all_to_all(rows, ("lat", "lev"), split_axis=0, concat_axis=0, tiled=True)
    rows = jnp.sum(rows.reshape(band_count, group_count, SLOTS, levels_here), axis=0)
    region_sens = jnp.transpose(rows, (1, 0, 2)).reshape(SLOTS, group_count * levels_here)
    return (adjoint_out, region_sens)


def solution(mesh):
    placed = (
        P("lev", "lat", None),
        P("lev", "lat", None),
        P("lev", "lat", None),
        P("lev", "lat", None),
        P("lev", "lat", None),
        P(None, "lat", "lev"),
        P(None, "lat", "lev"),
        P("lat", None, None, None),
        P("lat", None, None, None),
        P("lat", None, None, None),
        P("lat", None),
        P(),
    )
    return jax.shard_map(
        local,
        mesh=mesh,
        in_specs=placed,
        out_specs=(P("lev", "lat", None), P(("lat", "lev"), None)),
        check_vma=False,
    )
```

time: 1530 us -> 122 us (0.08)
  the two profiles are of different devices: /device:TPU:128 before, /device:TPU:1 now
where the time goes in v1:
time: 122 us; the launch traced here: 121 us
  blocking collectives  45.5 us (37%)
  Pallas kernels  25.4 us (21%)
  starting transfers between devices  20 us (16%)
  waiting for transfers between devices  15.1 us (12%)
  local copies, waits for them, and re-layouts  12.9 us (11%)
    all_to_all x1, blocking collectives, local(): lax.all_to_all(rows, ('lat', 'lev'), split_axis=0, concat_axis=0, tiled=T...  25.8 us
    all_to_all x1, blocking collectives, local(): lax.all_to_all(columns, 'lev', split_axis=0, concat_axis=0, tiled=True)  19.8 us
    pallas_call x2, Pallas kernels, horizontal(): pl.pallas_call(functools.partial(horizontal_kernel, final=final), out_sha...  8.26 us
    all_to_all x1, waiting for transfers between devices, local(): lax.all_to_all(sent, 'lev', split_axis=0, concat_axis=0, tiled=True)  8.02 us
    pallas_call x1, Pallas kernels, regions(): pl.pallas_call(functools.partial(region_kernel, scale=scale), out_shape=(...  8.01 us
    ppermute x2, starting transfers between devices, neighbours(): lax.ppermute(down, 'lat', backward)  7.07 us
    unnamed x34, local copies, waits for them, and re-layouts  6.87 us
    all_to_all x1, starting transfers between devices, local(): lax.all_to_all(sent, 'lev', split_axis=0, concat_axis=0, tiled=True)  6.57 us
  transfers between devices with their start and end apart: 5, of which 4 were waited for; matrix products, arithmetic and copies ran while one was open for 0% of the time, Pallas kernels for 4%

profile of v1, /device:TPU:1, one launch (start us, length us, event | category | flops | bytes accessed | tf_op | source)
XLA Modules:
  0.0 120.9 jit_solution(1370953698595458993)
XLA Ops:
  0.7 1.3 %fusion.9 = (s32[8,1,1440]{2,1,0:T(1,128)S(1)}, s32[8,1,1440]{2,1,0:T(1,128)S(1)}) fusion(s32[8,16,1440]{2,1,0:T(8,128)} %klat_ref.3), kind=kLoop, calls=%fused_computation.20 | loop fusion | bytes 184320 | tf_op jit(solution)/shard_map/slice | solution.py:360
  2.0 1.4 %fusion.8 = (f32[8,1,1440]{2,1,0:T(1,128)S(1)}, f32[8,1,1440]{2,1,0:T(1,128)S(1)}, f32[8,1,1440]{2,1,0:T(1,128)S(1)}) fusion(f32[8,16,1440]{2,1,0:T(8,128)} %clat_ref.3), kind=kLoop, calls=%fused_computation.19 | loop fusion | bytes 276480 | tf_op jit(solution)/shard_map/slice | solution.py:360
  3.4 1.5 %fusion.7 = (f32[8,1,1440]{2,1,0:T(1,128)S(1)}, f32[8,1,1440]{2,1,0:T(1,128)S(1)}, f32[8,1,1440]{2,1,0:T(1,128)S(1)}, f32[8,1,1440]{2,1,0:T(1,128)S(1)}) fusion(f32[8,16,1440]{2,1,0:T(8,128)} %a_ref.1), kind=kLoop, calls=%fused_computation.18 | loop fusion | bytes 368640 | tf_op jit(solution)/shard_map/slice | solution.py:360
  5.0 5.1 %collective-permute-start.1 = (f32[4,8,1440]{2,1,0:T(8,128)S(1)}, f32[4,8,1440]{2,1,0:T(8,128)S(1)}, u32[]{:S(2)}, u32[]{:S(2)}) collective-permute-start(f32[4,8,1440]{2,1,0:T(8,128)S(1)} %pad_maximum_fusion), channel_id=1, source_target_pairs={{8,0},{16,8},{24,16},{32,24},{40,32},{48,40},{56,48},{64,56},{72,6... | collective-permute-start | bytes 552968 | tf_op jit(solution)/shard_map/ppermute | solution.py:323
  10.2 1.9 %collective-permute-start = (f32[5,8,1440]{2,1,0:T(8,128)S(1)}, f32[5,8,1440]{2,1,0:T(8,128)S(1)}, u32[]{:S(2)}, u32[]{:S(2)}) collective-permute-start(f32[5,8,1440]{2,1,0:T(8,128)S(1)} %fusion.2), channel_id=1, source_target_pairs={{0,8},{8,16},{16,24},{24,32},{32,40},{40,48},{48,56},{56,64},{64,7... | collective-permute-start | bytes 691208 | tf_op jit(solution)/shard_map/ppermute | solution.py:323
  12.1 1.1 collective-permute-done.1
  13.3 2.0 %collective-permute-done = f32[5,8,1440]{2,1,0:T(8,128)S(1)} collective-permute-done((f32[5,8,1440]{2,1,0:T(8,128)S(1)}, f32[5,8,1440]{2,1,0:T(8,128)S(1)}, u32[]{:S(2)}, u32[]{:S(2)}) %collective-permute-start) | collective-permute-done | bytes 230432 | tf_op jit(solution)/shard_map/ppermute | solution.py:323
  15.3 1.1 copy-done.3
  16.4 1.1 copy-done.4
  17.6 3.3 %horizontal.2 = (f32[8,16,1440]{2,1,0:T(8,128)S(1)}, f32[2,8,1440]{2,1,0:T(8,128)S(1)}, f32[2,8,1440]{2,1,0:T(8,128)S(1)}) custom-call(s32[1]{0:T(128)} %bitcast.last_ref, f32[8,16,1440]{2,1,0:T(8,128)S(1)} %copy-done.4, f32[8,16,1440]{2,1,0:T(8,128)S(1)} %copy-done, s32[8,16,1440]{2,1,0:T(8,128)S(1)} %copy-done.1, f32[8,16,1440]{2,1,0:T(8,128)S(1)} %copy-done.2, ...), custom_call_target="tpu_custom_call" | custom-call | tf_op jit(solution)/shard_map/horizontal/pallas_call | solution.py:142
  20.9 4.4 %collective-permute-start.2 = (f32[2,8,1440]{2,1,0:T(8,128)S(1)}, f32[2,8,1440]{2,1,0:T(8,128)S(1)}, u32[]{:S(2)}, u32[]{:S(2)}) collective-permute-start(f32[2,8,1440]{2,1,0:T(8,128)S(1)} %get-tuple-element.10), channel_id=1, source_target_pairs={{0,8},{8,16},{16,24},{24,32},{32,40},{40,48},{48,56},{56,64},{64,7... | collective-permute-start | bytes 276488 | tf_op jit(solution)/shard_map/ppermute | solution.py:323
  25.3 1.9 %collective-permute-start.3 = (f32[2,8,1440]{2,1,0:T(8,128)S(1)}, f32[2,8,1440]{2,1,0:T(8,128)S(1)}, u32[]{:S(2)}, u32[]{:S(2)}) collective-permute-start(f32[2,8,1440]{2,1,0:T(8,128)S(1)} %get-tuple-element.11), channel_id=1, source_target_pairs={{8,0},{16,8},{24,16},{32,24},{40,32},{48,40},{56,48},{64,56},{72,6... | collective-permute-start | bytes 276488 | tf_op jit(solution)/shard_map/ppermute | solution.py:323
  27.3 4.0 %collective-permute-done.3.above_ref = f32[2,8,1440]{2,1,0:T(8,128)S(1)} collective-permute-done((f32[2,8,1440]{2,1,0:T(8,128)S(1)}, f32[2,8,1440]{2,1,0:T(8,128)S(1)}, u32[]{:S(2)}, u32[]{:S(2)}) %collective-permute-start.3) | collective-permute-done | bytes 92192 | tf_op jit(solution)/shard_map/ppermute | solution.py:323
  31.3 4.9 %horizontal.3 = f32[8,8,16,180]{3,2,1,0:T(8,128)} custom-call(s32[1]{0:T(128)} %bitcast.last_ref, f32[8,16,1440]{2,1,0:T(8,128)S(1)} %get-tuple-element.9.a_ref, f32[8,16,1440]{2,1,0:T(8,128)S(1)} %copy-done, s32[8,16,1440]{2,1,0:T(8,128)S(1)} %copy-done.1, f32[8,16,1440]{2,1,0:T(8,128)S(1)} %copy-done.2, s32[8,16,1440]{2,1,0:T(8,128)S(1)} %copy-done.3, ...), custom_call_target="tpu_custom_call" | custom-call | tf_op jit(solution)/shard_map/horizontal/pallas_call | solution.py:142
  36.2 6.6 %all-to-all-start = ((f32[8,8,16,180]{3,2,1,0:T(8,128)}), f32[8,8,16,180]{3,2,1,0:T(8,128)S(1)}, u32[]{:S(2)}, u32[]{:S(2)}) async-start(f32[8,8,16,180]{3,2,1,0:T(8,128)} %horizontal.3), calls=%async_computation | async-start | bytes 2097152 | tf_op jit(solution)/shard_map/all_to_all | solution.py:370
  42.8 1.0 copy-done.9
  44.8 4.6 %prep.1 = (bf16[16,64,192]{2,1,0:T(8,128)(2,1)S(1)}, s32[16,128]{1,0:T(8,128)S(1)}) custom-call(f32[16,4,16,16]{3,2,1,0:T(8,128)S(1)} %copy-done.9, f32[16,3,16,16]{3,2,1,0:T(8,128)S(1)} %copy-done.10, f32[16,3,16,16]{3,2,1,0:T(8,128)S(1)} %copy-done.11, s32[16,128]{1,0:T(8,128)S(1)} %pad_bitcast_fusion.owner_ref), custom_call_target="tpu_custom_call" | custom-call | tf_op jit(solution)/shard_map/prep/pallas_call | solution.py:198
  50.2 8.0 %all-to-all-done = f32[8,8,16,180]{3,2,1,0:T(8,128)S(1)} async-done(((f32[8,8,16,180]{3,2,1,0:T(8,128)}), f32[8,8,16,180]{3,2,1,0:T(8,128)S(1)}, u32[]{:S(2)}, u32[]{:S(2)}) %all-to-all-start) | async-done | bytes 737312 | tf_op jit(solution)/shard_map/all_to_all | solution.py:370
  58.2 1.0 copy-done.8
  59.3 4.6 %vertical.1 = f32[64,16,180]{2,1,0:T(8,128)S(1)} custom-call(f32[64,16,180]{2,1,0:T(8,128)S(1)} %bitcast.39, bf16[16,64,192]{2,1,0:T(8,128)(2,1)S(1)} %copy-done.8, f32[64,16,180]{2,1,0:T(8,128)S(1)} %copy-done.5, s32[64,16,180]{2,1,0:T(8,128)S(1)} %copy-done.6), custom_call_target="tpu_custom_call" | custom-call | tf_op jit(solution)/shard_map/vertical/pallas_call | solution.py:243
  63.9 19.8 %all_to_all.19.field_ref = f32[8,8,16,180]{3,2,1,0:T(8,128)S(1)} all-to-all(f32[8,8,16,180]{3,2,1,0:T(8,128)S(1)} %bitcast.40), channel_id=1, replica_groups=mesh['lat'=32,'lev'=8] {'lev'}, dimensions={0} | all-to-all | bytes 1474560 | tf_op jit(solution)/shard_map/all_to_all | solution.py:374
  83.6 8.0 %regions.1 = (f32[8,16,1440]{2,1,0:T(8,128)}, f32[256,128]{1,0:T(8,128)S(1)}) custom-call(f32[8,8,16,180]{3,2,1,0:T(8,128)S(1)} %all_to_all.19.field_ref, s32[16,1440]{1,0:T(8,128)S(1)} %copy-done.12, s32[16,128]{1,0:T(8,128)S(1)} %pad_bitcast_fusion.owner_ref, s32[16,128]{1,0:T(8,128)S(1)} %get-tuple-element.13.slot_ref), custom_call_target="tpu_custom_call" | custom-call | tf_op jit(solution)/shard_map/regions/pallas_call | solution.py:300
  91.7 25.8 %all_to_all.20 = f32[256,1,128]{2,1,0:T(1,128)S(1)} all-to-all(f32[256,1,128]{2,1,0:T(1,128)S(1)} %bitcast.41), channel_id=1, replica_groups=mesh['lat'=32,'lev'=8] {'lat','lev'}, dimensions={0} | all-to-all | bytes 262144 | tf_op jit(solution)/shard_map/all_to_all | solution.py:377
  118.9 1.1 reshape.54
  (43 shorter events, 4.3 us)
Async XLA Ops:
  0.6 14.6 %copy-start.1 = (s32[8,16,1440]{2,1,0:T(8,128)S(1)}, s32[8,16,1440]{2,1,0:T(8,128)}, u32[]{:S(2)}) copy-start(s32[8,16,1440]{2,1,0:T(8,128)} %klat_ref.3) | copy-start | bytes 2211844
  0.6 14.6 %copy-start = (f32[8,16,1440]{2,1,0:T(8,128)S(1)}, f32[8,16,1440]{2,1,0:T(8,128)}, u32[]{:S(2)}) copy-start(f32[8,16,1440]{2,1,0:T(8,128)} %clat_ref.3) | copy-start | bytes 2211844
  0.7 14.6 %copy-start.2 = (f32[8,16,1440]{2,1,0:T(8,128)S(1)}, f32[8,16,1440]{2,1,0:T(8,128)}, u32[]{:S(2)}) copy-start(f32[8,16,1440]{2,1,0:T(8,128)} %clon_ref.3) | copy-start | bytes 2211844
  5.0 8.3 %collective-permute-start.1 = (f32[4,8,1440]{2,1,0:T(8,128)S(1)}, f32[4,8,1440]{2,1,0:T(8,128)S(1)}, u32[]{:S(2)}, u32[]{:S(2)}) collective-permute-start(f32[4,8,1440]{2,1,0:T(8,128)S(1)} %pad_maximum_fusion), channel_id=1, source_target_pairs={{8,0},{16,8},{24,16},{32,24},{40,32},{48,40},{56,48},{64,56},{72,6... | collective-permute-start | bytes 552968 | tf_op jit(solution)/shard_map/ppermute | solution.py:323
  10.2 5.0 %collective-permute-start = (f32[5,8,1440]{2,1,0:T(8,128)S(1)}, f32[5,8,1440]{2,1,0:T(8,128)S(1)}, u32[]{:S(2)}, u32[]{:S(2)}) collective-permute-start(f32[5,8,1440]{2,1,0:T(8,128)S(1)} %fusion.2), channel_id=1, source_target_pairs={{0,8},{8,16},{16,24},{24,32},{32,40},{40,48},{48,56},{56,64},{64,7... | collective-permute-start | bytes 691208 | tf_op jit(solution)/shard_map/ppermute | solution.py:323
  15.3 1.1 copy-start.3
  16.4 1.1 copy-start.4
  20.9 6.3 %collective-permute-start.2 = (f32[2,8,1440]{2,1,0:T(8,128)S(1)}, f32[2,8,1440]{2,1,0:T(8,128)S(1)}, u32[]{:S(2)}, u32[]{:S(2)}) collective-permute-start(f32[2,8,1440]{2,1,0:T(8,128)S(1)} %get-tuple-element.10), channel_id=1, source_target_pairs={{0,8},{8,16},{16,24},{24,32},{32,40},{40,48},{48,56},{56,64},{64,7... | collective-permute-start | bytes 276488 | tf_op jit(solution)/shard_map/ppermute | solution.py:323
  25.3 5.9 %collective-permute-start.3 = (f32[2,8,1440]{2,1,0:T(8,128)S(1)}, f32[2,8,1440]{2,1,0:T(8,128)S(1)}, u32[]{:S(2)}, u32[]{:S(2)}) collective-permute-start(f32[2,8,1440]{2,1,0:T(8,128)S(1)} %get-tuple-element.11), channel_id=1, source_target_pairs={{8,0},{16,8},{24,16},{32,24},{40,32},{48,40},{56,48},{64,56},{72,6... | collective-permute-start | bytes 276488 | tf_op jit(solution)/shard_map/ppermute | solution.py:323
  31.3 11.5 %copy-start.13 = (s32[2000]{0:T(1024)S(1)}, s32[2000]{0:T(1024)}, u32[]{:S(2)}) copy-start(s32[2000]{0:T(1024)} %param.23) | copy-start | bytes 24004
  31.3 11.5 %copy-start.10 = (f32[16,3,16,16]{3,2,1,0:T(8,128)S(1)}, f32[16,3,16,16]{3,2,1,0:T(8,128)}, u32[]{:S(2)}) copy-start(f32[16,3,16,16]{3,2,1,0:T(8,128)} %lower_ref.1) | copy-start | bytes 147460
  36.2 22.1 %copy-start.5 = (f32[64,16,180]{2,1,0:T(8,128)S(1)}, f32[64,16,180]{2,1,0:T(8,128)}, u32[]{:S(2)}) copy-start(f32[64,16,180]{2,1,0:T(8,128)} %c_ref.1) | copy-start | bytes 2211844
  36.2 22.1 %copy-start.6 = (s32[64,16,180]{2,1,0:T(8,128)S(1)}, s32[64,16,180]{2,1,0:T(8,128)}, u32[]{:S(2)}) copy-start(s32[64,16,180]{2,1,0:T(8,128)} %k_ref.1) | copy-start | bytes 2211844
  36.2 22.0 %all-to-all-start = ((f32[8,8,16,180]{3,2,1,0:T(8,128)}), f32[8,8,16,180]{3,2,1,0:T(8,128)S(1)}, u32[]{:S(2)}, u32[]{:S(2)}) async-start(f32[8,8,16,180]{3,2,1,0:T(8,128)} %horizontal.3), calls=%async_computation | async-start | bytes 2097152 | tf_op jit(solution)/shard_map/all_to_all | solution.py:370
  42.8 1.0 copy-start.9
  43.8 1.0 copy-start.11
  49.4 0.8 copy-start.7
  58.2 1.0 copy-start.8
  63.9 19.8 %copy-start.12 = (s32[16,1440]{1,0:T(8,128)S(1)}, s32[16,1440]{1,0:T(8,128)}, u32[]{:S(2)}) copy-start(s32[16,1440]{1,0:T(8,128)} %ids_ref.1) | copy-start | bytes 276484

commit v2 on v1

v2 whole, which is shorter than its diff:
```python
import functools

import jax
import jax.numpy as jnp
from jax import lax
from jax.experimental import pallas as pl
from jax.experimental.pallas import tpu as pltpu
from jax.sharding import PartitionSpec as P

SUB = 2
SLOTS = 16
LANES = 128
HALF = LANES // 2
F32 = jnp.float32
BF16 = jnp.bfloat16
VMEM = pl.BlockSpec(memory_space=pltpu.VMEM)
SMEM = pl.BlockSpec(memory_space=pltpu.SMEM)
HBM = pl.BlockSpec(memory_space=pltpu.HBM)


def params(mib=20):
    return pltpu.CompilerParams(vmem_limit_bytes=mib * 2**20)


def cost(microseconds):
    return pl.CostEstimate(flops=microseconds * 10**9, bytes_accessed=microseconds * 10**6, transcendentals=0)


def flux_parts(courant):
    up = jnp.maximum(courant, 0.0)
    down = jnp.minimum(courant, 0.0)
    half = 0.5 * courant
    return up, down, up * (0.5 - half), down * (0.5 + half)


def slope_parts(codes):
    centred = jnp.where(codes == 3, 0.5, 0.0)
    ahead = jnp.where(codes == 1, 1.0, centred)
    behind = jnp.where(codes == 2, 1.0, centred)
    return ahead, behind


def split(value):
    high = value.astype(BF16)
    low = (value - high.astype(F32)).astype(BF16)
    return high, low


def roll(value, shift, axis):
    return pltpu.roll(value, shift % value.shape[axis], axis)


def wrapped(value, width):
    length = value.shape[1]
    spare = width - length
    first = spare // 2
    return jnp.concatenate([value, value[:, :first], value[:, length - spare + first :]], axis=1)


def sweep_lon(value, up, down, uph, downh, ahead, behind):
    f = roll(value, -1, 1) - value
    s = uph * f - roll(downh * f, 1, 1)
    q = roll(down * f + ahead * s, 1, 1)
    r = roll(behind * s, -1, 1)
    return value + up * f + (behind - ahead) * s + q - r


def lon_parts(courant, codes, width):
    return (*flux_parts(wrapped(courant, width)), *slope_parts(wrapped(codes, width)))


def edge_rows(rows):
    return (0, 1, rows - 2, rows - 1)


def interior_kernel(last_ref, *refs, final):
    if final:
        a_ref, up_ref, down_ref, clat_ref, klat_ref, clon_ref, klon_ref, send_ref, swept_ref, rows_ref = refs
    else:
        a_ref, clat_ref, klat_ref, clon_ref, klon_ref, out_ref, swept_ref, edge_ref, lonc_ref, rows_ref = refs
    levels, rows, lons = a_ref.shape
    width = rows_ref.shape[2]
    half = levels // 2
    last = last_ref[0]
    step = 4 * LANES
    chunks = [(start, min(step, lons - start)) for start in range(0, lons, step)]
    tile = 8

    def level(l, upper):
        for start, size in chunks:
            cols = slice(start, start + size)
            row = lax.broadcasted_iota(jnp.int32, (rows, size), 0)
            lowest, highest = row == 0, row == rows - 1
            a = a_ref[l, :, cols]
            if final:
                a = jnp.where(lowest, down_ref[0, pl.ds(l, 1), cols], a)
                a = jnp.where(row == 1, down_ref[1, pl.ds(l, 1), cols], a)
                a = jnp.where(row == rows - 2, up_ref[1, pl.ds(l, 1), cols], a)
                a = jnp.where(highest, up_ref[0, pl.ds(l, 1), cols], a)
            courant = jnp.where(highest & (last == 1), 0.0, clat_ref[l, :, cols])
            up, down, uph, downh = flux_parts(courant)
            ahead, behind = slope_parts(klat_ref[l, :, cols])
            f = jnp.where(highest, 0.0, roll(a, -1, 0)) - a
            s = uph * f - jnp.where(lowest, 0.0, roll(downh * f, 1, 0))
            q = jnp.where(lowest, 0.0, roll(down * f + ahead * s, 1, 0))
            r = jnp.where(highest, 0.0, roll(behind * s, -1, 0))
            rows_ref[l, :, cols] = a + up * f + (behind - ahead) * s + q - r
        for low in range(0, rows, tile):
            band = slice(low, low + tile)
            value = sweep_lon(
                wrapped(rows_ref[l, band, :lons], width), *lon_parts(clon_ref[l, band, :], klon_ref[l, band, :], width)
            )
            if final:
                parts = send_ref.shape[0]
                share = lons // parts
                for part in range(parts):
                    start = part * share
                    send_ref[part, l, band, :] = value[:, start : start + LANES]
                    rest = value[:, start + LANES : start + share]
                    if upper:
                        send_ref[part, half + l, band, HALF : HALF + share - LANES] = rest
                    else:
                        send_ref[part, levels + l, band, : share - LANES] = rest
            else:
                out_ref[l, band, :] = value[:, :lons]

    def pair(index, carry):
        level(index, False)
        level(index + half, True)
        return carry

    lax.fori_loop(0, half, pair, 0)
    for n, row in enumerate(edge_rows(rows)):
        swept_ref[n] = rows_ref[:, row, :lons]
    if not final:
        high = rows - 1
        courant = jnp.where(last == 1, 0.0, clat_ref[:, high, :])
        up, _, uph, downh = flux_parts(courant)
        ahead, behind = slope_parts(klat_ref[:, high, :])
        ahead0, behind0 = slope_parts(klat_ref[:, 0, :])
        edge_ref[0] = a_ref[:, 0, :]
        edge_ref[1] = a_ref[:, high, :]
        edge_ref[2] = behind0 - ahead0
        edge_ref[3] = ahead0
        edge_ref[4] = up + (behind - ahead) * uph
        edge_ref[5] = behind * uph
        edge_ref[6] = downh
        for n, row in enumerate(edge_rows(rows)):
            for m, part in enumerate(lon_parts(clon_ref[:, row, :], klon_ref[:, row, :], width)):
                lonc_ref[n, m] = part


def interior(last, fields, coefficients, parts):
    levels, rows, lons = fields[0].shape
    width = -(-lons // LANES) * LANES
    final = parts > 0
    whole = (levels, rows, lons)
    swept = jax.ShapeDtypeStruct((4, levels, lons), F32)
    if final:
        out_shape = (jax.ShapeDtypeStruct((parts, levels + levels // 2, rows, LANES), F32), swept)
    else:
        out_shape = (
            jax.ShapeDtypeStruct(whole, F32),
            swept,
            jax.ShapeDtypeStruct((7, levels, lons), F32),
            jax.ShapeDtypeStruct((4, 6, levels, width), F32),
        )
    return pl.pallas_call(
        functools.partial(interior_kernel, final=final),
        out_shape=out_shape,
        in_specs=[SMEM] + [VMEM] * (len(fields) + len(coefficients)),
        out_specs=(VMEM,) * len(out_shape),
        scratch_shapes=[pltpu.VMEM((levels, rows, width), F32)],
        compiler_params=params(),
        cost_estimate=cost(4),
        name="interior",
    )(last, *fields, *coefficients)


def edges_kernel(below_ref, above_ref, edge_ref, lonc_ref, swept_ref, *refs, final):
    width = lonc_ref.shape[3]
    _, levels, lons = swept_ref.shape
    if final:
        below_next, above_next, up_in, down_in, sent_ref, send_ref, main_ref, rest_ref = refs
        row0, row15 = down_in[0], up_in[0]
        am1, am2, a16, a17 = below_next[0], below_next[1], above_next[0], above_next[1]
    else:
        up_ref, down_ref = refs
        row0, row15 = edge_ref[0], edge_ref[1]
        am1, am2, a16, a17 = below_ref[0], below_ref[1], above_ref[0], above_ref[1]
    _, down1, uph1, downh1 = flux_parts(below_ref[2])
    _, _, _, downh2 = flux_parts(below_ref[3])
    ahead1, _ = slope_parts(below_ref[4])
    f1 = row0 - am1
    w = downh1 * f1
    q = down1 * f1 + ahead1 * (uph1 * f1 - downh2 * (am1 - am2))
    _, _, uph16, _ = flux_parts(above_ref[2])
    _, behind16 = slope_parts(above_ref[3])
    r = behind16 * (uph16 * (a17 - a16) - edge_ref[6] * (a16 - row15))
    fixed = (
        swept_ref[0] - edge_ref[2] * w + q,
        swept_ref[1] - edge_ref[3] * w,
        swept_ref[2] - edge_ref[5] * a16,
        swept_ref[3] + edge_ref[4] * a16 - r,
    )
    rows = []
    for n, row in enumerate(fixed):
        rows.append(sweep_lon(wrapped(row, width), *(lonc_ref[n, m] for m in range(6))))
    if final:
        parts, _, count, _ = send_ref.shape
        share = lons // parts
        half = levels // 2
        tile = 8
        sublane = lax.broadcasted_iota(jnp.int32, (tile, LANES), 0)
        lower = lax.broadcasted_iota(jnp.int32, (tile, LANES), 1) < HALF
        first = lax.broadcasted_iota(jnp.int32, (levels, LANES), 0) < half
        blank = jnp.zeros((levels, LANES - (share - LANES)), F32)

        for n, row in enumerate(rows):
            for part in range(parts):
                start = part * share
                main_ref[n, part] = row[:, start : start + LANES]
                rest = jnp.concatenate([row[:, start + LANES : start + share], blank], axis=1)
                rest_ref[n, part] = jnp.where(first, rest, roll(rest, HALF, 1))
        places = edge_rows(count)
        for low in range(0, count, tile):
            band = slice(low, low + tile)
            mine = [(n, place - low) for n, place in enumerate(places) if low <= place < low + tile]
            for part in range(parts):
                for l in range(levels):
                    value = sent_ref[part, l, band, :]
                    for n, place in mine:
                        value = jnp.where(sublane == place, main_ref[n, part, l : l + 1, :], value)
                    send_ref[part, l, band, :] = value
                for l in range(half):
                    value = sent_ref[part, levels + l, band, :]
                    for n, place in mine:
                        both = jnp.where(
                            lower, rest_ref[n, part, l : l + 1, :], rest_ref[n, part, l + half : l + half + 1, :]
                        )
                        value = jnp.where(sublane == place, both, value)
                    send_ref[part, levels + l, band, :] = value
    else:
        down_ref[0], down_ref[1] = rows[0][:, :lons], rows[1][:, :lons]
        up_ref[0], up_ref[1] = rows[3][:, :lons], rows[2][:, :lons]


def edges(below, above, edge, lonc, swept, *more):
    _, levels, lons = swept.shape
    final = len(more) > 0
    args = (below, above, edge, lonc, swept, *more)
    if final:
        out_shape = jax.ShapeDtypeStruct(more[-1].shape, F32)
        scratch = [pltpu.VMEM((4, more[-1].shape[0], levels, LANES), F32)] * 2
    else:
        out_shape = (jax.ShapeDtypeStruct((2, levels, lons), F32),) * 2
        scratch = []
    return pl.pallas_call(
        functools.partial(edges_kernel, final=final),
        out_shape=out_shape,
        in_specs=[VMEM] * len(args),
        out_specs=VMEM if final else (VMEM, VMEM),
        scratch_shapes=scratch,
        compiler_params=params(),
        cost_estimate=cost(1),
        name="edges",
    )(*args)


def pack_kernel(*refs):
    *sources, up_ref, down_ref, a_ref, clat_ref, klat_ref, sems = refs
    fields = (a_ref, clat_ref, klat_ref)
    levels, rows, _ = a_ref.shape
    half = levels // 2
    copies = []
    for n, (src, dst) in enumerate(zip(sources, fields)):
        for part in range(2):
            span = pl.ds(part * half, half)
            copies.append(pltpu.make_async_copy(src.at[span], dst.at[span], sems.at[n, part]))
    for copy in copies:
        copy.start()
    for copy in copies:
        copy.wait()
    edge = rows - 1
    up_ref[0] = a_ref[:, edge, :]
    up_ref[1] = a_ref[:, edge - 1, :]
    down_ref[0] = a_ref[:, 0, :]
    down_ref[1] = a_ref[:, 1, :]
    up_ref[2] = clat_ref[:, edge, :]
    up_ref[3] = clat_ref[:, edge - 1, :]
    down_ref[2] = clat_ref[:, 0, :]
    up_ref[4] = klat_ref[:, edge, :].astype(F32)
    down_ref[3] = klat_ref[:, 0, :].astype(F32)


def pack(a, clat, klat):
    levels, _, lons = a.shape
    return pl.pallas_call(
        pack_kernel,
        out_shape=(jax.ShapeDtypeStruct((5, levels, lons), F32), jax.ShapeDtypeStruct((4, levels, lons), F32)),
        in_specs=[HBM] * 3,
        out_specs=(VMEM, VMEM),
        scratch_shapes=[pltpu.VMEM(a.shape, x.dtype) for x in (a, clat, klat)] + [pltpu.SemaphoreType.DMA((3, 2))],
        compiler_params=params(60),
        cost_estimate=cost(2),
        name="pack",
    )(a, clat, klat)


def prep_kernel(
    inverse_ref, lower_ref, upper_ref, owner_ref, ids_ref, matrix_ref, slot_ref, fine_ref, device_ref, *, devices
):
    lats, blocks, size, _ = inverse_ref.shape
    group = LANES // size
    levels = blocks * size
    row = lax.broadcasted_iota(jnp.int32, (LANES, LANES), 0)
    col = lax.broadcasted_iota(jnp.int32, (LANES, LANES), 1)
    diagonal = (row // size) == (col // size)
    row_l = lax.broadcasted_iota(jnp.int32, (LANES, levels), 0)
    col_l = lax.broadcasted_iota(jnp.int32, (LANES, levels), 1)

    def times(matrix, vector):
        wide = jnp.concatenate([matrix.reshape(LANES, size)] * group, axis=1)
        wide = jnp.where(diagonal, wide, 0.0)
        return jnp.dot(wide, vector, precision=lax.Precision.HIGHEST, preferred_element_type=F32)

    for first in range(0, lats, group):
        lat = slice(first, first + group)
        solved = []
        for k in range(blocks):
            rhs = jnp.where(col_l == row_l % size + size * k, 1.0, 0.0)
            if k > 0:
                rhs = rhs - times(lower_ref[lat, k - 1], solved[-1])
            solved.append(times(inverse_ref[lat, k], rhs))
        result = [solved[-1]]
        for k in range(blocks - 2, -1, -1):
            result.insert(0, solved[k] - times(upper_ref[lat, k], result[0]))
        for g in range(group):
            dense = jnp.concatenate([block[g * size : (g + 1) * size] for block in result], axis=0)
            high, low = split(dense.T)
            matrix_ref[first + g] = jnp.concatenate([high, low, high], axis=1)

    tiles = owner_ref.shape[0]
    device = lax.broadcasted_iota(jnp.int32, (devices, LANES), 0)
    earlier = jnp.where(row < col, 1.0, 0.0).astype(BF16)
    running = jnp.zeros((devices, 1), F32)
    for t in range(tiles):
        owned = jnp.where(owner_ref[pl.ds(t, 1), :] == device, 1.0, 0.0)
        before = jnp.dot(owned.astype(BF16), earlier, preferred_element_type=F32) + running
        slot_ref[pl.ds(t, 1), :] = jnp.sum(owned * before, axis=0, keepdims=True).astype(jnp.int32)
        running = running + jnp.sum(owned, axis=1, keepdims=True)
    fine_ref[...] = (ids_ref[...] % LANES).astype(F32).T
    device_ref[...] = owner_ref[...].astype(F32).T


def prep(inverse, lower, upper, owner_tiles, ids, devices):
    lats, blocks, size, _ = inverse.shape
    levels = blocks * size
    return pl.pallas_call(
        functools.partial(prep_kernel, devices=devices),
        out_shape=(
            jax.ShapeDtypeStruct((lats, levels, 3 * levels), BF16),
            jax.ShapeDtypeStruct(owner_tiles.shape, jnp.int32),
            jax.ShapeDtypeStruct(ids.shape[::-1], F32),
            jax.ShapeDtypeStruct(owner_tiles.shape[::-1], F32),
        ),
        in_specs=[VMEM] * 5,
        out_specs=(VMEM,) * 4,
        compiler_params=params(),
        cost_estimate=cost(5),
        name="prep",
    )(inverse, lower, upper, owner_tiles, ids)


def unpacked(main, rest, upper, spare):
    if upper:
        rest = roll(rest, HALF, rest.ndim - 1)
    return jnp.concatenate([main, rest[..., :spare]], axis=-1)


def vertical_kernel(x_ref, matrix_ref, c_ref, k_ref, out_ref, field_ref, y_ref):
    levels, rows, share = c_ref.shape
    parts = x_ref.shape[0]
    group = levels // parts
    half = group // 2
    spare = share - LANES
    for level in range(levels):
        part, l = level // group, level % group
        field_ref[level] = unpacked(x_ref[part, l], x_ref[part, group + l % half], l // half, spare)
    for lat in range(rows):
        high, low = split(field_ref[:, lat, :])
        stacked = jnp.concatenate([high, high, low], axis=0)
        y_ref[:, lat, :] = jnp.dot(matrix_ref[lat], stacked, preferred_element_type=F32)

    def emit(level, value):
        part, l = level // group, level % group
        out_ref[part, l] = value[:, :LANES]
        place = group + l % half
        if l // half:
            out_ref[part, place, :, HALF : HALF + spare] = value[:, LANES:]
        else:
            out_ref[part, place, :, :spare] = value[:, LANES:]

    zero = jnp.zeros((rows, share), F32)
    y = y_ref[0]
    prior_w, prior_q, pending = zero, zero, None
    for i in range(levels):
        ahead, behind = slope_parts(k_ref[i])
        if i < levels - 1:
            up, down, uph, downh = flux_parts(c_ref[i])
            y_next = y_ref[i + 1]
            f = y_next - y
            s = uph * f - prior_w
            here = y + up * f + prior_q
            prior_w = downh * f
            prior_q = down * f + ahead * s
        else:
            y_next = None
            s = -prior_w
            here = y + prior_q
        here = here + (behind - ahead) * s
        if i > 0:
            emit(i - 1, pending - behind * s)
        pending = here
        y = y_next
    emit(levels - 1, pending)


def vertical(x, matrix, courant, codes):
    return pl.pallas_call(
        vertical_kernel,
        out_shape=jax.ShapeDtypeStruct(x.shape, F32),
        in_specs=[VMEM] * 4,
        out_specs=VMEM,
        scratch_shapes=[pltpu.VMEM(courant.shape, F32)] * 2,
        compiler_params=params(),
        cost_estimate=cost(5),
        name="vertical",
    )(x, matrix, courant, codes)


def region_kernel(
    field_ref, ids_ref, fine_ref, device_ref, slot_ref, out_ref, send_ref, high_ref, low_ref, acc_ref, table_ref, *, scale
):
    levels, rows, lons = out_ref.shape
    parts = field_ref.shape[0]
    share = lons // parts
    half = levels // 2
    tiles = slot_ref.shape[0]
    devices = send_ref.shape[0]
    for l in range(levels):
        pieces = [
            unpacked(field_ref[part, l], field_ref[part, levels + l % half], l // half, share - LANES)
            for part in range(parts)
        ]
        whole = jnp.concatenate(pieces, axis=1)
        out_ref[l] = whole
        high = whole.astype(BF16).astype(F32)
        high_ref[l] = high
        low_ref[l] = whole - high
    coarse = lax.broadcasted_iota(jnp.int32, (tiles, lons), 0)
    lane = lax.broadcasted_iota(jnp.int32, (lons, LANES), 1).astype(F32)
    for lat in range(rows):
        mask = jnp.where((ids_ref[lat : lat + 1, :] // LANES) == coarse, 1.0, 0.0).astype(BF16)
        onehot = jnp.where(fine_ref[:, lat : lat + 1] == lane, 1.0, 0.0).astype(BF16)
        pieces = []
        for ref in (high_ref, low_ref):
            for l in range(levels):
                row = jnp.broadcast_to(ref[l, lat : lat + 1, :], (tiles, lons))
                pieces.append(row.astype(BF16) * mask)
        stacked = jnp.concatenate(pieces, axis=0)
        term = jnp.dot(stacked, onehot, preferred_element_type=F32)
        if lat == 0:
            acc_ref[...] = term
        else:
            acc_ref[...] += term
    size = levels * tiles
    table_ref[...] = acc_ref[pl.ds(0, size), :] + acc_ref[pl.ds(size, size), :]
    device = lax.broadcasted_iota(jnp.int32, (LANES, devices), 1).astype(F32)
    place = lax.broadcasted_iota(jnp.int32, (SLOTS * levels, LANES), 0) // levels
    total = jnp.zeros((SLOTS * levels, devices), F32)
    for t in range(tiles):
        owned = jnp.where(device_ref[:, t : t + 1] == device, 1.0, 0.0).astype(BF16)
        sums = table_ref[pl.ds(t, levels, stride=tiles), :]
        spread = jnp.where(slot_ref[t : t + 1, :] == place, jnp.concatenate([sums] * SLOTS, axis=0), 0.0)
        for piece in split(spread):
            total += jnp.dot(piece, owned, preferred_element_type=F32)
    send_ref[...] = (total * scale).T


def regions(field, ids, fine, device, slot_tiles, levels, devices, scale):
    tiles = slot_tiles.shape[0]
    rows, lons = ids.shape
    whole = (levels, rows, lons)
    return pl.pallas_call(
        functools.partial(region_kernel, scale=scale),
        out_shape=(jax.ShapeDtypeStruct(whole, F32), jax.ShapeDtypeStruct((devices, SLOTS * levels), F32)),
        in_specs=[VMEM] * 5,
        out_specs=(VMEM, VMEM),
        scratch_shapes=[
            pltpu.VMEM(whole, F32),
            pltpu.VMEM(whole, F32),
            pltpu.VMEM((2 * levels * tiles, LANES), F32),
            pltpu.VMEM((levels * tiles, LANES), F32),
        ],
        compiler_params=params(),
        cost_estimate=cost(6),
        name="regions",
    )(field, ids, fine, device, slot_tiles)


def owners_kernel(rows_ref, out_ref):
    devices, lanes = rows_ref.shape
    slots, width = out_ref.shape
    levels = lanes // slots
    groups = width // levels
    total = rows_ref[pl.ds(0, groups), :]
    for first in range(groups, devices, groups):
        total += rows_ref[pl.ds(first, groups), :]
    slot = lax.broadcasted_iota(jnp.int32, (slots, lanes), 0)
    lane = lax.broadcasted_iota(jnp.int32, (slots, lanes), 1)
    mine = slot == lane // levels
    spread = jnp.concatenate([jnp.where(mine, total[j : j + 1], 0.0) for j in range(groups)], axis=1)
    row = lax.broadcasted_iota(jnp.int32, (groups * lanes, width), 0)
    col = lax.broadcasted_iota(jnp.int32, (groups * lanes, width), 1)
    fold = jnp.where(col == row // lanes * levels + row % levels, 1.0, 0.0)
    out_ref[...] = jnp.dot(spread, fold, precision=lax.Precision.HIGHEST, preferred_element_type=F32)


def owners(rows, groups, levels):
    return pl.pallas_call(
        owners_kernel,
        out_shape=jax.ShapeDtypeStruct((SLOTS, groups * levels), F32),
        in_specs=[VMEM],
        out_specs=VMEM,
        compiler_params=params(),
        name="owners",
    )(rows)


def neighbours(up, down):
    count = lax.axis_size("lat")
    forward = [(i, i + 1) for i in range(count - 1)]
    backward = [(target, source) for source, target in forward]
    return lax.ppermute(up, "lat", forward), lax.ppermute(down, "lat", backward)


def local(
    adjoint_in,
    courant_lon,
    codes_lon,
    courant_lat,
    codes_lat,
    courant_lev,
    codes_lev,
    block_inverse,
    block_lower,
    block_upper,
    region_ids,
    owner,
):
    levels_here, bands_here, lon_cells = adjoint_in.shape
    band_count = lax.axis_size("lat")
    group_count = lax.axis_size("lev")
    devices = band_count * group_count
    region_count = owner.shape[0]
    tiles = -(-region_count // LANES)
    tiles = -(-tiles // 8) * 8
    owner_tiles = jnp.pad(owner, (0, tiles * LANES - region_count), constant_values=-1).reshape(tiles, LANES)
    matrix, slot_tiles, fine, device = prep(
        block_inverse, block_lower, block_upper, owner_tiles, region_ids, devices
    )
    last = (lax.axis_index("lat") == band_count - 1).astype(jnp.int32).reshape(1)
    up, down = pack(adjoint_in, courant_lat, codes_lat)
    below, above = neighbours(up, down)
    coefficients = (courant_lat, codes_lat, courant_lon, codes_lon)
    adjoint, swept, edge, lonc = interior(last, (adjoint_in,), coefficients, 0)
    up, down = edges(below, above, edge, lonc, swept)
    below_next, above_next = neighbours(up, down)
    sent, swept = interior(last, (adjoint, up, down), coefficients, group_count)
    sent = edges(below, above, edge, lonc, swept, below_next, above_next, up, down, sent)
    columns = lax.all_to_all(sent, "lev", split_axis=0, concat_axis=0, tiled=True)
    columns = vertical(columns, matrix, courant_lev, codes_lev)
    field = lax.all_to_all(columns, "lev", split_axis=0, concat_axis=0, tiled=True)
    scale = (region_count / (bands_here * band_count * lon_cells)) ** 0.5
    adjoint_out, rows = regions(
        field, region_ids, fine, device, slot_tiles, levels_here, devices, scale
    )
    rows = lax.all_to_all(rows, ("lat", "lev"), split_axis=0, concat_axis=0, tiled=True)
    region_sens = owners(rows, group_count, levels_here)
    return (adjoint_out, region_sens)


def solution(mesh):
    placed = (
        P("lev", "lat", None),
        P("lev", "lat", None),
        P("lev", "lat", None),
        P("lev", "lat", None),
        P("lev", "lat", None),
        P(None, "lat", "lev"),
        P(None, "lat", "lev"),
        P("lat", None, None, None),
        P("lat", None, None, None),
        P("lat", None, None, None),
        P("lat", None),
        P(),
    )
    return jax.shard_map(
        local,
        mesh=mesh,
        in_specs=placed,
        out_specs=(P("lev", "lat", None), P(("lat", "lev"), None)),
        check_vma=False,
    )
```

time: 122 us -> 102 us (0.84)
  waiting for transfers between devices: 15.1 us -> 5.05 us
  local copies, waits for them, and re-layouts: 12.9 us -> 7.65 us
  blocking collectives: 45.5 us -> 41.5 us
  Pallas kernels: 25.4 us -> 27.4 us
    slice x6 -> x0, local copies, waits for them, and re-layouts: 4.27 us -> none  [the longest x1 1.51 us: local(): adjoint_in[:, 0]]
    all_to_all x1, waiting for transfers between devices: 8.02 us -> 3.82 us  [local(): lax.all_to_all(sent, 'lev', split_axis=0, concat_axis=0, tiled=True)]
    ppermute x2, waiting for transfers between devices: 5.12 us -> 1.23 us  [neighbours(): lax.ppermute(down, 'lat', backward)]
    ppermute x2, starting transfers between devices: 7.07 us -> 3.84 us  [neighbours(): lax.ppermute(down, 'lat', backward)]
    pallas_call x2 -> x6, Pallas kernels: 8.26 us -> 11.5 us  [the longest x2 5.7 us: interior(): pl.pallas_call(functools.partial(interior_kernel, final=final), out_shape...]
    all_to_all x1, blocking collectives: 19.8 us -> 17.5 us  [local(): lax.all_to_all(columns, 'lev', split_axis=0, concat_axis=0, tiled=True)]
    ppermute x2, starting transfers between devices: 6.32 us -> 8.44 us  [neighbours(): lax.ppermute(up, 'lat', forward)]
    ppermute x2, waiting for transfers between devices: 1.98 us -> 0.01 us  [neighbours(): lax.ppermute(up, 'lat', forward)]
  transfers between devices with their start and end apart: 5 -> 5, of which waited for: 4 -> 3; matrix products, arithmetic and copies ran while one was open for 0% -> 0% of each run, Pallas kernels for 4% -> 10%
where the time goes in v2:
time: 102 us
  blocking collectives  41.5 us (41%)
  Pallas kernels  27.4 us (27%)
  starting transfers between devices  19.1 us (19%)
  local copies, waits for them, and re-layouts  7.65 us (8%)
  waiting for transfers between devices  5.05 us (5%)
    all_to_all x1, blocking collectives, local(): lax.all_to_all(rows, ('lat', 'lev'), split_axis=0, concat_axis=0, tiled=T...  23.9 us
    all_to_all x1, blocking collectives, local(): lax.all_to_all(columns, 'lev', split_axis=0, concat_axis=0, tiled=True)  17.5 us
    ppermute x2, starting transfers between devices, neighbours(): lax.ppermute(up, 'lat', forward)  8.44 us
    unnamed x40, local copies, waits for them, and re-layouts  7.65 us
    all_to_all x1, starting transfers between devices, local(): lax.all_to_all(sent, 'lev', split_axis=0, concat_axis=0, tiled=True)  6.78 us
    pallas_call x1, Pallas kernels, regions(): pl.pallas_call(functools.partial(region_kernel, scale=scale), out_shape=(...  6.65 us
    pallas_call x2, Pallas kernels, interior(): pl.pallas_call(functools.partial(interior_kernel, final=final), out_shape...  5.7 us
    pallas_call x1, Pallas kernels, vertical(): pl.pallas_call(vertical_kernel, out_shape=jax.ShapeDtypeStruct(x.shape, F...  4.65 us
  transfers between devices with their start and end apart: 5, of which 3 were waited for; matrix products, arithmetic and copies ran while one was open for 0% of the time, Pallas kernels for 10%

profile of v2, /device:TPU:1, one launch (start us, length us, event | category | flops | bytes accessed | tf_op | source)
XLA Modules:
  0.0 101.5 jit_solution(16773979028297506372)
XLA Ops:
  0.7 2.6 %pack.1 = (f32[5,8,1440]{2,1,0:T(8,128)}, f32[4,8,1440]{2,1,0:T(8,128)}) custom-call(f32[8,16,1440]{2,1,0:T(8,128)} %refs_0_.3, f32[8,16,1440]{2,1,0:T(8,128)} %refs_3_.3, s32[8,16,1440]{2,1,0:T(8,128)} %refs_4_.3), custom_call_target="tpu_custom_call" | custom-call | flops 2000000000 | bytes 2000000 | tf_op jit(solution)/shard_map/pack/pallas_call | solution.py:298
  3.3 4.9 %collective-permute-start = (f32[5,8,1440]{2,1,0:T(8,128)}, f32[5,8,1440]{2,1,0:T(8,128)S(1)}, u32[]{:S(2)}, u32[]{:S(2)}) collective-permute-start(f32[5,8,1440]{2,1,0:T(8,128)} %get-tuple-element.18), channel_id=1, source_target_pairs={{0,8},{8,16},{16,24},{24,32},{32,40},{40,48},{48,56},{56,64},{64,7... | collective-permute-start | bytes 691208 | tf_op jit(solution)/shard_map/ppermute | solution.py:545
  8.2 1.9 %collective-permute-start.1 = (f32[4,8,1440]{2,1,0:T(8,128)}, f32[4,8,1440]{2,1,0:T(8,128)S(1)}, u32[]{:S(2)}, u32[]{:S(2)}) collective-permute-start(f32[4,8,1440]{2,1,0:T(8,128)} %get-tuple-element.19), channel_id=1, source_target_pairs={{8,0},{16,8},{24,16},{32,24},{40,32},{48,40},{56,48},{64,56},{72,6... | collective-permute-start | bytes 552968 | tf_op jit(solution)/shard_map/ppermute | solution.py:545
  10.2 1.1 %copy-done.5 = f32[8,16,1440]{2,1,0:T(8,128)S(1)} copy-done((f32[8,16,1440]{2,1,0:T(8,128)S(1)}, f32[8,16,1440]{2,1,0:T(8,128)}, u32[]{:S(2)}) %copy-start.5) | copy-done | bytes 737304
  11.3 1.1 %copy-done.7 = s32[8,16,1440]{2,1,0:T(8,128)S(1)} copy-done((s32[8,16,1440]{2,1,0:T(8,128)S(1)}, s32[8,16,1440]{2,1,0:T(8,128)}, u32[]{:S(2)}) %copy-start.7) | copy-done | bytes 737304
  12.5 2.8 %interior.2 = (f32[8,16,1440]{2,1,0:T(8,128)S(1)}, f32[4,8,1440]{2,1,0:T(8,128)S(1)}, f32[7,8,1440]{2,1,0:T(8,128)S(1)}, f32[4,6,8,1536]{3,2,1,0:T(8,128)S(1)}) custom-call(s32[1]{0:T(128)} %bitcast.last_ref, f32[8,16,1440]{2,1,0:T(8,128)S(1)} %copy-done.2, f32[8,16,1440]{2,1,0:T(8,128)S(1)} %copy-done.3, s32[8,16,1440]{2,1,0:T(8,128)S(1)} %copy-done.4, ...), custom_call_target="tpu_custom_call" | custom-call | flops 4000000000 | bytes 4000000 | tf_op jit(solution)/shard_map/interior/pallas_call | solution.py:168
  15.9 3.5 %collective-permute-start.2 = (f32[2,8,1440]{2,1,0:T(8,128)S(1)}, f32[2,8,1440]{2,1,0:T(8,128)S(1)}, u32[]{:S(2)}, u32[]{:S(2)}) collective-permute-start(f32[2,8,1440]{2,1,0:T(8,128)S(1)} %get-tuple-element.24.refs_1_.refs_2_), channel_id=1, source_target_pairs={{0,8},{8,16},{16,24},{24,32},{32,40},{40,48},{48,56},{56,64},{64,7... | collective-permute-start | bytes 276488 | tf_op jit(solution)/shard_map/ppermute | solution.py:545
  19.4 1.9 %collective-permute-start.3 = (f32[2,8,1440]{2,1,0:T(8,128)S(1)}, f32[2,8,1440]{2,1,0:T(8,128)S(1)}, u32[]{:S(2)}, u32[]{:S(2)}) collective-permute-start(f32[2,8,1440]{2,1,0:T(8,128)S(1)} %get-tuple-element.25.refs_2_.refs_3_), channel_id=1, source_target_pairs={{8,0},{16,8},{24,16},{32,24},{40,32},{48,40},{56,48},{64,56},{72,6... | collective-permute-start | bytes 276488 | tf_op jit(solution)/shard_map/ppermute | solution.py:545
  21.4 2.9 %interior.3 = (f32[8,12,16,128]{3,2,1,0:T(8,128)S(1)}, f32[4,8,1440]{2,1,0:T(8,128)S(1)}) custom-call(s32[1]{0:T(128)} %bitcast.last_ref, f32[8,16,1440]{2,1,0:T(8,128)S(1)} %get-tuple-element.22.refs_0_, f32[2,8,1440]{2,1,0:T(8,128)S(1)} %get-tuple-element.24.refs_1_.refs_2_, f32[2,8,1440]{2,1,0:T(8,128)S(1)} %get-tuple-element.25.refs_2_.refs_3_, ...), custom_call_target="tpu_custom_call" | custom-call | flops 4000000000 | bytes 4000000 | tf_op jit(solution)/shard_map/interior/pallas_call | solution.py:168
  24.3 1.1 %collective-permute-done.3.refs_1_ = f32[2,8,1440]{2,1,0:T(8,128)S(1)} collective-permute-done((f32[2,8,1440]{2,1,0:T(8,128)S(1)}, f32[2,8,1440]{2,1,0:T(8,128)S(1)}, u32[]{:S(2)}, u32[]{:S(2)}) %collective-permute-start.3) | collective-permute-done | bytes 92192 | tf_op jit(solution)/shard_map/ppermute | solution.py:545
  25.4 1.7 %edges.3 = f32[8,12,16,128]{3,2,1,0:T(8,128)} custom-call(f32[5,8,1440]{2,1,0:T(8,128)S(1)} %collective-permute-done.below_ref, f32[4,8,1440]{2,1,0:T(8,128)S(1)} %collective-permute-done.1.above_ref, f32[7,8,1440]{2,1,0:T(8,128)S(1)} %get-tuple-element.20.edge_ref, f32[4,6,8,1536]{3,2,1,0:T(8,128)S(1)} %get-tuple-element.21.lonc_ref, ...), custom_call_target="tpu_custom_call" | custom-call | flops 1000000000 | bytes 1000000 | tf_op jit(solution)/shard_map/edges/pallas_call | solution.py:258
  27.0 6.8 %all-to-all-start = ((f32[8,12,16,128]{3,2,1,0:T(8,128)}), f32[8,12,16,128]{3,2,1,0:T(8,128)S(1)}, u32[]{:S(2)}, u32[]{:S(2)}) async-start(f32[8,12,16,128]{3,2,1,0:T(8,128)} %edges.3), calls=%async_computation | async-start | bytes 1572864 | tf_op jit(solution)/shard_map/all_to_all | solution.py:582
  33.9 1.0 copy-done.10
  34.9 1.0 copy-done.11
  35.9 4.6 %prep.1 = (bf16[16,64,192]{2,1,0:T(8,128)(2,1)S(1)}, s32[16,128]{1,0:T(8,128)S(1)}, f32[1440,16]{1,0:T(8,128)S(1)}, f32[128,16]{1,0:T(8,128)S(1)}) custom-call(f32[16,4,16,16]{3,2,1,0:T(8,128)S(1)} %copy-done.9, f32[16,3,16,16]{3,2,1,0:T(8,128)S(1)} %copy-done.10, f32[16,3,16,16]{3,2,1,0:T(8,128)S(1)} %copy-done.11, ...), custom_call_target="tpu_custom_call" | custom-call | flops 5000000000 | bytes 5000000 | tf_op jit(solution)/shard_map/prep/pallas_call | solution.py:359
  40.5 0.8 copy-done.13
  41.3 0.9 copy-done.15
  42.8 3.8 %all-to-all-done.x_ref = f32[8,12,16,128]{3,2,1,0:T(8,128)S(1)} async-done(((f32[8,12,16,128]{3,2,1,0:T(8,128)}), f32[8,12,16,128]{3,2,1,0:T(8,128)S(1)}, u32[]{:S(2)}, u32[]{:S(2)}) %all-to-all-start) | async-done | bytes 786464 | tf_op jit(solution)/shard_map/all_to_all | solution.py:582
  46.6 1.0 %copy-done.14 = bf16[16,64,192]{2,1,0:T(8,128)(2,1)S(1)} copy-done((bf16[16,64,192]{2,1,0:T(8,128)(2,1)S(1)}, bf16[16,64,192]{2,1,0:T(8,128)(2,1)}, u32[]{:S(2)}) %copy-start.14) | copy-done | bytes 393240
  47.6 4.7 %vertical.1 = f32[8,12,16,128]{3,2,1,0:T(8,128)S(1)} custom-call(f32[8,12,16,128]{3,2,1,0:T(8,128)S(1)} %all-to-all-done.x_ref, bf16[16,64,192]{2,1,0:T(8,128)(2,1)S(1)} %copy-done.14, f32[64,16,180]{2,1,0:T(8,128)S(1)} %copy-done, s32[64,16,180]{2,1,0:T(8,128)S(1)} %copy-done.1), custom_call_target="tpu_custom_call" | custom-call | flops 5000000000 | bytes 5000000 | tf_op jit(solution)/shard_map/vertical/pallas_call | solution.py:430
  52.3 17.5 %all_to_all.21.field_ref = f32[8,12,16,128]{3,2,1,0:T(8,128)S(1)} all-to-all(f32[8,12,16,128]{3,2,1,0:T(8,128)S(1)} %vertical.1), channel_id=1, replica_groups=mesh['lat'=32,'lev'=8] {'lev'}, dimensions={0} | all-to-all | bytes 1572864 | tf_op jit(solution)/shard_map/all_to_all | solution.py:584
  69.9 6.7 %regions.1 = (f32[8,16,1440]{2,1,0:T(8,128)}, f32[256,128]{1,0:T(8,128)S(1)}) custom-call(f32[8,12,16,128]{3,2,1,0:T(8,128)S(1)} %all_to_all.21.field_ref, s32[16,1440]{1,0:T(8,128)S(1)} %copy-done.12, f32[1440,16]{1,0:T(8,128)S(1)} %copy-done.16, f32[128,16]{1,0:T(8,128)S(1)} %copy-done.18, s32[16,128]{1,0:T(8,128)S(1)} %get-tuple-element.31.slot_ref), custom_call_target="tpu_custom_call" | custom-call | flops 6000000000 | bytes 6000000 | tf_op jit(solution)/shard_map/regions/pallas_call | solution.py:495
  76.5 23.9 %all_to_all.22 = f32[256,1,128]{2,1,0:T(1,128)S(1)} all-to-all(f32[256,1,128]{2,1,0:T(1,128)S(1)} %bitcast.8), channel_id=1, replica_groups=mesh['lat'=32,'lev'=8] {'lat','lev'}, dimensions={0} | all-to-all | bytes 262144 | tf_op jit(solution)/shard_map/all_to_all | solution.py:589
  100.5 1.0 %owners.1 = f32[16,64]{1,0:T(8,128)} custom-call(f32[256,128]{1,0:T(8,128)S(1)} %bitcast.7), custom_call_target="tpu_custom_call" | custom-call | tf_op jit(solution)/shard_map/owners/pallas_call | solution.py:531
  (38 shorter events, 1.3 us)
Async XLA Ops:
  0.6 9.6 %copy-start.2 = (f32[8,16,1440]{2,1,0:T(8,128)S(1)}, f32[8,16,1440]{2,1,0:T(8,128)}, u32[]{:S(2)}) copy-start(f32[8,16,1440]{2,1,0:T(8,128)} %refs_0_.3) | copy-start | bytes 2211844
  0.6 9.6 %copy-start.3 = (f32[8,16,1440]{2,1,0:T(8,128)S(1)}, f32[8,16,1440]{2,1,0:T(8,128)}, u32[]{:S(2)}) copy-start(f32[8,16,1440]{2,1,0:T(8,128)} %refs_3_.3) | copy-start | bytes 2211844
  0.6 9.6 %copy-start.4 = (s32[8,16,1440]{2,1,0:T(8,128)S(1)}, s32[8,16,1440]{2,1,0:T(8,128)}, u32[]{:S(2)}) copy-start(s32[8,16,1440]{2,1,0:T(8,128)} %refs_4_.3) | copy-start | bytes 2211844
  3.3 12.1 %collective-permute-start = (f32[5,8,1440]{2,1,0:T(8,128)}, f32[5,8,1440]{2,1,0:T(8,128)S(1)}, u32[]{:S(2)}, u32[]{:S(2)}) collective-permute-start(f32[5,8,1440]{2,1,0:T(8,128)} %get-tuple-element.18), channel_id=1, source_target_pairs={{0,8},{8,16},{16,24},{24,32},{32,40},{40,48},{48,56},{56,64},{64,7... | collective-permute-start | bytes 691208 | tf_op jit(solution)/shard_map/ppermute | solution.py:545
  8.2 7.2 %collective-permute-start.1 = (f32[4,8,1440]{2,1,0:T(8,128)}, f32[4,8,1440]{2,1,0:T(8,128)S(1)}, u32[]{:S(2)}, u32[]{:S(2)}) collective-permute-start(f32[4,8,1440]{2,1,0:T(8,128)} %get-tuple-element.19), channel_id=1, source_target_pairs={{8,0},{16,8},{24,16},{32,24},{40,32},{48,40},{56,48},{64,56},{72,6... | collective-permute-start | bytes 552968 | tf_op jit(solution)/shard_map/ppermute | solution.py:545
  10.2 1.1 %copy-start.5 = (f32[8,16,1440]{2,1,0:T(8,128)S(1)}, f32[8,16,1440]{2,1,0:T(8,128)}, u32[]{:S(2)}) copy-start(f32[8,16,1440]{2,1,0:T(8,128)} %refs_5_.1) | copy-start | bytes 2211844
  11.3 1.1 %copy-start.7 = (s32[8,16,1440]{2,1,0:T(8,128)S(1)}, s32[8,16,1440]{2,1,0:T(8,128)}, u32[]{:S(2)}) copy-start(s32[8,16,1440]{2,1,0:T(8,128)} %refs_6_.1) | copy-start | bytes 2211844
  15.4 5.9 %copy-start.6 = (f32[8,16,1440]{2,1,0:T(8,128)S(1)}, f32[8,16,1440]{2,1,0:T(8,128)}, u32[]{:S(2)}) copy-start(f32[8,16,1440]{2,1,0:T(8,128)} %refs_5_.1) | copy-start | bytes 2211844
  15.4 5.9 %copy-start.8 = (s32[8,16,1440]{2,1,0:T(8,128)S(1)}, s32[8,16,1440]{2,1,0:T(8,128)}, u32[]{:S(2)}) copy-start(s32[8,16,1440]{2,1,0:T(8,128)} %refs_6_.1) | copy-start | bytes 2211844
  15.9 8.4 %collective-permute-start.2 = (f32[2,8,1440]{2,1,0:T(8,128)S(1)}, f32[2,8,1440]{2,1,0:T(8,128)S(1)}, u32[]{:S(2)}, u32[]{:S(2)}) collective-permute-start(f32[2,8,1440]{2,1,0:T(8,128)S(1)} %get-tuple-element.24.refs_1_.refs_2_), channel_id=1, source_target_pairs={{0,8},{8,16},{16,24},{24,32},{32,40},{40,48},{48,56},{56,64},{64,7... | collective-permute-start | bytes 276488 | tf_op jit(solution)/shard_map/ppermute | solution.py:545
  19.4 5.9 %collective-permute-start.3 = (f32[2,8,1440]{2,1,0:T(8,128)S(1)}, f32[2,8,1440]{2,1,0:T(8,128)S(1)}, u32[]{:S(2)}, u32[]{:S(2)}) collective-permute-start(f32[2,8,1440]{2,1,0:T(8,128)S(1)} %get-tuple-element.25.refs_2_.refs_3_), channel_id=1, source_target_pairs={{8,0},{16,8},{24,16},{32,24},{40,32},{48,40},{56,48},{64,56},{72,6... | collective-permute-start | bytes 276488 | tf_op jit(solution)/shard_map/ppermute | solution.py:545
  27.0 6.8 %copy-start.19 = (s32[2000]{0:T(1024)S(1)}, s32[2000]{0:T(1024)}, u32[]{:S(2)}) copy-start(s32[2000]{0:T(1024)} %param.23) | copy-start | bytes 24004
  27.0 6.8 %copy-start.9 = (f32[16,4,16,16]{3,2,1,0:T(8,128)S(1)}, f32[16,4,16,16]{3,2,1,0:T(8,128)}, u32[]{:S(2)}) copy-start(f32[16,4,16,16]{3,2,1,0:T(8,128)} %inverse_ref.1) | copy-start | bytes 196612
  27.0 6.8 %copy-start.12 = (s32[16,1440]{1,0:T(8,128)S(1)}, s32[16,1440]{1,0:T(8,128)}, u32[]{:S(2)}) copy-start(s32[16,1440]{1,0:T(8,128)} %ids_ref.3) | copy-start | bytes 276484
  27.0 19.6 %all-to-all-start = ((f32[8,12,16,128]{3,2,1,0:T(8,128)}), f32[8,12,16,128]{3,2,1,0:T(8,128)S(1)}, u32[]{:S(2)}, u32[]{:S(2)}) async-start(f32[8,12,16,128]{3,2,1,0:T(8,128)} %edges.3), calls=%async_computation | async-start | bytes 1572864 | tf_op jit(solution)/shard_map/all_to_all | solution.py:582
  33.9 1.0 copy-start.10
  34.9 1.0 copy-start.11
  35.9 10.7 %copy-start = (f32[64,16,180]{2,1,0:T(8,128)S(1)}, f32[64,16,180]{2,1,0:T(8,128)}, u32[]{:S(2)}) copy-start(f32[64,16,180]{2,1,0:T(8,128)} %c_ref.1) | copy-start | bytes 2211844
  35.9 10.7 %copy-start.1 = (s32[64,16,180]{2,1,0:T(8,128)S(1)}, s32[64,16,180]{2,1,0:T(8,128)}, u32[]{:S(2)}) copy-start(s32[64,16,180]{2,1,0:T(8,128)} %k_ref.1) | copy-start | bytes 2211844
  40.5 0.8 copy-start.13
  41.3 0.9 copy-start.15
  46.6 1.0 %copy-start.14 = (bf16[16,64,192]{2,1,0:T(8,128)(2,1)S(1)}, bf16[16,64,192]{2,1,0:T(8,128)(2,1)}, u32[]{:S(2)}) copy-start(bf16[16,64,192]{2,1,0:T(8,128)(2,1)} %copy-done.13) | copy-start | bytes 1179652
  52.3 17.6 %copy-start.16 = (f32[1440,16]{1,0:T(8,128)S(1)}, f32[1440,16]{1,0:T(8,128)}, u32[]{:S(2)}) copy-start(f32[1440,16]{1,0:T(8,128)} %copy-done.15) | copy-start | bytes 276484
  52.3 17.6 %copy-start.18 = (f32[128,16]{1,0:T(8,128)S(1)}, f32[128,16]{1,0:T(8,128)}, u32[]{:S(2)}) copy-start(f32[128,16]{1,0:T(8,128)} %copy-done.17) | copy-start | bytes 24580
  (1 other events, 0.6 us)

commit v3 on v2

--- a/solution.py
+++ b/solution.py
@@ -11,6 +11,7 @@
 SLOTS = 16
 LANES = 128
 HALF = LANES // 2
+LANE_BITS = 7
 F32 = jnp.float32
 BF16 = jnp.bfloat16
 VMEM = pl.BlockSpec(memory_space=pltpu.VMEM)
@@ -267,48 +268,45 @@
     )(*args)
 
 
-def pack_kernel(*refs):
-    *sources, up_ref, down_ref, a_ref, clat_ref, klat_ref, sems = refs
-    fields = (a_ref, clat_ref, klat_ref)
-    levels, rows, _ = a_ref.shape
-    half = levels // 2
-    copies = []
-    for n, (src, dst) in enumerate(zip(sources, fields)):
-        for part in range(2):
-            span = pl.ds(part * half, half)
-            copies.append(pltpu.make_async_copy(src.at[span], dst.at[span], sems.at[n, part]))
+def pack_kernel(a_in, c_in, k_in, up_ref, down_ref, high_ref, low_ref, sems):
+    edge = a_in.shape[1] - 1
+    moves = (
+        (k_in, edge, high_ref),
+        (k_in, 0, low_ref),
+        (a_in, edge, up_ref.at[0]),
+        (a_in, edge - 1, up_ref.at[1]),
+        (c_in, edge, up_ref.at[2]),
+        (c_in, edge - 1, up_ref.at[3]),
+        (a_in, 0, down_ref.at[0]),
+        (a_in, 1, down_ref.at[1]),
+        (c_in, 0, down_ref.at[2]),
+    )
+    copies = [pltpu.make_async_copy(src.at[:, row, :], dst, sems.at[n]) for n, (src, row, dst) in enumerate(moves)]
     for copy in copies:
         copy.start()
     for copy in copies:
         copy.wait()
-    edge = rows - 1
-    up_ref[0] = a_ref[:, edge, :]
-    up_ref[1] = a_ref[:, edge - 1, :]
-    down_ref[0] = a_ref[:, 0, :]
-    down_ref[1] = a_ref[:, 1, :]
-    up_ref[2] = clat_ref[:, edge, :]
-    up_ref[3] = clat_ref[:, edge - 1, :]
-    down_ref[2] = clat_ref[:, 0, :]
-    up_ref[4] = klat_ref[:, edge, :].astype(F32)
-    down_ref[3] = klat_ref[:, 0, :].astype(F32)
+    up_ref[4] = high_ref[...].astype(F32)
+    down_ref[3] = low_ref[...].astype(F32)
 
 
 def pack(a, clat, klat):
     levels, _, lons = a.shape
+    row = (levels, lons)
     return pl.pallas_call(
         pack_kernel,
-        out_shape=(jax.ShapeDtypeStruct((5, levels, lons), F32), jax.ShapeDtypeStruct((4, levels, lons), F32)),
+        out_shape=(jax.ShapeDtypeStruct((5, *row), F32), jax.ShapeDtypeStruct((4, *row), F32)),
         in_specs=[HBM] * 3,
         out_specs=(VMEM, VMEM),
-        scratch_shapes=[pltpu.VMEM(a.shape, x.dtype) for x in (a, clat, klat)] + [pltpu.SemaphoreType.DMA((3, 2))],
-        compiler_params=params(60),
+        scratch_shapes=[pltpu.VMEM(row, klat.dtype)] * 2 + [pltpu.SemaphoreType.DMA((9,))],
+        compiler_params=params(58),
         cost_estimate=cost(2),
         name="pack",
     )(a, clat, klat)
 
 
 def prep_kernel(
-    inverse_ref, lower_ref, upper_ref, owner_ref, ids_ref, matrix_ref, slot_ref, fine_ref, device_ref, *, devices
+    inverse_ref, lower_ref, upper_ref, owner_ref, ids_ref, matrix_ref, slot_ref, coarse_ref, fine_ref, device_ref, *, devices, parts
 ):
     lats, blocks, size, _ = inverse_ref.shape
     group = LANES // size
@@ -349,23 +347,33 @@
         before = jnp.dot(owned.astype(BF16), earlier, preferred_element_type=F32) + running
         slot_ref[pl.ds(t, 1), :] = jnp.sum(owned * before, axis=0, keepdims=True).astype(jnp.int32)
         running = running + jnp.sum(owned, axis=1, keepdims=True)
-    fine_ref[...] = (ids_ref[...] % LANES).astype(F32).T
+    ids = ids_ref[...]
+    share = ids.shape[1] // parts
+    gap = jnp.full((lats, HALF - (share - LANES)), -1, jnp.int32)
+    pieces = [ids[:, part * share : part * share + LANES] for part in range(parts)]
+    for part in range(parts):
+        pieces += [ids[:, part * share + LANES : (part + 1) * share], gap]
+    ids = jnp.concatenate(pieces, axis=1)
+    coarse_ref[...] = (ids >> LANE_BITS).astype(F32)
+    fine_ref[...] = (ids & (LANES - 1)).astype(F32).T
     device_ref[...] = owner_ref[...].astype(F32).T
 
 
-def prep(inverse, lower, upper, owner_tiles, ids, devices):
+def prep(inverse, lower, upper, owner_tiles, ids, devices, parts):
     lats, blocks, size, _ = inverse.shape
+    width = parts * (LANES + HALF)
     levels = blocks * size
     return pl.pallas_call(
-        functools.partial(prep_kernel, devices=devices),
+        functools.partial(prep_kernel, devices=devices, parts=parts),
         out_shape=(
             jax.ShapeDtypeStruct((lats, levels, 3 * levels), BF16),
             jax.ShapeDtypeStruct(owner_tiles.shape, jnp.int32),
-            jax.ShapeDtypeStruct(ids.shape[::-1], F32),
+            jax.ShapeDtypeStruct((lats, width), F32),
+            jax.ShapeDtypeStruct((width, lats), F32),
             jax.ShapeDtypeStruct(owner_tiles.shape[::-1], F32),
         ),
         in_specs=[VMEM] * 5,
-        out_specs=(VMEM,) * 4,
+        out_specs=(VMEM,) * 5,
         compiler_params=params(),
         cost_estimate=cost(5),
         name="prep",
@@ -378,37 +386,52 @@
     return jnp.concatenate([main, rest[..., :spare]], axis=-1)
 
 
-def vertical_kernel(x_ref, matrix_ref, c_ref, k_ref, out_ref, field_ref, y_ref):
+def column_rows(ref, part, lat, group, rows):
+    half = group // 2
+    first = part * (group + half) * rows + lat
+    main = ref[pl.ds(first, group, stride=rows), :]
+    return main, ref[pl.ds(first + group * rows, half, stride=rows), :]
+
+
+def vertical_kernel(x_ref, matrix_ref, c_ref, k_ref, out_ref, main_ref, rest_ref, *, group):
     levels, rows, share = c_ref.shape
-    parts = x_ref.shape[0]
-    group = levels // parts
     half = group // 2
+    parts = levels // group
     spare = share - LANES
-    for level in range(levels):
-        part, l = level // group, level % group
-        field_ref[level] = unpacked(x_ref[part, l], x_ref[part, group + l % half], l // half, spare)
     for lat in range(rows):
-        high, low = split(field_ref[:, lat, :])
+        mains, rests = [], []
+        for part in range(parts):
+            main, rest = column_rows(x_ref, part, lat, group, rows)
+            mains.append(main)
+            rests += [rest, roll(rest, HALF, 1)]
+        x = jnp.concatenate([jnp.concatenate(mains, axis=0), jnp.concatenate(rests, axis=0)], axis=1)
+        high, low = split(x)
         stacked = jnp.concatenate([high, high, low], axis=0)
-        y_ref[:, lat, :] = jnp.dot(matrix_ref[lat], stacked, preferred_element_type=F32)
+        y = jnp.dot(matrix_ref[lat], stacked, preferred_element_type=F32)
+        main_ref[pl.ds(lat, levels, stride=rows), :] = y[:, :LANES]
+        rest_ref[pl.ds(lat, levels, stride=rows), :] = y[:, LANES:]
+
+    def y_at(level):
+        band = slice(level * rows, (level + 1) * rows)
+        return jnp.concatenate([main_ref[band, :], rest_ref[band, :spare]], axis=1)
 
     def emit(level, value):
         part, l = level // group, level % group
-        out_ref[part, l] = value[:, :LANES]
-        place = group + l % half
-        if l // half:
-            out_ref[part, place, :, HALF : HALF + spare] = value[:, LANES:]
-        else:
-            out_ref[part, place, :, :spare] = value[:, LANES:]
+        first = part * (group + half) * rows
+        band = slice(first + l * rows, first + (l + 1) * rows)
+        out_ref[band, :] = value[:, :LANES]
+        place = first + (group + l % half) * rows
+        side = l // half * HALF
+        out_ref[place : place + rows, side : side + spare] = value[:, LANES:]
 
     zero = jnp.zeros((rows, share), F32)
-    y = y_ref[0]
+    y = y_at(0)
     prior_w, prior_q, pending = zero, zero, None
     for i in range(levels):
         ahead, behind = slope_parts(k_ref[i])
         if i < levels - 1:
             up, down, uph, downh = flux_parts(c_ref[i])
-            y_next = y_ref[i + 1]
+            y_next = y_at(i + 1)
             f = y_next - y
             s = uph * f - prior_w
             here = y + up * f + prior_q
@@ -426,87 +449,101 @@
     emit(levels - 1, pending)
 
 
-def vertical(x, matrix, courant, codes):
-    return pl.pallas_call(
-        vertical_kernel,
+def vertical(x, matrix, courant, codes, group):
+    levels, rows, _ = courant.shape
+    return pl.pallas_call(
+        functools.partial(vertical_kernel, group=group),
         out_shape=jax.ShapeDtypeStruct(x.shape, F32),
         in_specs=[VMEM] * 4,
         out_specs=VMEM,
-        scratch_shapes=[pltpu.VMEM(courant.shape, F32)] * 2,
+        scratch_shapes=[pltpu.VMEM((levels * rows, LANES), F32)] * 2,
         compiler_params=params(),
         cost_estimate=cost(5),
         name="vertical",
     )(x, matrix, courant, codes)
 
 
-def region_kernel(
-    field_ref, ids_ref, fine_ref, device_ref, slot_ref, out_ref, send_ref, high_ref, low_ref, acc_ref, table_ref, *, scale
-):
-    levels, rows, lons = out_ref.shape
+def whole_row(field_ref, l, levels, lons):
     parts = field_ref.shape[0]
-    share = lons // parts
+    half = levels // 2
+    spare = lons // parts - LANES
+    return jnp.concatenate(
+        [unpacked(field_ref[p, l], field_ref[p, levels + l % half], l // half, spare) for p in range(parts)], axis=1
+    )
+
+
+def rejoin_kernel(field_ref, out_ref):
+    levels, _, lons = out_ref.shape
+    for l in range(levels):
+        out_ref[l] = whole_row(field_ref, l, levels, lons)
+
+
+def rejoin(field, shape):
+    return pl.pallas_call(
+        rejoin_kernel,
+        out_shape=jax.ShapeDtypeStruct(shape, F32),
+        in_specs=[VMEM],
+        out_specs=VMEM,
+        compiler_params=params(),
+        cost_estimate=cost(2),
+        name="rejoin",
+    )(field)
+
+
+def region_kernel(field_ref, coarse_ref, fine_ref, device_ref, slot_ref, send_ref, acc_ref, *, levels, scale):
+    rows, width = coarse_ref.shape
+    parts = width // (LANES + HALF)
     half = levels // 2
     tiles = slot_ref.shape[0]
     devices = send_ref.shape[0]
-    for l in range(levels):
-        pieces = [
-            unpacked(field_ref[part, l], field_ref[part, levels + l % half], l // half, share - LANES)
-            for part in range(parts)
-        ]
-        whole = jnp.concatenate(pieces, axis=1)
-        out_ref[l] = whole
-        high = whole.astype(BF16).astype(F32)
-        high_ref[l] = high
-        low_ref[l] = whole - high
-    coarse = lax.broadcasted_iota(jnp.int32, (tiles, lons), 0)
-    lane = lax.broadcasted_iota(jnp.int32, (lons, LANES), 1).astype(F32)
+    lane = lax.broadcasted_iota(jnp.int32, (width, LANES), 1).astype(F32)
+    lower = lax.broadcasted_iota(jnp.int32, (half, LANES), 1) < HALF
     for lat in range(rows):
-        mask = jnp.where((ids_ref[lat : lat + 1, :] // LANES) == coarse, 1.0, 0.0).astype(BF16)
+        mains, rests = [], []
+        for part in range(parts):
+            main, rest = column_rows(field_ref, part, lat, levels, rows)
+            mains.append(main)
+            rests.append(rest)
+        for even, odd in zip(rests[::2], rests[1::2]):
+            first = jnp.where(lower, even, roll(odd, HALF, 1))
+            second = jnp.where(lower, roll(even, HALF, 1), odd)
+            mains.append(jnp.concatenate([first, second], axis=0))
+        field = jnp.concatenate(mains, axis=1)
+        high = field.astype(BF16).astype(F32)
+        both = jnp.concatenate([high, field - high], axis=0)
+        coarse = jnp.broadcast_to(coarse_ref[lat : lat + 1, :], both.shape)
         onehot = jnp.where(fine_ref[:, lat : lat + 1] == lane, 1.0, 0.0).astype(BF16)
-        pieces = []
-        for ref in (high_ref, low_ref):
-            for l in range(levels):
-                row = jnp.broadcast_to(ref[l, lat : lat + 1, :], (tiles, lons))
-                pieces.append(row.astype(BF16) * mask)
-        stacked = jnp.concatenate(pieces, axis=0)
+        stacked = jnp.concatenate([jnp.where(coarse == t, both, 0.0).astype(BF16) for t in range(tiles)], axis=0)
         term = jnp.dot(stacked, onehot, preferred_element_type=F32)
         if lat == 0:
             acc_ref[...] = term
         else:
             acc_ref[...] += term
-    size = levels * tiles
-    table_ref[...] = acc_ref[pl.ds(0, size), :] + acc_ref[pl.ds(size, size), :]
     device = lax.broadcasted_iota(jnp.int32, (LANES, devices), 1).astype(F32)
     place = lax.broadcasted_iota(jnp.int32, (SLOTS * levels, LANES), 0) // levels
     total = jnp.zeros((SLOTS * levels, devices), F32)
     for t in range(tiles):
         owned = jnp.where(device_ref[:, t : t + 1] == device, 1.0, 0.0).astype(BF16)
-        sums = table_ref[pl.ds(t, levels, stride=tiles), :]
+        base = 2 * levels * t
+        sums = acc_ref[base : base + levels, :] + acc_ref[base + levels : base + 2 * levels, :]
         spread = jnp.where(slot_ref[t : t + 1, :] == place, jnp.concatenate([sums] * SLOTS, axis=0), 0.0)
         for piece in split(spread):
             total += jnp.dot(piece, owned, preferred_element_type=F32)
     send_ref[...] = (total * scale).T
 
 
-def regions(field, ids, fine, device, slot_tiles, levels, devices, scale):
+def regions(field, coarse, fine, device, slot_tiles, levels, devices, scale):
     tiles = slot_tiles.shape[0]
-    rows, lons = ids.shape
-    whole = (levels, rows, lons)
-    return pl.pallas_call(
-        functools.partial(region_kernel, scale=scale),
-        out_shape=(jax.ShapeDtypeStruct(whole, F32), jax.ShapeDtypeStruct((devices, SLOTS * levels), F32)),
+    return pl.pallas_call(
+        functools.partial(region_kernel, levels=levels, scale=scale),
+        out_shape=jax.ShapeDtypeStruct((devices, SLOTS * levels), F32),
         in_specs=[VMEM] * 5,
-        out_specs=(VMEM, VMEM),
-        scratch_shapes=[
-            pltpu.VMEM(whole, F32),
-            pltpu.VMEM(whole, F32),
-            pltpu.VMEM((2 * levels * tiles, LANES), F32),
-            pltpu.VMEM((levels * tiles, LANES), F32),
-        ],
+        out_specs=VMEM,
+        scratch_shapes=[pltpu.VMEM((2 * levels * tiles, LANES), F32)],
         compiler_params=params(),
         cost_estimate=cost(6),
         name="regions",
-    )(field, ids, fine, device, slot_tiles)
+    )(field, coarse, fine, device, slot_tiles)
 
 
 def owners_kernel(rows_ref, out_ref):
@@ -567,8 +604,8 @@
     tiles = -(-region_count // LANES)
     tiles = -(-tiles // 8) * 8
     owner_tiles = jnp.pad(owner, (0, tiles * LANES - region_count), constant_values=-1).reshape(tiles, LANES)
-    matrix, slot_tiles, fine, device = prep(
-        block_inverse, block_lower, block_upper, owner_tiles, region_ids, devices
+    matrix, slot_tiles, coarse, fine, device = prep(
+        block_inverse, block_lower, block_upper, owner_tiles, region_ids, devices, group_count
     )
     last = (lax.axis_index("lat") == band_count - 1).astype(jnp.int32).reshape(1)
     up, down = pack(adjoint_in, courant_lat, codes_lat)
@@ -580,13 +617,12 @@
     sent, swept = interior(last, (adjoint, up, down), coefficients, group_count)
     sent = edges(below, above, edge, lonc, swept, below_next, above_next, up, down, sent)
     columns = lax.all_to_all(sent, "lev", split_axis=0, concat_axis=0, tiled=True)
-    columns = vertical(columns, matrix, courant_lev, codes_lev)
-    field = lax.all_to_all(columns, "lev", split_axis=0, concat_axis=0, tiled=True)
+    columns = vertical(columns.reshape(-1, LANES), matrix, courant_lev, codes_lev, levels_here)
+    field = lax.all_to_all(columns.reshape(sent.shape), "lev", split_axis=0, concat_axis=0, tiled=True)
     scale = (region_count / (bands_here * band_count * lon_cells)) ** 0.5
-    adjoint_out, rows = regions(
-        field, region_ids, fine, device, slot_tiles, levels_here, devices, scale
-    )
+    rows = regions(field.reshape(-1, LANES), coarse, fine, device, slot_tiles, levels_here, devices, scale)
     rows = lax.all_to_all(rows, ("lat", "lev"), split_axis=0, concat_axis=0, tiled=True)
+    adjoint_out = rejoin(field, adjoint_in.shape)
     region_sens = owners(rows, group_count, levels_here)
     return (adjoint_out, region_sens)
 

time: 102 us -> 97.9 us (0.960)
  blocking collectives: 41.5 us -> 17.6 us
  waiting for transfers between devices: 5.05 us -> 16 us
  starting transfers between devices: 19.1 us -> 29.9 us
  Pallas kernels: 27.4 us -> 24.6 us
    all_to_all x2 -> x1, blocking collectives: 41.5 us -> 17.6 us  [local(): lax.all_to_all(columns.reshape(sent.shape), 'lev', split_axis=0, concat_a...]
    all_to_all x0 -> x1, waiting for transfers between devices: none -> 11.6 us  [local(): lax.all_to_all(rows, ('lat', 'lev'), split_axis=0, concat_axis=0, tiled=T...]
    all_to_all x0 -> x1, starting transfers between devices: none -> 10.9 us  [local(): lax.all_to_all(rows, ('lat', 'lev'), split_axis=0, concat_axis=0, tiled=T...]
    pallas_call x4 -> x5, Pallas kernels: 18.5 us -> 15.8 us  [the longest x1 6.09 us: regions(): pl.pallas_call(functools.partial(region_kernel, levels=levels, scale=scal...]
    unnamed x40 -> x44, local copies, waits for them, and re-layouts: 7.65 us -> 8.32 us
  transfers between devices with their start and end apart: 5 -> 6, of which waited for: 3 -> 4; matrix products, arithmetic and copies ran while one was open for 0% -> 0% of each run, Pallas kernels for 10% -> 12%
where the time goes in v3:
time: 97.9 us; the launch traced here: 97.3 us
  starting transfers between devices  29.9 us (31%)
  Pallas kernels  24.6 us (25%)
  blocking collectives  17.6 us (18%)
  waiting for transfers between devices  16 us (16%)
  local copies, waits for them, and re-layouts  8.32 us (8%)
    all_to_all x1, blocking collectives, local(): lax.all_to_all(columns.reshape(sent.shape), 'lev', split_axis=0, concat_a...  17.6 us
    all_to_all x1, waiting for transfers between devices, local(): lax.all_to_all(rows, ('lat', 'lev'), split_axis=0, concat_axis=0, tiled=T...  11.6 us
    all_to_all x1, starting transfers between devices, local(): lax.all_to_all(rows, ('lat', 'lev'), split_axis=0, concat_axis=0, tiled=T...  10.9 us
    ppermute x2, starting transfers between devices, neighbours(): lax.ppermute(up, 'lat', forward)  8.44 us
    unnamed x44, local copies, waits for them, and re-layouts  8.32 us
    all_to_all x1, starting transfers between devices, local(): lax.all_to_all(sent, 'lev', split_axis=0, concat_axis=0, tiled=True)  6.78 us
    pallas_call x1, Pallas kernels, regions(): pl.pallas_call(functools.partial(region_kernel, levels=levels, scale=scal...  6.09 us
    pallas_call x2, Pallas kernels, interior(): pl.pallas_call(functools.partial(interior_kernel, final=final), out_shape...  5.7 us
  transfers between devices with their start and end apart: 6, of which 4 were waited for; matrix products, arithmetic and copies ran while one was open for 0% of the time, Pallas kernels for 12%

profile of v3, /device:TPU:1, one launch (start us, length us, event | category | flops | bytes accessed | tf_op | source)
XLA Modules:
  0.0 97.3 jit_solution(2619870865692582150)
XLA Ops:
  0.7 2.0 %pack.1 = (f32[5,8,1440]{2,1,0:T(8,128)}, f32[4,8,1440]{2,1,0:T(8,128)}) custom-call(f32[8,16,1440]{2,1,0:T(8,128)} %refs_0_.1, f32[8,16,1440]{2,1,0:T(8,128)} %refs_3_.3, s32[8,16,1440]{2,1,0:T(8,128)} %refs_4_.3), custom_call_target="tpu_custom_call" | custom-call | flops 2000000000 | bytes 2000000 | tf_op jit(solution)/shard_map/pack/pallas_call | solution.py:296
  2.7 4.9 %collective-permute-start = (f32[5,8,1440]{2,1,0:T(8,128)}, f32[5,8,1440]{2,1,0:T(8,128)S(1)}, u32[]{:S(2)}, u32[]{:S(2)}) collective-permute-start(f32[5,8,1440]{2,1,0:T(8,128)} %get-tuple-element.17), channel_id=1, source_target_pairs={{0,8},{8,16},{16,24},{24,32},{32,40},{40,48},{48,56},{56,64},{64,7... | collective-permute-start | bytes 691208 | tf_op jit(solution)/shard_map/ppermute | solution.py:582
  7.7 1.9 %collective-permute-start.1 = (f32[4,8,1440]{2,1,0:T(8,128)}, f32[4,8,1440]{2,1,0:T(8,128)S(1)}, u32[]{:S(2)}, u32[]{:S(2)}) collective-permute-start(f32[4,8,1440]{2,1,0:T(8,128)} %get-tuple-element.18), channel_id=1, source_target_pairs={{8,0},{16,8},{24,16},{32,24},{40,32},{48,40},{56,48},{64,56},{72,6... | collective-permute-start | bytes 552968 | tf_op jit(solution)/shard_map/ppermute | solution.py:582
  9.6 1.1 %copy-done.5 = f32[8,16,1440]{2,1,0:T(8,128)S(1)} copy-done((f32[8,16,1440]{2,1,0:T(8,128)S(1)}, f32[8,16,1440]{2,1,0:T(8,128)}, u32[]{:S(2)}) %copy-start.5) | copy-done | bytes 737304
  10.8 1.1 %copy-done.7 = s32[8,16,1440]{2,1,0:T(8,128)S(1)} copy-done((s32[8,16,1440]{2,1,0:T(8,128)S(1)}, s32[8,16,1440]{2,1,0:T(8,128)}, u32[]{:S(2)}) %copy-start.7) | copy-done | bytes 737304
  11.9 2.8 %interior.2 = (f32[8,16,1440]{2,1,0:T(8,128)S(1)}, f32[4,8,1440]{2,1,0:T(8,128)S(1)}, f32[7,8,1440]{2,1,0:T(8,128)S(1)}, f32[4,6,8,1536]{3,2,1,0:T(8,128)S(1)}) custom-call(s32[1]{0:T(128)} %bitcast.last_ref, f32[8,16,1440]{2,1,0:T(8,128)S(1)} %copy-done.2, f32[8,16,1440]{2,1,0:T(8,128)S(1)} %copy-done.3, s32[8,16,1440]{2,1,0:T(8,128)S(1)} %copy-done.4, ...), custom_call_target="tpu_custom_call" | custom-call | flops 4000000000 | bytes 4000000 | tf_op jit(solution)/shard_map/interior/pallas_call | solution.py:169
  15.3 3.5 %collective-permute-start.2 = (f32[2,8,1440]{2,1,0:T(8,128)S(1)}, f32[2,8,1440]{2,1,0:T(8,128)S(1)}, u32[]{:S(2)}, u32[]{:S(2)}) collective-permute-start(f32[2,8,1440]{2,1,0:T(8,128)S(1)} %get-tuple-element.23.refs_1_.refs_2_), channel_id=1, source_target_pairs={{0,8},{8,16},{16,24},{24,32},{32,40},{40,48},{48,56},{56,64},{64,7... | collective-permute-start | bytes 276488 | tf_op jit(solution)/shard_map/ppermute | solution.py:582
  18.8 1.9 %collective-permute-start.3 = (f32[2,8,1440]{2,1,0:T(8,128)S(1)}, f32[2,8,1440]{2,1,0:T(8,128)S(1)}, u32[]{:S(2)}, u32[]{:S(2)}) collective-permute-start(f32[2,8,1440]{2,1,0:T(8,128)S(1)} %get-tuple-element.24.refs_2_.refs_3_), channel_id=1, source_target_pairs={{8,0},{16,8},{24,16},{32,24},{40,32},{48,40},{56,48},{64,56},{72,6... | collective-permute-start | bytes 276488 | tf_op jit(solution)/shard_map/ppermute | solution.py:582
  20.8 2.9 %interior.3 = (f32[8,12,16,128]{3,2,1,0:T(8,128)S(1)}, f32[4,8,1440]{2,1,0:T(8,128)S(1)}) custom-call(s32[1]{0:T(128)} %bitcast.last_ref, f32[8,16,1440]{2,1,0:T(8,128)S(1)} %get-tuple-element.21.refs_0_, f32[2,8,1440]{2,1,0:T(8,128)S(1)} %get-tuple-element.23.refs_1_.refs_2_, f32[2,8,1440]{2,1,0:T(8,128)S(1)} %get-tuple-element.24.refs_2_.refs_3_, ...), custom_call_target="tpu_custom_call" | custom-call | flops 4000000000 | bytes 4000000 | tf_op jit(solution)/shard_map/interior/pallas_call | solution.py:169
  23.7 1.1 %collective-permute-done.3.refs_1_ = f32[2,8,1440]{2,1,0:T(8,128)S(1)} collective-permute-done((f32[2,8,1440]{2,1,0:T(8,128)S(1)}, f32[2,8,1440]{2,1,0:T(8,128)S(1)}, u32[]{:S(2)}, u32[]{:S(2)}) %collective-permute-start.3) | collective-permute-done | bytes 92192 | tf_op jit(solution)/shard_map/ppermute | solution.py:582
  24.8 1.7 %edges.3 = f32[8,12,16,128]{3,2,1,0:T(8,128)} custom-call(f32[5,8,1440]{2,1,0:T(8,128)S(1)} %collective-permute-done.below_ref, f32[4,8,1440]{2,1,0:T(8,128)S(1)} %collective-permute-done.1.above_ref, f32[7,8,1440]{2,1,0:T(8,128)S(1)} %get-tuple-element.19.edge_ref, f32[4,6,8,1536]{3,2,1,0:T(8,128)S(1)} %get-tuple-element.20.lonc_ref, ...), custom_call_target="tpu_custom_call" | custom-call | flops 1000000000 | bytes 1000000 | tf_op jit(solution)/shard_map/edges/pallas_call | solution.py:259
  26.4 6.8 %all-to-all-start = ((f32[8,12,16,128]{3,2,1,0:T(8,128)}), f32[8,12,16,128]{3,2,1,0:T(8,128)S(1)}, u32[]{:S(2)}, u32[]{:S(2)}) async-start(f32[8,12,16,128]{3,2,1,0:T(8,128)} %edges.3), calls=%async_computation | async-start | bytes 1572864 | tf_op jit(solution)/shard_map/all_to_all | solution.py:619
  33.3 1.0 %copy-done.10 = f32[16,3,16,16]{3,2,1,0:T(8,128)S(1)} copy-done((f32[16,3,16,16]{3,2,1,0:T(8,128)S(1)}, f32[16,3,16,16]{3,2,1,0:T(8,128)}, u32[]{:S(2)}) %copy-start.10) | copy-done | bytes 49176
  34.3 1.0 %copy-done.11 = f32[16,3,16,16]{3,2,1,0:T(8,128)S(1)} copy-done((f32[16,3,16,16]{3,2,1,0:T(8,128)S(1)}, f32[16,3,16,16]{3,2,1,0:T(8,128)}, u32[]{:S(2)}) %copy-start.11) | copy-done | bytes 49176
  35.3 4.6 %prep.1 = (bf16[16,64,192]{2,1,0:T(8,128)(2,1)S(1)}, s32[16,128]{1,0:T(8,128)S(1)}, f32[16,1536]{1,0:T(8,128)S(1)}, f32[1536,16]{1,0:T(8,128)S(1)}, f32[128,16]{1,0:T(8,128)S(1)}) custom-call(f32[16,4,16,16]{3,2,1,0:T(8,128)S(1)} %copy-done.9, f32[16,3,16,16]{3,2,1,0:T(8,128)S(1)} %copy-done.10, f32[16,3,16,16]{3,2,1,0:T(8,128)S(1)} %copy-done.11, ...), custom_call_target="tpu_custom_call" | custom-call | flops 5000000000 | bytes 5000000 | tf_op jit(solution)/shard_map/prep/pallas_call | solution.py:366
  42.9 3.2 %all-to-all-done = f32[8,12,16,128]{3,2,1,0:T(8,128)S(1)} async-done(((f32[8,12,16,128]{3,2,1,0:T(8,128)}), f32[8,12,16,128]{3,2,1,0:T(8,128)S(1)}, u32[]{:S(2)}, u32[]{:S(2)}) %all-to-all-start) | async-done | bytes 786464 | tf_op jit(solution)/shard_map/all_to_all | solution.py:619
  46.0 1.0 %copy-done.16 = bf16[16,64,192]{2,1,0:T(8,128)(2,1)S(1)} copy-done((bf16[16,64,192]{2,1,0:T(8,128)(2,1)S(1)}, bf16[16,64,192]{2,1,0:T(8,128)(2,1)}, u32[]{:S(2)}) %copy-start.16) | copy-done | bytes 393240
  47.1 1.6 %vertical.1 = f32[1536,128]{1,0:T(8,128)S(1)} custom-call(f32[1536,128]{1,0:T(8,128)S(1)} %bitcast.10, bf16[16,64,192]{2,1,0:T(8,128)(2,1)S(1)} %copy-done.16, f32[64,16,180]{2,1,0:T(8,128)S(1)} %copy-done, s32[64,16,180]{2,1,0:T(8,128)S(1)} %copy-done.1), custom_call_target="tpu_custom_call" | custom-call | flops 5000000000 | bytes 5000000 | tf_op jit(solution)/shard_map/vertical/pallas_call | solution.py:454
  48.7 17.6 %all_to_all.21.field_ref = f32[8,12,16,128]{3,2,1,0:T(8,128)S(1)} all-to-all(f32[8,12,16,128]{3,2,1,0:T(8,128)S(1)} %bitcast.12), channel_id=1, replica_groups=mesh['lat'=32,'lev'=8] {'lev'}, dimensions={0} | all-to-all | bytes 1572864 | tf_op jit(solution)/shard_map/all_to_all | solution.py:621
  66.3 6.1 %regions.1 = f32[256,128]{1,0:T(8,128)} custom-call(f32[1536,128]{1,0:T(8,128)S(1)} %bitcast.11, f32[16,1536]{1,0:T(8,128)S(1)} %copy-done.18, f32[1536,16]{1,0:T(8,128)S(1)} %copy-done.14, f32[128,16]{1,0:T(8,128)S(1)} %copy-done.20, s32[16,128]{1,0:T(8,128)S(1)} %get-tuple-element.31.slot_ref), custom_call_target="tpu_custom_call" | custom-call | flops 6000000000 | bytes 6000000 | tf_op jit(solution)/shard_map/regions/pallas_call | solution.py:537
  72.4 10.9 %all-to-all-start.2 = ((f32[256,1,128]{2,1,0:T(1,128)}), f32[256,1,128]{2,1,0:T(1,128)S(1)}, u32[]{:S(2)}, u32[]{:S(2)}) async-start(f32[256,1,128]{2,1,0:T(1,128)} %bitcast.6), calls=%async_computation.2 | async-start | bytes 262144 | tf_op jit(solution)/shard_map/all_to_all | solution.py:624
  83.3 1.4 %rejoin.1 = f32[8,16,1440]{2,1,0:T(8,128)} custom-call(f32[8,12,16,128]{3,2,1,0:T(8,128)S(1)} %all_to_all.21.field_ref), custom_call_target="tpu_custom_call" | custom-call | flops 2000000000 | bytes 2000000 | tf_op jit(solution)/shard_map/rejoin/pallas_call | solution.py:482
  84.7 11.6 %all-to-all-done.2 = f32[256,1,128]{2,1,0:T(1,128)S(1)} async-done(((f32[256,1,128]{2,1,0:T(1,128)}), f32[256,1,128]{2,1,0:T(1,128)S(1)}, u32[]{:S(2)}, u32[]{:S(2)}) %all-to-all-start.2) | async-done | bytes 131104 | tf_op jit(solution)/shard_map/all_to_all | solution.py:624
  96.3 1.0 %owners.1 = f32[16,64]{1,0:T(8,128)} custom-call(f32[256,128]{1,0:T(8,128)S(1)} %bitcast.13), custom_call_target="tpu_custom_call" | custom-call | tf_op jit(solution)/shard_map/owners/pallas_call | solution.py:568
  (44 shorter events, 3.7 us)
Async XLA Ops:
  0.6 9.0 %copy-start.2 = (f32[8,16,1440]{2,1,0:T(8,128)S(1)}, f32[8,16,1440]{2,1,0:T(8,128)}, u32[]{:S(2)}) copy-start(f32[8,16,1440]{2,1,0:T(8,128)} %refs_0_.1) | copy-start | bytes 2211844
  0.6 9.0 %copy-start.3 = (f32[8,16,1440]{2,1,0:T(8,128)S(1)}, f32[8,16,1440]{2,1,0:T(8,128)}, u32[]{:S(2)}) copy-start(f32[8,16,1440]{2,1,0:T(8,128)} %refs_3_.3) | copy-start | bytes 2211844
  0.6 9.0 %copy-start.4 = (s32[8,16,1440]{2,1,0:T(8,128)S(1)}, s32[8,16,1440]{2,1,0:T(8,128)}, u32[]{:S(2)}) copy-start(s32[8,16,1440]{2,1,0:T(8,128)} %refs_4_.3) | copy-start | bytes 2211844
  2.7 12.1 %collective-permute-start = (f32[5,8,1440]{2,1,0:T(8,128)}, f32[5,8,1440]{2,1,0:T(8,128)S(1)}, u32[]{:S(2)}, u32[]{:S(2)}) collective-permute-start(f32[5,8,1440]{2,1,0:T(8,128)} %get-tuple-element.17), channel_id=1, source_target_pairs={{0,8},{8,16},{16,24},{24,32},{32,40},{40,48},{48,56},{56,64},{64,7... | collective-permute-start | bytes 691208 | tf_op jit(solution)/shard_map/ppermute | solution.py:582
  7.7 7.2 %collective-permute-start.1 = (f32[4,8,1440]{2,1,0:T(8,128)}, f32[4,8,1440]{2,1,0:T(8,128)S(1)}, u32[]{:S(2)}, u32[]{:S(2)}) collective-permute-start(f32[4,8,1440]{2,1,0:T(8,128)} %get-tuple-element.18), channel_id=1, source_target_pairs={{8,0},{16,8},{24,16},{32,24},{40,32},{48,40},{56,48},{64,56},{72,6... | collective-permute-start | bytes 552968 | tf_op jit(solution)/shard_map/ppermute | solution.py:582
  9.6 1.1 %copy-start.5 = (f32[8,16,1440]{2,1,0:T(8,128)S(1)}, f32[8,16,1440]{2,1,0:T(8,128)}, u32[]{:S(2)}) copy-start(f32[8,16,1440]{2,1,0:T(8,128)} %refs_5_.1) | copy-start | bytes 2211844
  10.8 1.1 %copy-start.7 = (s32[8,16,1440]{2,1,0:T(8,128)S(1)}, s32[8,16,1440]{2,1,0:T(8,128)}, u32[]{:S(2)}) copy-start(s32[8,16,1440]{2,1,0:T(8,128)} %refs_6_.1) | copy-start | bytes 2211844
  14.9 5.9 %copy-start.6 = (f32[8,16,1440]{2,1,0:T(8,128)S(1)}, f32[8,16,1440]{2,1,0:T(8,128)}, u32[]{:S(2)}) copy-start(f32[8,16,1440]{2,1,0:T(8,128)} %refs_5_.1) | copy-start | bytes 2211844
  14.9 5.9 %copy-start.8 = (s32[8,16,1440]{2,1,0:T(8,128)S(1)}, s32[8,16,1440]{2,1,0:T(8,128)}, u32[]{:S(2)}) copy-start(s32[8,16,1440]{2,1,0:T(8,128)} %refs_6_.1) | copy-start | bytes 2211844
  15.3 8.4 %collective-permute-start.2 = (f32[2,8,1440]{2,1,0:T(8,128)S(1)}, f32[2,8,1440]{2,1,0:T(8,128)S(1)}, u32[]{:S(2)}, u32[]{:S(2)}) collective-permute-start(f32[2,8,1440]{2,1,0:T(8,128)S(1)} %get-tuple-element.23.refs_1_.refs_2_), channel_id=1, source_target_pairs={{0,8},{8,16},{16,24},{24,32},{32,40},{40,48},{48,56},{56,64},{64,7... | collective-permute-start | bytes 276488 | tf_op jit(solution)/shard_map/ppermute | solution.py:582
  18.8 5.9 %collective-permute-start.3 = (f32[2,8,1440]{2,1,0:T(8,128)S(1)}, f32[2,8,1440]{2,1,0:T(8,128)S(1)}, u32[]{:S(2)}, u32[]{:S(2)}) collective-permute-start(f32[2,8,1440]{2,1,0:T(8,128)S(1)} %get-tuple-element.24.refs_2_.refs_3_), channel_id=1, source_target_pairs={{8,0},{16,8},{24,16},{32,24},{40,32},{48,40},{56,48},{64,56},{72,6... | collective-permute-start | bytes 276488 | tf_op jit(solution)/shard_map/ppermute | solution.py:582
  26.4 6.8 %copy-start.21 = (s32[2000]{0:T(1024)S(1)}, s32[2000]{0:T(1024)}, u32[]{:S(2)}) copy-start(s32[2000]{0:T(1024)} %param.23) | copy-start | bytes 24004
  26.4 6.8 %copy-start.9 = (f32[16,4,16,16]{3,2,1,0:T(8,128)S(1)}, f32[16,4,16,16]{3,2,1,0:T(8,128)}, u32[]{:S(2)}) copy-start(f32[16,4,16,16]{3,2,1,0:T(8,128)} %inverse_ref.1) | copy-start | bytes 196612
  26.4 6.8 %copy-start.12 = (s32[16,1440]{1,0:T(8,128)S(1)}, s32[16,1440]{1,0:T(8,128)}, u32[]{:S(2)}) copy-start(s32[16,1440]{1,0:T(8,128)} %ids_ref.1) | copy-start | bytes 276484
  26.4 19.6 %all-to-all-start = ((f32[8,12,16,128]{3,2,1,0:T(8,128)}), f32[8,12,16,128]{3,2,1,0:T(8,128)S(1)}, u32[]{:S(2)}, u32[]{:S(2)}) async-start(f32[8,12,16,128]{3,2,1,0:T(8,128)} %edges.3), calls=%async_computation | async-start | bytes 1572864 | tf_op jit(solution)/shard_map/all_to_all | solution.py:619
  33.3 1.0 %copy-start.10 = (f32[16,3,16,16]{3,2,1,0:T(8,128)S(1)}, f32[16,3,16,16]{3,2,1,0:T(8,128)}, u32[]{:S(2)}) copy-start(f32[16,3,16,16]{3,2,1,0:T(8,128)} %lower_ref.1) | copy-start | bytes 147460
  34.3 1.0 %copy-start.11 = (f32[16,3,16,16]{3,2,1,0:T(8,128)S(1)}, f32[16,3,16,16]{3,2,1,0:T(8,128)}, u32[]{:S(2)}) copy-start(f32[16,3,16,16]{3,2,1,0:T(8,128)} %upper_ref.1) | copy-start | bytes 147460
  35.3 10.7 %copy-start = (f32[64,16,180]{2,1,0:T(8,128)S(1)}, f32[64,16,180]{2,1,0:T(8,128)}, u32[]{:S(2)}) copy-start(f32[64,16,180]{2,1,0:T(8,128)} %c_ref.1) | copy-start | bytes 2211844
  35.3 10.7 %copy-start.1 = (s32[64,16,180]{2,1,0:T(8,128)S(1)}, s32[64,16,180]{2,1,0:T(8,128)}, u32[]{:S(2)}) copy-start(s32[64,16,180]{2,1,0:T(8,128)} %k_ref.1) | copy-start | bytes 2211844
  46.0 1.0 %copy-start.16 = (bf16[16,64,192]{2,1,0:T(8,128)(2,1)S(1)}, bf16[16,64,192]{2,1,0:T(8,128)(2,1)}, u32[]{:S(2)}) copy-start(bf16[16,64,192]{2,1,0:T(8,128)(2,1)} %copy-done.15) | copy-start | bytes 1179652
  48.7 17.6 %copy-start.14 = (f32[1536,16]{1,0:T(8,128)S(1)}, f32[1536,16]{1,0:T(8,128)}, u32[]{:S(2)}) copy-start(f32[1536,16]{1,0:T(8,128)} %copy-done.13) | copy-start | bytes 294916
  48.7 17.6 %copy-start.18 = (f32[16,1536]{1,0:T(8,128)S(1)}, f32[16,1536]{1,0:T(8,128)}, u32[]{:S(2)}) copy-start(f32[16,1536]{1,0:T(8,128)} %copy-done.17) | copy-start | bytes 294916
  48.7 17.6 %copy-start.20 = (f32[128,16]{1,0:T(8,128)S(1)}, f32[128,16]{1,0:T(8,128)}, u32[]{:S(2)}) copy-start(f32[128,16]{1,0:T(8,128)} %copy-done.19) | copy-start | bytes 24580
  72.4 23.9 %all-to-all-start.2 = ((f32[256,1,128]{2,1,0:T(1,128)}), f32[256,1,128]{2,1,0:T(1,128)S(1)}, u32[]{:S(2)}, u32[]{:S(2)}) async-start(f32[256,1,128]{2,1,0:T(1,128)} %bitcast.6), calls=%async_computation.2 | async-start | bytes 262144 | tf_op jit(solution)/shard_map/all_to_all | solution.py:624
  (4 other events, 3.0 us)

commit v4 on v3

--- a/solution.py
+++ b/solution.py
@@ -11,7 +11,8 @@
 SLOTS = 16
 LANES = 128
 HALF = LANES // 2
-LANE_BITS = 7
+FINE_BITS = 8
+FINE = 2**FINE_BITS
 F32 = jnp.float32
 BF16 = jnp.bfloat16
 VMEM = pl.BlockSpec(memory_space=pltpu.VMEM)
@@ -339,8 +340,10 @@
             matrix_ref[first + g] = jnp.concatenate([high, low, high], axis=1)
 
     tiles = owner_ref.shape[0]
-    device = lax.broadcasted_iota(jnp.int32, (devices, LANES), 0)
-    earlier = jnp.where(row < col, 1.0, 0.0).astype(BF16)
+    device = lax.broadcasted_iota(jnp.int32, (devices, FINE), 0)
+    row_f = lax.broadcasted_iota(jnp.int32, (FINE, FINE), 0)
+    col_f = lax.broadcasted_iota(jnp.int32, (FINE, FINE), 1)
+    earlier = jnp.where(row_f < col_f, 1.0, 0.0).astype(BF16)
     running = jnp.zeros((devices, 1), F32)
     for t in range(tiles):
         owned = jnp.where(owner_ref[pl.ds(t, 1), :] == device, 1.0, 0.0)
@@ -354,8 +357,8 @@
     for part in range(parts):
         pieces += [ids[:, part * share + LANES : (part + 1) * share], gap]
     ids = jnp.concatenate(pieces, axis=1)
-    coarse_ref[...] = (ids >> LANE_BITS).astype(F32)
-    fine_ref[...] = (ids & (LANES - 1)).astype(F32).T
+    coarse_ref[...] = (ids >> FINE_BITS).astype(F32)
+    fine_ref[...] = (ids & (FINE - 1)).astype(F32).T
     device_ref[...] = owner_ref[...].astype(F32).T
 
 
@@ -496,7 +499,7 @@
     half = levels // 2
     tiles = slot_ref.shape[0]
     devices = send_ref.shape[0]
-    lane = lax.broadcasted_iota(jnp.int32, (width, LANES), 1).astype(F32)
+    lane = lax.broadcasted_iota(jnp.int32, (width, FINE), 1).astype(F32)
     lower = lax.broadcasted_iota(jnp.int32, (half, LANES), 1) < HALF
     for lat in range(rows):
         mains, rests = [], []
@@ -519,8 +522,8 @@
             acc_ref[...] = term
         else:
             acc_ref[...] += term
-    device = lax.broadcasted_iota(jnp.int32, (LANES, devices), 1).astype(F32)
-    place = lax.broadcasted_iota(jnp.int32, (SLOTS * levels, LANES), 0) // levels
+    device = lax.broadcasted_iota(jnp.int32, (FINE, devices), 1).astype(F32)
+    place = lax.broadcasted_iota(jnp.int32, (SLOTS * levels, FINE), 0) // levels
     total = jnp.zeros((SLOTS * levels, devices), F32)
     for t in range(tiles):
         owned = jnp.where(device_ref[:, t : t + 1] == device, 1.0, 0.0).astype(BF16)
@@ -539,7 +542,7 @@
         out_shape=jax.ShapeDtypeStruct((devices, SLOTS * levels), F32),
         in_specs=[VMEM] * 5,
         out_specs=VMEM,
-        scratch_shapes=[pltpu.VMEM((2 * levels * tiles, LANES), F32)],
+        scratch_shapes=[pltpu.VMEM((2 * levels * tiles, FINE), F32)],
         compiler_params=params(),
         cost_estimate=cost(6),
         name="regions",
@@ -601,9 +604,8 @@
     group_count = lax.axis_size("lev")
     devices = band_count * group_count
     region_count = owner.shape[0]
-    tiles = -(-region_count // LANES)
-    tiles = -(-tiles // 8) * 8
-    owner_tiles = jnp.pad(owner, (0, tiles * LANES - region_count), constant_values=-1).reshape(tiles, LANES)
+    tiles = -(-region_count // (8 * FINE)) * 8
+    owner_tiles = jnp.pad(owner, (0, tiles * FINE - region_count), constant_values=-1).reshape(tiles, FINE)
     matrix, slot_tiles, coarse, fine, device = prep(
         block_inverse, block_lower, block_upper, owner_tiles, region_ids, devices, group_count
     )

time: 97.9 us -> 96.8 us (0.989)
    pallas_call x1, Pallas kernels: 6.09 us -> 5.01 us  [regions(): pl.pallas_call(functools.partial(region_kernel, levels=levels, scale=scal...]
where the time goes in v4:
time: 96.8 us; the launch traced here: 96.3 us
  starting transfers between devices  29.9 us (31%)
  Pallas kernels  23.7 us (24%)
  blocking collectives  17.6 us (18%)
  waiting for transfers between devices  15.8 us (16%)
  local copies, waits for them, and re-layouts  8.35 us (9%)
    all_to_all x1, blocking collectives, local(): lax.all_to_all(columns.reshape(sent.shape), 'lev', split_axis=0, concat_a...  17.6 us
    all_to_all x1, waiting for transfers between devices, local(): lax.all_to_all(rows, ('lat', 'lev'), split_axis=0, concat_axis=0, tiled=T...  11.6 us
    all_to_all x1, starting transfers between devices, local(): lax.all_to_all(rows, ('lat', 'lev'), split_axis=0, concat_axis=0, tiled=T...  10.9 us
    ppermute x2, starting transfers between devices, neighbours(): lax.ppermute(up, 'lat', forward)  8.44 us
    unnamed x44, local copies, waits for them, and re-layouts  8.34 us
    all_to_all x1, starting transfers between devices, local(): lax.all_to_all(sent, 'lev', split_axis=0, concat_axis=0, tiled=True)  6.78 us
    pallas_call x2, Pallas kernels, interior(): pl.pallas_call(functools.partial(interior_kernel, final=final), out_shape...  5.7 us
    pallas_call x1, Pallas kernels, regions(): pl.pallas_call(functools.partial(region_kernel, levels=levels, scale=scal...  5.01 us
  transfers between devices with their start and end apart: 6, of which 4 were waited for; matrix products, arithmetic and copies ran while one was open for 0% of the time, Pallas kernels for 12%

profile of v4, /device:TPU:1, one launch (start us, length us, event | category | flops | bytes accessed | tf_op | source)
XLA Modules:
  0.0 96.3 jit_solution(13155807255615079164)
XLA Ops:
  0.7 2.0 %pack.1 = (f32[5,8,1440]{2,1,0:T(8,128)}, f32[4,8,1440]{2,1,0:T(8,128)}) custom-call(f32[8,16,1440]{2,1,0:T(8,128)} %refs_0_.1, f32[8,16,1440]{2,1,0:T(8,128)} %refs_3_.3, s32[8,16,1440]{2,1,0:T(8,128)} %refs_4_.3), custom_call_target="tpu_custom_call" | custom-call | flops 2000000000 | bytes 2000000 | tf_op jit(solution)/shard_map/pack/pallas_call | solution.py:297
  2.7 4.9 %collective-permute-start = (f32[5,8,1440]{2,1,0:T(8,128)}, f32[5,8,1440]{2,1,0:T(8,128)S(1)}, u32[]{:S(2)}, u32[]{:S(2)}) collective-permute-start(f32[5,8,1440]{2,1,0:T(8,128)} %get-tuple-element.17), channel_id=1, source_target_pairs={{0,8},{8,16},{16,24},{24,32},{32,40},{40,48},{48,56},{56,64},{64,7... | collective-permute-start | bytes 691208 | tf_op jit(solution)/shard_map/ppermute | solution.py:585
  7.7 1.9 %collective-permute-start.1 = (f32[4,8,1440]{2,1,0:T(8,128)}, f32[4,8,1440]{2,1,0:T(8,128)S(1)}, u32[]{:S(2)}, u32[]{:S(2)}) collective-permute-start(f32[4,8,1440]{2,1,0:T(8,128)} %get-tuple-element.18), channel_id=1, source_target_pairs={{8,0},{16,8},{24,16},{32,24},{40,32},{48,40},{56,48},{64,56},{72,6... | collective-permute-start | bytes 552968 | tf_op jit(solution)/shard_map/ppermute | solution.py:585
  9.6 1.1 %copy-done.5 = f32[8,16,1440]{2,1,0:T(8,128)S(1)} copy-done((f32[8,16,1440]{2,1,0:T(8,128)S(1)}, f32[8,16,1440]{2,1,0:T(8,128)}, u32[]{:S(2)}) %copy-start.5) | copy-done | bytes 737304
  10.8 1.1 %copy-done.7 = s32[8,16,1440]{2,1,0:T(8,128)S(1)} copy-done((s32[8,16,1440]{2,1,0:T(8,128)S(1)}, s32[8,16,1440]{2,1,0:T(8,128)}, u32[]{:S(2)}) %copy-start.7) | copy-done | bytes 737304
  11.9 2.8 %interior.2 = (f32[8,16,1440]{2,1,0:T(8,128)S(1)}, f32[4,8,1440]{2,1,0:T(8,128)S(1)}, f32[7,8,1440]{2,1,0:T(8,128)S(1)}, f32[4,6,8,1536]{3,2,1,0:T(8,128)S(1)}) custom-call(s32[1]{0:T(128)} %bitcast.last_ref, f32[8,16,1440]{2,1,0:T(8,128)S(1)} %copy-done.2, f32[8,16,1440]{2,1,0:T(8,128)S(1)} %copy-done.3, s32[8,16,1440]{2,1,0:T(8,128)S(1)} %copy-done.4, ...), custom_call_target="tpu_custom_call" | custom-call | flops 4000000000 | bytes 4000000 | tf_op jit(solution)/shard_map/interior/pallas_call | solution.py:170
  15.3 3.5 %collective-permute-start.2 = (f32[2,8,1440]{2,1,0:T(8,128)S(1)}, f32[2,8,1440]{2,1,0:T(8,128)S(1)}, u32[]{:S(2)}, u32[]{:S(2)}) collective-permute-start(f32[2,8,1440]{2,1,0:T(8,128)S(1)} %get-tuple-element.23.refs_1_.refs_2_), channel_id=1, source_target_pairs={{0,8},{8,16},{16,24},{24,32},{32,40},{40,48},{48,56},{56,64},{64,7... | collective-permute-start | bytes 276488 | tf_op jit(solution)/shard_map/ppermute | solution.py:585
  18.8 1.9 %collective-permute-start.3 = (f32[2,8,1440]{2,1,0:T(8,128)S(1)}, f32[2,8,1440]{2,1,0:T(8,128)S(1)}, u32[]{:S(2)}, u32[]{:S(2)}) collective-permute-start(f32[2,8,1440]{2,1,0:T(8,128)S(1)} %get-tuple-element.24.refs_2_.refs_3_), channel_id=1, source_target_pairs={{8,0},{16,8},{24,16},{32,24},{40,32},{48,40},{56,48},{64,56},{72,6... | collective-permute-start | bytes 276488 | tf_op jit(solution)/shard_map/ppermute | solution.py:585
  20.8 2.9 %interior.3 = (f32[8,12,16,128]{3,2,1,0:T(8,128)S(1)}, f32[4,8,1440]{2,1,0:T(8,128)S(1)}) custom-call(s32[1]{0:T(128)} %bitcast.last_ref, f32[8,16,1440]{2,1,0:T(8,128)S(1)} %get-tuple-element.21.refs_0_, f32[2,8,1440]{2,1,0:T(8,128)S(1)} %get-tuple-element.23.refs_1_.refs_2_, f32[2,8,1440]{2,1,0:T(8,128)S(1)} %get-tuple-element.24.refs_2_.refs_3_, ...), custom_call_target="tpu_custom_call" | custom-call | flops 4000000000 | bytes 4000000 | tf_op jit(solution)/shard_map/interior/pallas_call | solution.py:170
  23.7 1.1 %collective-permute-done.3.refs_1_ = f32[2,8,1440]{2,1,0:T(8,128)S(1)} collective-permute-done((f32[2,8,1440]{2,1,0:T(8,128)S(1)}, f32[2,8,1440]{2,1,0:T(8,128)S(1)}, u32[]{:S(2)}, u32[]{:S(2)}) %collective-permute-start.3) | collective-permute-done | bytes 92192 | tf_op jit(solution)/shard_map/ppermute | solution.py:585
  24.8 1.7 %edges.3 = f32[8,12,16,128]{3,2,1,0:T(8,128)} custom-call(f32[5,8,1440]{2,1,0:T(8,128)S(1)} %collective-permute-done.below_ref, f32[4,8,1440]{2,1,0:T(8,128)S(1)} %collective-permute-done.1.above_ref, f32[7,8,1440]{2,1,0:T(8,128)S(1)} %get-tuple-element.19.edge_ref, f32[4,6,8,1536]{3,2,1,0:T(8,128)S(1)} %get-tuple-element.20.lonc_ref, ...), custom_call_target="tpu_custom_call" | custom-call | flops 1000000000 | bytes 1000000 | tf_op jit(solution)/shard_map/edges/pallas_call | solution.py:260
  26.4 6.8 %all-to-all-start = ((f32[8,12,16,128]{3,2,1,0:T(8,128)}), f32[8,12,16,128]{3,2,1,0:T(8,128)S(1)}, u32[]{:S(2)}, u32[]{:S(2)}) async-start(f32[8,12,16,128]{3,2,1,0:T(8,128)} %edges.3), calls=%async_computation | async-start | bytes 1572864 | tf_op jit(solution)/shard_map/all_to_all | solution.py:621
  33.3 1.0 %copy-done.10 = f32[16,3,16,16]{3,2,1,0:T(8,128)S(1)} copy-done((f32[16,3,16,16]{3,2,1,0:T(8,128)S(1)}, f32[16,3,16,16]{3,2,1,0:T(8,128)}, u32[]{:S(2)}) %copy-start.10) | copy-done | bytes 49176
  34.3 1.0 %copy-done.11 = f32[16,3,16,16]{3,2,1,0:T(8,128)S(1)} copy-done((f32[16,3,16,16]{3,2,1,0:T(8,128)S(1)}, f32[16,3,16,16]{3,2,1,0:T(8,128)}, u32[]{:S(2)}) %copy-start.11) | copy-done | bytes 49176
  35.3 4.7 %prep.1 = (bf16[16,64,192]{2,1,0:T(8,128)(2,1)S(1)}, s32[8,256]{1,0:T(8,128)S(1)}, f32[16,1536]{1,0:T(8,128)S(1)}, f32[1536,16]{1,0:T(8,128)S(1)}, f32[256,8]{1,0:T(8,128)S(1)}) custom-call(f32[16,4,16,16]{3,2,1,0:T(8,128)S(1)} %copy-done.9, f32[16,3,16,16]{3,2,1,0:T(8,128)S(1)} %copy-done.10, f32[16,3,16,16]{3,2,1,0:T(8,128)S(1)} %copy-done.11, ...), custom_call_target="tpu_custom_call" | custom-call | flops 5000000000 | bytes 5000000 | tf_op jit(solution)/shard_map/prep/pallas_call | solution.py:369
  43.0 3.0 %all-to-all-done = f32[8,12,16,128]{3,2,1,0:T(8,128)S(1)} async-done(((f32[8,12,16,128]{3,2,1,0:T(8,128)}), f32[8,12,16,128]{3,2,1,0:T(8,128)S(1)}, u32[]{:S(2)}, u32[]{:S(2)}) %all-to-all-start) | async-done | bytes 786464 | tf_op jit(solution)/shard_map/all_to_all | solution.py:621
  46.0 1.0 %copy-done.16 = bf16[16,64,192]{2,1,0:T(8,128)(2,1)S(1)} copy-done((bf16[16,64,192]{2,1,0:T(8,128)(2,1)S(1)}, bf16[16,64,192]{2,1,0:T(8,128)(2,1)}, u32[]{:S(2)}) %copy-start.16) | copy-done | bytes 393240
  47.1 1.6 %vertical.1 = f32[1536,128]{1,0:T(8,128)S(1)} custom-call(f32[1536,128]{1,0:T(8,128)S(1)} %bitcast.8, bf16[16,64,192]{2,1,0:T(8,128)(2,1)S(1)} %copy-done.16, f32[64,16,180]{2,1,0:T(8,128)S(1)} %copy-done, s32[64,16,180]{2,1,0:T(8,128)S(1)} %copy-done.1), custom_call_target="tpu_custom_call" | custom-call | flops 5000000000 | bytes 5000000 | tf_op jit(solution)/shard_map/vertical/pallas_call | solution.py:457
  48.7 17.6 %all_to_all.21.field_ref = f32[8,12,16,128]{3,2,1,0:T(8,128)S(1)} all-to-all(f32[8,12,16,128]{3,2,1,0:T(8,128)S(1)} %bitcast.10), channel_id=1, replica_groups=mesh['lat'=32,'lev'=8] {'lev'}, dimensions={0} | all-to-all | bytes 1572864 | tf_op jit(solution)/shard_map/all_to_all | solution.py:623
  66.3 5.0 %regions.1 = f32[256,128]{1,0:T(8,128)} custom-call(f32[1536,128]{1,0:T(8,128)S(1)} %bitcast.9, f32[16,1536]{1,0:T(8,128)S(1)} %copy-done.20, f32[1536,16]{1,0:T(8,128)S(1)} %copy-done.14, f32[256,8]{1,0:T(8,128)S(1)} %copy-done.18, s32[8,256]{1,0:T(8,128)S(1)} %get-tuple-element.31.slot_ref), custom_call_target="tpu_custom_call" | custom-call | flops 6000000000 | bytes 6000000 | tf_op jit(solution)/shard_map/regions/pallas_call | solution.py:540
  71.3 10.9 %all-to-all-start.2 = ((f32[256,1,128]{2,1,0:T(1,128)}), f32[256,1,128]{2,1,0:T(1,128)S(1)}, u32[]{:S(2)}, u32[]{:S(2)}) async-start(f32[256,1,128]{2,1,0:T(1,128)} %bitcast.5), calls=%async_computation.2 | async-start | bytes 262144 | tf_op jit(solution)/shard_map/all_to_all | solution.py:626
  82.2 1.4 %rejoin.1 = f32[8,16,1440]{2,1,0:T(8,128)} custom-call(f32[8,12,16,128]{3,2,1,0:T(8,128)S(1)} %all_to_all.21.field_ref), custom_call_target="tpu_custom_call" | custom-call | flops 2000000000 | bytes 2000000 | tf_op jit(solution)/shard_map/rejoin/pallas_call | solution.py:485
  83.7 11.6 %all-to-all-done.2 = f32[256,1,128]{2,1,0:T(1,128)S(1)} async-done(((f32[256,1,128]{2,1,0:T(1,128)}), f32[256,1,128]{2,1,0:T(1,128)S(1)}, u32[]{:S(2)}, u32[]{:S(2)}) %all-to-all-start.2) | async-done | bytes 131104 | tf_op jit(solution)/shard_map/all_to_all | solution.py:626
  95.2 1.0 %owners.1 = f32[16,64]{1,0:T(8,128)} custom-call(f32[256,128]{1,0:T(8,128)S(1)} %bitcast.11), custom_call_target="tpu_custom_call" | custom-call | tf_op jit(solution)/shard_map/owners/pallas_call | solution.py:571
  (45 shorter events, 3.7 us)
Async XLA Ops:
  0.6 9.0 %copy-start.2 = (f32[8,16,1440]{2,1,0:T(8,128)S(1)}, f32[8,16,1440]{2,1,0:T(8,128)}, u32[]{:S(2)}) copy-start(f32[8,16,1440]{2,1,0:T(8,128)} %refs_0_.1) | copy-start | bytes 2211844
  0.6 9.0 %copy-start.3 = (f32[8,16,1440]{2,1,0:T(8,128)S(1)}, f32[8,16,1440]{2,1,0:T(8,128)}, u32[]{:S(2)}) copy-start(f32[8,16,1440]{2,1,0:T(8,128)} %refs_3_.3) | copy-start | bytes 2211844
  0.6 9.0 %copy-start.4 = (s32[8,16,1440]{2,1,0:T(8,128)S(1)}, s32[8,16,1440]{2,1,0:T(8,128)}, u32[]{:S(2)}) copy-start(s32[8,16,1440]{2,1,0:T(8,128)} %refs_4_.3) | copy-start | bytes 2211844
  2.7 12.1 %collective-permute-start = (f32[5,8,1440]{2,1,0:T(8,128)}, f32[5,8,1440]{2,1,0:T(8,128)S(1)}, u32[]{:S(2)}, u32[]{:S(2)}) collective-permute-start(f32[5,8,1440]{2,1,0:T(8,128)} %get-tuple-element.17), channel_id=1, source_target_pairs={{0,8},{8,16},{16,24},{24,32},{32,40},{40,48},{48,56},{56,64},{64,7... | collective-permute-start | bytes 691208 | tf_op jit(solution)/shard_map/ppermute | solution.py:585
  7.7 7.2 %collective-permute-start.1 = (f32[4,8,1440]{2,1,0:T(8,128)}, f32[4,8,1440]{2,1,0:T(8,128)S(1)}, u32[]{:S(2)}, u32[]{:S(2)}) collective-permute-start(f32[4,8,1440]{2,1,0:T(8,128)} %get-tuple-element.18), channel_id=1, source_target_pairs={{8,0},{16,8},{24,16},{32,24},{40,32},{48,40},{56,48},{64,56},{72,6... | collective-permute-start | bytes 552968 | tf_op jit(solution)/shard_map/ppermute | solution.py:585
  9.6 1.1 %copy-start.5 = (f32[8,16,1440]{2,1,0:T(8,128)S(1)}, f32[8,16,1440]{2,1,0:T(8,128)}, u32[]{:S(2)}) copy-start(f32[8,16,1440]{2,1,0:T(8,128)} %refs_5_.1) | copy-start | bytes 2211844
  10.8 1.1 %copy-start.7 = (s32[8,16,1440]{2,1,0:T(8,128)S(1)}, s32[8,16,1440]{2,1,0:T(8,128)}, u32[]{:S(2)}) copy-start(s32[8,16,1440]{2,1,0:T(8,128)} %refs_6_.1) | copy-start | bytes 2211844
  14.9 5.9 %copy-start.6 = (f32[8,16,1440]{2,1,0:T(8,128)S(1)}, f32[8,16,1440]{2,1,0:T(8,128)}, u32[]{:S(2)}) copy-start(f32[8,16,1440]{2,1,0:T(8,128)} %refs_5_.1) | copy-start | bytes 2211844
  14.9 5.9 %copy-start.8 = (s32[8,16,1440]{2,1,0:T(8,128)S(1)}, s32[8,16,1440]{2,1,0:T(8,128)}, u32[]{:S(2)}) copy-start(s32[8,16,1440]{2,1,0:T(8,128)} %refs_6_.1) | copy-start | bytes 2211844
  15.3 8.4 %collective-permute-start.2 = (f32[2,8,1440]{2,1,0:T(8,128)S(1)}, f32[2,8,1440]{2,1,0:T(8,128)S(1)}, u32[]{:S(2)}, u32[]{:S(2)}) collective-permute-start(f32[2,8,1440]{2,1,0:T(8,128)S(1)} %get-tuple-element.23.refs_1_.refs_2_), channel_id=1, source_target_pairs={{0,8},{8,16},{16,24},{24,32},{32,40},{40,48},{48,56},{56,64},{64,7... | collective-permute-start | bytes 276488 | tf_op jit(solution)/shard_map/ppermute | solution.py:585
  18.8 5.9 %collective-permute-start.3 = (f32[2,8,1440]{2,1,0:T(8,128)S(1)}, f32[2,8,1440]{2,1,0:T(8,128)S(1)}, u32[]{:S(2)}, u32[]{:S(2)}) collective-permute-start(f32[2,8,1440]{2,1,0:T(8,128)S(1)} %get-tuple-element.24.refs_2_.refs_3_), channel_id=1, source_target_pairs={{8,0},{16,8},{24,16},{32,24},{40,32},{48,40},{56,48},{64,56},{72,6... | collective-permute-start | bytes 276488 | tf_op jit(solution)/shard_map/ppermute | solution.py:585
  26.4 6.8 %copy-start.21 = (s32[2000]{0:T(1024)S(1)}, s32[2000]{0:T(1024)}, u32[]{:S(2)}) copy-start(s32[2000]{0:T(1024)} %param.23) | copy-start | bytes 24004
  26.4 6.8 %copy-start.9 = (f32[16,4,16,16]{3,2,1,0:T(8,128)S(1)}, f32[16,4,16,16]{3,2,1,0:T(8,128)}, u32[]{:S(2)}) copy-start(f32[16,4,16,16]{3,2,1,0:T(8,128)} %inverse_ref.1) | copy-start | bytes 196612
  26.4 6.8 %copy-start.12 = (s32[16,1440]{1,0:T(8,128)S(1)}, s32[16,1440]{1,0:T(8,128)}, u32[]{:S(2)}) copy-start(s32[16,1440]{1,0:T(8,128)} %ids_ref.1) | copy-start | bytes 276484
  26.4 19.6 %all-to-all-start = ((f32[8,12,16,128]{3,2,1,0:T(8,128)}), f32[8,12,16,128]{3,2,1,0:T(8,128)S(1)}, u32[]{:S(2)}, u32[]{:S(2)}) async-start(f32[8,12,16,128]{3,2,1,0:T(8,128)} %edges.3), calls=%async_computation | async-start | bytes 1572864 | tf_op jit(solution)/shard_map/all_to_all | solution.py:621
  33.3 1.0 %copy-start.10 = (f32[16,3,16,16]{3,2,1,0:T(8,128)S(1)}, f32[16,3,16,16]{3,2,1,0:T(8,128)}, u32[]{:S(2)}) copy-start(f32[16,3,16,16]{3,2,1,0:T(8,128)} %lower_ref.1) | copy-start | bytes 147460
  34.3 1.0 %copy-start.11 = (f32[16,3,16,16]{3,2,1,0:T(8,128)S(1)}, f32[16,3,16,16]{3,2,1,0:T(8,128)}, u32[]{:S(2)}) copy-start(f32[16,3,16,16]{3,2,1,0:T(8,128)} %upper_ref.1) | copy-start | bytes 147460
  35.3 10.7 %copy-start = (f32[64,16,180]{2,1,0:T(8,128)S(1)}, f32[64,16,180]{2,1,0:T(8,128)}, u32[]{:S(2)}) copy-start(f32[64,16,180]{2,1,0:T(8,128)} %c_ref.1) | copy-start | bytes 2211844
  35.3 10.7 %copy-start.1 = (s32[64,16,180]{2,1,0:T(8,128)S(1)}, s32[64,16,180]{2,1,0:T(8,128)}, u32[]{:S(2)}) copy-start(s32[64,16,180]{2,1,0:T(8,128)} %k_ref.1) | copy-start | bytes 2211844
  46.0 1.0 %copy-start.16 = (bf16[16,64,192]{2,1,0:T(8,128)(2,1)S(1)}, bf16[16,64,192]{2,1,0:T(8,128)(2,1)}, u32[]{:S(2)}) copy-start(bf16[16,64,192]{2,1,0:T(8,128)(2,1)} %copy-done.15) | copy-start | bytes 1179652
  48.7 17.6 %copy-start.14 = (f32[1536,16]{1,0:T(8,128)S(1)}, f32[1536,16]{1,0:T(8,128)}, u32[]{:S(2)}) copy-start(f32[1536,16]{1,0:T(8,128)} %copy-done.13) | copy-start | bytes 294916
  48.7 17.6 %copy-start.18 = (f32[256,8]{1,0:T(8,128)S(1)}, f32[256,8]{1,0:T(8,128)}, u32[]{:S(2)}) copy-start(f32[256,8]{1,0:T(8,128)} %copy-done.17) | copy-start | bytes 24580
  48.7 17.6 %copy-start.20 = (f32[16,1536]{1,0:T(8,128)S(1)}, f32[16,1536]{1,0:T(8,128)}, u32[]{:S(2)}) copy-start(f32[16,1536]{1,0:T(8,128)} %copy-done.19) | copy-start | bytes 294916
  71.3 23.9 %all-to-all-start.2 = ((f32[256,1,128]{2,1,0:T(1,128)}), f32[256,1,128]{2,1,0:T(1,128)S(1)}, u32[]{:S(2)}, u32[]{:S(2)}) async-start(f32[256,1,128]{2,1,0:T(1,128)} %bitcast.5), calls=%async_computation.2 | async-start | bytes 262144 | tf_op jit(solution)/shard_map/all_to_all | solution.py:626
  (4 other events, 3.0 us)

commit v5 on v4

--- a/solution.py
+++ b/solution.py
@@ -75,56 +75,142 @@
     return (0, 1, rows - 2, rows - 1)
 
 
-def interior_kernel(last_ref, *refs, final):
-    if final:
-        a_ref, up_ref, down_ref, clat_ref, klat_ref, clon_ref, klon_ref, send_ref, swept_ref, rows_ref = refs
-    else:
-        a_ref, clat_ref, klat_ref, clon_ref, klon_ref, out_ref, swept_ref, edge_ref, lonc_ref, rows_ref = refs
+def sweep_lat(a, courant, codes):
+    rows, size = a.shape
+    row = lax.broadcasted_iota(jnp.int32, (rows, size), 0)
+    lowest, highest = row == 0, row == rows - 1
+    up, down, uph, downh = flux_parts(courant)
+    ahead, behind = slope_parts(codes)
+    f = jnp.where(highest, 0.0, roll(a, -1, 0)) - a
+    s = uph * f - jnp.where(lowest, 0.0, roll(downh * f, 1, 0))
+    q = jnp.where(lowest, 0.0, roll(down * f + ahead * s, 1, 0))
+    r = jnp.where(highest, 0.0, roll(behind * s, -1, 0))
+    return a + up * f + (behind - ahead) * s + q - r
+
+
+def lane_chunks(lons):
+    step = 4 * LANES
+    return [slice(start, min(start + step, lons)) for start in range(0, lons, step)]
+
+
+def walled(last, courant):
+    rows = courant.shape[0]
+    row = lax.broadcasted_iota(jnp.int32, courant.shape, 0)
+    return jnp.where((row == rows - 1) & (last == 1), 0.0, courant)
+
+
+def first_lat_kernel(last_ref, a_ref, clat_ref, klat_ref, rows_ref, swept_ref, edge_ref):
+    levels, rows, lons = a_ref.shape
+    last = last_ref[0]
+
+    def level(l, carry):
+        for cols in lane_chunks(lons):
+            rows_ref[l, :, cols] = sweep_lat(
+                a_ref[l, :, cols], walled(last, clat_ref[l, :, cols]), klat_ref[l, :, cols]
+            )
+        return carry
+
+    lax.fori_loop(0, levels, level, 0)
+    for n, row in enumerate(edge_rows(rows)):
+        swept_ref[n] = rows_ref[:, row, :]
+    high = rows - 1
+    courant = jnp.where(last == 1, 0.0, clat_ref[:, high, :])
+    up, _, uph, downh = flux_parts(courant)
+    ahead, behind = slope_parts(klat_ref[:, high, :])
+    ahead0, behind0 = slope_parts(klat_ref[:, 0, :])
+    edge_ref[0] = a_ref[:, 0, :]
+    edge_ref[1] = a_ref[:, high, :]
+    edge_ref[2] = behind0 - ahead0
+    edge_ref[3] = ahead0
+    edge_ref[4] = up + (behind - ahead) * uph
+    edge_ref[5] = behind * uph
+    edge_ref[6] = downh
+
+
+def first_lat(last, a, clat, klat):
+    levels, rows, lons = a.shape
+    return pl.pallas_call(
+        first_lat_kernel,
+        out_shape=(
+            jax.ShapeDtypeStruct(a.shape, F32),
+            jax.ShapeDtypeStruct((4, levels, lons), F32),
+            jax.ShapeDtypeStruct((7, levels, lons), F32),
+        ),
+        in_specs=[SMEM] + [VMEM] * 3,
+        out_specs=(VMEM,) * 3,
+        compiler_params=params(),
+        cost_estimate=cost(2),
+        name="first_lat",
+    )(last, a, clat, klat)
+
+
+def first_lon_kernel(rows_ref, clon_ref, klon_ref, out_ref, lonc_ref):
+    levels, rows, lons = rows_ref.shape
+    width = lonc_ref.shape[3]
+    tile = 8
+
+    def level(l, carry):
+        for low in range(0, rows, tile):
+            band = slice(low, low + tile)
+            value = sweep_lon(
+                wrapped(rows_ref[l, band, :], width), *lon_parts(clon_ref[l, band, :], klon_ref[l, band, :], width)
+            )
+            out_ref[l, band, :] = value[:, :lons]
+        return carry
+
+    lax.fori_loop(0, levels, level, 0)
+    for n, row in enumerate(edge_rows(rows)):
+        for m, part in enumerate(lon_parts(clon_ref[:, row, :], klon_ref[:, row, :], width)):
+            lonc_ref[n, m] = part
+
+
+def first_lon(swept, clon, klon):
+    levels, _, lons = swept.shape
+    width = -(-lons // LANES) * LANES
+    return pl.pallas_call(
+        first_lon_kernel,
+        out_shape=(jax.ShapeDtypeStruct(swept.shape, F32), jax.ShapeDtypeStruct((4, 6, levels, width), F32)),
+        in_specs=[VMEM] * 3,
+        out_specs=(VMEM,) * 2,
+        compiler_params=params(),
+        cost_estimate=cost(2),
+        name="first_lon",
+    )(swept, clon, klon)
+
+
+def interior_kernel(
+    last_ref, a_ref, up_ref, down_ref, clat_ref, klat_ref, clon_ref, klon_ref, send_ref, swept_ref, rows_ref
+):
     levels, rows, lons = a_ref.shape
     width = rows_ref.shape[2]
     half = levels // 2
     last = last_ref[0]
-    step = 4 * LANES
-    chunks = [(start, min(step, lons - start)) for start in range(0, lons, step)]
     tile = 8
 
     def level(l, upper):
-        for start, size in chunks:
-            cols = slice(start, start + size)
-            row = lax.broadcasted_iota(jnp.int32, (rows, size), 0)
-            lowest, highest = row == 0, row == rows - 1
+        for cols in lane_chunks(lons):
             a = a_ref[l, :, cols]
-            if final:
-                a = jnp.where(lowest, down_ref[0, pl.ds(l, 1), cols], a)
-                a = jnp.where(row == 1, down_ref[1, pl.ds(l, 1), cols], a)
-                a = jnp.where(row == rows - 2, up_ref[1, pl.ds(l, 1), cols], a)
-                a = jnp.where(highest, up_ref[0, pl.ds(l, 1), cols], a)
-            courant = jnp.where(highest & (last == 1), 0.0, clat_ref[l, :, cols])
-            up, down, uph, downh = flux_parts(courant)
-            ahead, behind = slope_parts(klat_ref[l, :, cols])
-            f = jnp.where(highest, 0.0, roll(a, -1, 0)) - a
-            s = uph * f - jnp.where(lowest, 0.0, roll(downh * f, 1, 0))
-            q = jnp.where(lowest, 0.0, roll(down * f + ahead * s, 1, 0))
-            r = jnp.where(highest, 0.0, roll(behind * s, -1, 0))
-            rows_ref[l, :, cols] = a + up * f + (behind - ahead) * s + q - r
+            row = lax.broadcasted_iota(jnp.int32, a.shape, 0)
+            a = jnp.where(row == 0, down_ref[0, pl.ds(l, 1), cols], a)
+            a = jnp.where(row == 1, down_ref[1, pl.ds(l, 1), cols], a)
+            a = jnp.where(row == rows - 2, up_ref[1, pl.ds(l, 1), cols], a)
+            a = jnp.where(row == rows - 1, up_ref[0, pl.ds(l, 1), cols], a)
+            rows_ref[l, :, cols] = sweep_lat(a, walled(last, clat_ref[l, :, cols]), klat_ref[l, :, cols])
+        parts = send_ref.shape[0]
+        share = lons // parts
         for low in range(0, rows, tile):
             band = slice(low, low + tile)
             value = sweep_lon(
                 wrapped(rows_ref[l, band, :lons], width), *lon_parts(clon_ref[l, band, :], klon_ref[l, band, :], width)
             )
-            if final:
-                parts = send_ref.shape[0]
-                share = lons // parts
-                for part in range(parts):
-                    start = part * share
-                    send_ref[part, l, band, :] = value[:, start : start + LANES]
-                    rest = value[:, start + LANES : start + share]
-                    if upper:
-                        send_ref[part, half + l, band, HALF : HALF + share - LANES] = rest
-                    else:
-                        send_ref[part, levels + l, band, : share - LANES] = rest
-            else:
-                out_ref[l, band, :] = value[:, :lons]
+            for part in range(parts):
+                start = part * share
+                send_ref[part, l, band, :] = value[:, start : start + LANES]
+                rest = value[:, start + LANES : start + share]
+                if upper:
+                    send_ref[part, half + l, band, HALF : HALF + share - LANES] = rest
+                else:
+                    send_ref[part, levels + l, band, : share - LANES] = rest
 
     def pair(index, carry):
         level(index, False)
@@ -134,44 +220,19 @@
     lax.fori_loop(0, half, pair, 0)
     for n, row in enumerate(edge_rows(rows)):
         swept_ref[n] = rows_ref[:, row, :lons]
-    if not final:
-        high = rows - 1
-        courant = jnp.where(last == 1, 0.0, clat_ref[:, high, :])
-        up, _, uph, downh = flux_parts(courant)
-        ahead, behind = slope_parts(klat_ref[:, high, :])
-        ahead0, behind0 = slope_parts(klat_ref[:, 0, :])
-        edge_ref[0] = a_ref[:, 0, :]
-        edge_ref[1] = a_ref[:, high, :]
-        edge_ref[2] = behind0 - ahead0
-        edge_ref[3] = ahead0
-        edge_ref[4] = up + (behind - ahead) * uph
-        edge_ref[5] = behind * uph
-        edge_ref[6] = downh
-        for n, row in enumerate(edge_rows(rows)):
-            for m, part in enumerate(lon_parts(clon_ref[:, row, :], klon_ref[:, row, :], width)):
-                lonc_ref[n, m] = part
 
 
 def interior(last, fields, coefficients, parts):
     levels, rows, lons = fields[0].shape
     width = -(-lons // LANES) * LANES
-    final = parts > 0
-    whole = (levels, rows, lons)
-    swept = jax.ShapeDtypeStruct((4, levels, lons), F32)
-    if final:
-        out_shape = (jax.ShapeDtypeStruct((parts, levels + levels // 2, rows, LANES), F32), swept)
-    else:
-        out_shape = (
-            jax.ShapeDtypeStruct(whole, F32),
-            swept,
-            jax.ShapeDtypeStruct((7, levels, lons), F32),
-            jax.ShapeDtypeStruct((4, 6, levels, width), F32),
-        )
-    return pl.pallas_call(
-        functools.partial(interior_kernel, final=final),
-        out_shape=out_shape,
+    return pl.pallas_call(
+        interior_kernel,
+        out_shape=(
+            jax.ShapeDtypeStruct((parts, levels + levels // 2, rows, LANES), F32),
+            jax.ShapeDtypeStruct((4, levels, lons), F32),
+        ),
         in_specs=[SMEM] + [VMEM] * (len(fields) + len(coefficients)),
-        out_specs=(VMEM,) * len(out_shape),
+        out_specs=(VMEM,) * 2,
         scratch_shapes=[pltpu.VMEM((levels, rows, width), F32)],
         compiler_params=params(),
         cost_estimate=cost(4),
@@ -613,7 +674,8 @@
     up, down = pack(adjoint_in, courant_lat, codes_lat)
     below, above = neighbours(up, down)
     coefficients = (courant_lat, codes_lat, courant_lon, codes_lon)
-    adjoint, swept, edge, lonc = interior(last, (adjoint_in,), coefficients, 0)
+    partial, swept, edge = first_lat(last, adjoint_in, courant_lat, codes_lat)
+    adjoint, lonc = first_lon(partial, courant_lon, codes_lon)
     up, down = edges(below, above, edge, lonc, swept)
     below_next, above_next = neighbours(up, down)
     sent, swept = interior(last, (adjoint, up, down), coefficients, group_count)

time: 96.8 us -> 97.2 us (level)
  local copies, waits for them, and re-layouts: 8.35 us -> 6.18 us
  waiting for transfers between devices: 15.8 us -> 17.9 us
  blocking collectives: 17.6 us -> 16.1 us
  Pallas kernels: 23.7 us -> 24.7 us
  starting transfers between devices: 29.9 us -> 30.9 us
    unnamed x44 -> x40, local copies, waits for them, and re-layouts: 8.34 us -> 6.17 us
    all_to_all x1, starting transfers between devices: 10.9 us -> 13 us  [local(): lax.all_to_all(rows, ('lat', 'lev'), split_axis=0, concat_axis=0, tiled=T...]
    all_to_all x1, blocking collectives: 17.6 us -> 16.1 us  [local(): lax.all_to_all(columns.reshape(sent.shape), 'lev', split_axis=0, concat_a...]
    ppermute x2, starting transfers between devices: 8.44 us -> 7.31 us  [neighbours(): lax.ppermute(up, 'lat', forward)]
    ppermute x2, waiting for transfers between devices: 1.23 us -> 2.35 us  [neighbours(): lax.ppermute(down, 'lat', backward)]
    pallas_call x2 -> x3, Pallas kernels: 5.7 us -> 6.7 us  [the longest x1 2.89 us: interior(): pl.pallas_call(interior_kernel, out_shape=(jax.ShapeDtypeStruct((parts, l...]
  transfers between devices with their start and end apart: 6 -> 6, of which waited for: 4 -> 4; matrix products, arithmetic and copies ran while one was open for 0% -> 0% of each run, Pallas kernels for 12% -> 13%
where the time goes in v5:
time: 97.2 us; the launch traced here: 96.7 us
  starting transfers between devices  30.9 us (32%)
  Pallas kernels  24.7 us (25%)
  waiting for transfers between devices  17.9 us (18%)
  blocking collectives  16.1 us (17%)
  local copies, waits for them, and re-layouts  6.18 us (6%)
    all_to_all x1, blocking collectives, local(): lax.all_to_all(columns.reshape(sent.shape), 'lev', split_axis=0, concat_a...  16.1 us
    all_to_all x1, starting transfers between devices, local(): lax.all_to_all(rows, ('lat', 'lev'), split_axis=0, concat_axis=0, tiled=T...  13 us
    all_to_all x1, waiting for transfers between devices, local(): lax.all_to_all(rows, ('lat', 'lev'), split_axis=0, concat_axis=0, tiled=T...  11.6 us
    ppermute x2, starting transfers between devices, neighbours(): lax.ppermute(up, 'lat', forward)  7.31 us
    all_to_all x1, starting transfers between devices, local(): lax.all_to_all(sent, 'lev', split_axis=0, concat_axis=0, tiled=True)  6.78 us
    unnamed x40, local copies, waits for them, and re-layouts  6.17 us
    pallas_call x1, Pallas kernels, regions(): pl.pallas_call(functools.partial(region_kernel, levels=levels, scale=scal...  5.02 us
    pallas_call x1, Pallas kernels, prep(): pl.pallas_call(functools.partial(prep_kernel, devices=devices, parts=part...  4.69 us
  transfers between devices with their start and end apart: 6, of which 4 were waited for; matrix products, arithmetic and copies ran while one was open for 0% of the time, Pallas kernels for 13%

profile of v5, /device:TPU:1, one launch (start us, length us, event | category | flops | bytes accessed | tf_op | source)
XLA Modules:
  0.0 96.7 jit_solution(12571140153755014651)
XLA Ops:
  0.7 2.0 %pack.1 = (f32[5,8,1440]{2,1,0:T(8,128)}, f32[4,8,1440]{2,1,0:T(8,128)}) custom-call(f32[8,16,1440]{2,1,0:T(8,128)} %a_ref.1, f32[8,16,1440]{2,1,0:T(8,128)} %clat_ref.3, s32[8,16,1440]{2,1,0:T(8,128)} %klat_ref.3), custom_call_target="tpu_custom_call" | custom-call | flops 2000000000 | bytes 2000000 | tf_op jit(solution)/shard_map/pack/pallas_call | solution.py:358
  2.7 4.9 %collective-permute-start = (f32[5,8,1440]{2,1,0:T(8,128)}, f32[5,8,1440]{2,1,0:T(8,128)S(1)}, u32[]{:S(2)}, u32[]{:S(2)}) collective-permute-start(f32[5,8,1440]{2,1,0:T(8,128)} %get-tuple-element.18), channel_id=1, source_target_pairs={{0,8},{8,16},{16,24},{24,32},{32,40},{40,48},{48,56},{56,64},{64,7... | collective-permute-start | bytes 691208 | tf_op jit(solution)/shard_map/ppermute | solution.py:646
  7.6 1.9 %collective-permute-start.1 = (f32[4,8,1440]{2,1,0:T(8,128)}, f32[4,8,1440]{2,1,0:T(8,128)S(1)}, u32[]{:S(2)}, u32[]{:S(2)}) collective-permute-start(f32[4,8,1440]{2,1,0:T(8,128)} %get-tuple-element.19), channel_id=1, source_target_pairs={{8,0},{16,8},{24,16},{32,24},{40,32},{48,40},{56,48},{64,56},{72,6... | collective-permute-start | bytes 552968 | tf_op jit(solution)/shard_map/ppermute | solution.py:646
  9.6 1.2 %first_lat.1 = (f32[8,16,1440]{2,1,0:T(8,128)S(1)}, f32[4,8,1440]{2,1,0:T(8,128)S(1)}, f32[7,8,1440]{2,1,0:T(8,128)S(1)}) custom-call(s32[1]{0:T(128)} %bitcast.last_ref, f32[8,16,1440]{2,1,0:T(8,128)S(1)} %copy-done.2, f32[8,16,1440]{2,1,0:T(8,128)S(1)} %copy-done.3, s32[8,16,1440]{2,1,0:T(8,128)S(1)} %copy-done.4), custom_call_target="tpu_custom_call" | custom-call | flops 2000000000 | bytes 2000000 | tf_op jit(solution)/shard_map/first_lat/pallas_call | solution.py:132
  11.0 2.6 %first_lon.1 = (f32[8,16,1440]{2,1,0:T(8,128)S(1)}, f32[4,6,8,1536]{3,2,1,0:T(8,128)S(1)}) custom-call(f32[8,16,1440]{2,1,0:T(8,128)S(1)} %get-tuple-element.21.rows_ref, f32[8,16,1440]{2,1,0:T(8,128)S(1)} %copy-done.5, s32[8,16,1440]{2,1,0:T(8,128)S(1)} %copy-done.6), custom_call_target="tpu_custom_call" | custom-call | flops 2000000000 | bytes 2000000 | tf_op jit(solution)/shard_map/first_lon/pallas_call | solution.py:170
  13.6 1.3 %collective-permute-done.1.above_ref = f32[4,8,1440]{2,1,0:T(8,128)S(1)} collective-permute-done((f32[4,8,1440]{2,1,0:T(8,128)}, f32[4,8,1440]{2,1,0:T(8,128)S(1)}, u32[]{:S(2)}, u32[]{:S(2)}) %collective-permute-start.1) | collective-permute-done | bytes 184352 | tf_op jit(solution)/shard_map/ppermute | solution.py:646
  15.3 2.4 %collective-permute-start.2 = (f32[2,8,1440]{2,1,0:T(8,128)S(1)}, f32[2,8,1440]{2,1,0:T(8,128)S(1)}, u32[]{:S(2)}, u32[]{:S(2)}) collective-permute-start(f32[2,8,1440]{2,1,0:T(8,128)S(1)} %get-tuple-element.25.up_ref.refs_2_), channel_id=1, source_target_pairs={{0,8},{8,16},{16,24},{24,32},{32,40},{40,48},{48,56},{56,64},{64,7... | collective-permute-start | bytes 276488 | tf_op jit(solution)/shard_map/ppermute | solution.py:646
  17.7 2.0 %collective-permute-start.3 = (f32[2,8,1440]{2,1,0:T(8,128)S(1)}, f32[2,8,1440]{2,1,0:T(8,128)S(1)}, u32[]{:S(2)}, u32[]{:S(2)}) collective-permute-start(f32[2,8,1440]{2,1,0:T(8,128)S(1)} %get-tuple-element.26.down_ref.refs_3_), channel_id=1, source_target_pairs={{8,0},{16,8},{24,16},{32,24},{40,32},{48,40},{56,48},{64,56},{72,6... | collective-permute-start | bytes 276488 | tf_op jit(solution)/shard_map/ppermute | solution.py:646
  19.6 2.9 %interior.1 = (f32[8,12,16,128]{3,2,1,0:T(8,128)S(1)}, f32[4,8,1440]{2,1,0:T(8,128)S(1)}) custom-call(s32[1]{0:T(128)} %bitcast.last_ref, f32[8,16,1440]{2,1,0:T(8,128)S(1)} %get-tuple-element.23.a_ref, f32[2,8,1440]{2,1,0:T(8,128)S(1)} %get-tuple-element.25.up_ref.refs_2_, f32[2,8,1440]{2,1,0:T(8,128)S(1)} %get-tuple-element.26.down_ref.refs_3_, ...), custom_call_target="tpu_custom_call" | custom-call | flops 4000000000 | bytes 4000000 | tf_op jit(solution)/shard_map/interior/pallas_call | solution.py:228
  22.6 1.1 %collective-permute-done.3.refs_1_ = f32[2,8,1440]{2,1,0:T(8,128)S(1)} collective-permute-done((f32[2,8,1440]{2,1,0:T(8,128)S(1)}, f32[2,8,1440]{2,1,0:T(8,128)S(1)}, u32[]{:S(2)}, u32[]{:S(2)}) %collective-permute-start.3) | collective-permute-done | bytes 92192 | tf_op jit(solution)/shard_map/ppermute | solution.py:646
  23.6 1.7 %edges.3 = f32[8,12,16,128]{3,2,1,0:T(8,128)} custom-call(f32[5,8,1440]{2,1,0:T(8,128)S(1)} %collective-permute-done.below_ref, f32[4,8,1440]{2,1,0:T(8,128)S(1)} %collective-permute-done.1.above_ref, f32[7,8,1440]{2,1,0:T(8,128)S(1)} %get-tuple-element.20.edge_ref, f32[4,6,8,1536]{3,2,1,0:T(8,128)S(1)} %get-tuple-element.22.lonc_ref, ...), custom_call_target="tpu_custom_call" | custom-call | flops 1000000000 | bytes 1000000 | tf_op jit(solution)/shard_map/edges/pallas_call | solution.py:321
  25.3 6.8 %all-to-all-start = ((f32[8,12,16,128]{3,2,1,0:T(8,128)}), f32[8,12,16,128]{3,2,1,0:T(8,128)S(1)}, u32[]{:S(2)}, u32[]{:S(2)}) async-start(f32[8,12,16,128]{3,2,1,0:T(8,128)} %edges.3), calls=%async_computation | async-start | bytes 1572864 | tf_op jit(solution)/shard_map/all_to_all | solution.py:683
  32.1 1.0 %copy-done.8 = f32[16,3,16,16]{3,2,1,0:T(8,128)S(1)} copy-done((f32[16,3,16,16]{3,2,1,0:T(8,128)S(1)}, f32[16,3,16,16]{3,2,1,0:T(8,128)}, u32[]{:S(2)}) %copy-start.8) | copy-done | bytes 49176
  33.1 1.0 %copy-done.9 = f32[16,3,16,16]{3,2,1,0:T(8,128)S(1)} copy-done((f32[16,3,16,16]{3,2,1,0:T(8,128)S(1)}, f32[16,3,16,16]{3,2,1,0:T(8,128)}, u32[]{:S(2)}) %copy-start.9) | copy-done | bytes 49176
  34.1 4.7 %prep.1 = (bf16[16,64,192]{2,1,0:T(8,128)(2,1)S(1)}, s32[8,256]{1,0:T(8,128)S(1)}, f32[16,1536]{1,0:T(8,128)S(1)}, f32[1536,16]{1,0:T(8,128)S(1)}, f32[256,8]{1,0:T(8,128)S(1)}) custom-call(f32[16,4,16,16]{3,2,1,0:T(8,128)S(1)} %copy-done.7, f32[16,3,16,16]{3,2,1,0:T(8,128)S(1)} %copy-done.8, f32[16,3,16,16]{3,2,1,0:T(8,128)S(1)} %copy-done.9, ...), custom_call_target="tpu_custom_call" | custom-call | flops 5000000000 | bytes 5000000 | tf_op jit(solution)/shard_map/prep/pallas_call | solution.py:430
  41.8 4.0 %all-to-all-done = f32[8,12,16,128]{3,2,1,0:T(8,128)S(1)} async-done(((f32[8,12,16,128]{3,2,1,0:T(8,128)}), f32[8,12,16,128]{3,2,1,0:T(8,128)S(1)}, u32[]{:S(2)}, u32[]{:S(2)}) %all-to-all-start) | async-done | bytes 786464 | tf_op jit(solution)/shard_map/all_to_all | solution.py:683
  45.8 1.0 %copy-done.14 = bf16[16,64,192]{2,1,0:T(8,128)(2,1)S(1)} copy-done((bf16[16,64,192]{2,1,0:T(8,128)(2,1)S(1)}, bf16[16,64,192]{2,1,0:T(8,128)(2,1)}, u32[]{:S(2)}) %copy-start.14) | copy-done | bytes 393240
  46.9 1.6 %vertical.1 = f32[1536,128]{1,0:T(8,128)S(1)} custom-call(f32[1536,128]{1,0:T(8,128)S(1)} %bitcast.8, bf16[16,64,192]{2,1,0:T(8,128)(2,1)S(1)} %copy-done.14, f32[64,16,180]{2,1,0:T(8,128)S(1)} %copy-done, s32[64,16,180]{2,1,0:T(8,128)S(1)} %copy-done.1), custom_call_target="tpu_custom_call" | custom-call | flops 5000000000 | bytes 5000000 | tf_op jit(solution)/shard_map/vertical/pallas_call | solution.py:518
  48.6 16.1 %all_to_all.21.field_ref = f32[8,12,16,128]{3,2,1,0:T(8,128)S(1)} all-to-all(f32[8,12,16,128]{3,2,1,0:T(8,128)S(1)} %bitcast.10), channel_id=1, replica_groups=mesh['lat'=32,'lev'=8] {'lev'}, dimensions={0} | all-to-all | bytes 1572864 | tf_op jit(solution)/shard_map/all_to_all | solution.py:685
  64.7 5.0 %regions.1 = f32[256,128]{1,0:T(8,128)} custom-call(f32[1536,128]{1,0:T(8,128)S(1)} %bitcast.9, f32[16,1536]{1,0:T(8,128)S(1)} %copy-done.18, f32[1536,16]{1,0:T(8,128)S(1)} %copy-done.12, f32[256,8]{1,0:T(8,128)S(1)} %copy-done.16, s32[8,256]{1,0:T(8,128)S(1)} %get-tuple-element.33.slot_ref), custom_call_target="tpu_custom_call" | custom-call | flops 6000000000 | bytes 6000000 | tf_op jit(solution)/shard_map/regions/pallas_call | solution.py:601
  69.7 13.0 %all-to-all-start.2 = ((f32[256,1,128]{2,1,0:T(1,128)}), f32[256,1,128]{2,1,0:T(1,128)S(1)}, u32[]{:S(2)}, u32[]{:S(2)}) async-start(f32[256,1,128]{2,1,0:T(1,128)} %bitcast.5), calls=%async_computation.2 | async-start | bytes 262144 | tf_op jit(solution)/shard_map/all_to_all | solution.py:688
  82.7 1.4 %rejoin.1 = f32[8,16,1440]{2,1,0:T(8,128)} custom-call(f32[8,12,16,128]{3,2,1,0:T(8,128)S(1)} %all_to_all.21.field_ref), custom_call_target="tpu_custom_call" | custom-call | flops 2000000000 | bytes 2000000 | tf_op jit(solution)/shard_map/rejoin/pallas_call | solution.py:546
  84.1 11.6 %all-to-all-done.2 = f32[256,1,128]{2,1,0:T(1,128)S(1)} async-done(((f32[256,1,128]{2,1,0:T(1,128)}), f32[256,1,128]{2,1,0:T(1,128)S(1)}, u32[]{:S(2)}, u32[]{:S(2)}) %all-to-all-start.2) | async-done | bytes 131104 | tf_op jit(solution)/shard_map/all_to_all | solution.py:688
  95.7 1.0 %owners.1 = f32[16,64]{1,0:T(8,128)} custom-call(f32[256,128]{1,0:T(8,128)S(1)} %bitcast.11), custom_call_target="tpu_custom_call" | custom-call | tf_op jit(solution)/shard_map/owners/pallas_call | solution.py:632
  (42 shorter events, 3.6 us)
Async XLA Ops:
  0.6 9.0 %copy-start.2 = (f32[8,16,1440]{2,1,0:T(8,128)S(1)}, f32[8,16,1440]{2,1,0:T(8,128)}, u32[]{:S(2)}) copy-start(f32[8,16,1440]{2,1,0:T(8,128)} %a_ref.1) | copy-start | bytes 2211844
  0.6 9.0 %copy-start.3 = (f32[8,16,1440]{2,1,0:T(8,128)S(1)}, f32[8,16,1440]{2,1,0:T(8,128)}, u32[]{:S(2)}) copy-start(f32[8,16,1440]{2,1,0:T(8,128)} %clat_ref.3) | copy-start | bytes 2211844
  0.6 9.0 %copy-start.4 = (s32[8,16,1440]{2,1,0:T(8,128)S(1)}, s32[8,16,1440]{2,1,0:T(8,128)}, u32[]{:S(2)}) copy-start(s32[8,16,1440]{2,1,0:T(8,128)} %klat_ref.3) | copy-start | bytes 2211844
  2.7 12.1 %collective-permute-start = (f32[5,8,1440]{2,1,0:T(8,128)}, f32[5,8,1440]{2,1,0:T(8,128)S(1)}, u32[]{:S(2)}, u32[]{:S(2)}) collective-permute-start(f32[5,8,1440]{2,1,0:T(8,128)} %get-tuple-element.18), channel_id=1, source_target_pairs={{0,8},{8,16},{16,24},{24,32},{32,40},{40,48},{48,56},{56,64},{64,7... | collective-permute-start | bytes 691208 | tf_op jit(solution)/shard_map/ppermute | solution.py:646
  7.6 7.2 %collective-permute-start.1 = (f32[4,8,1440]{2,1,0:T(8,128)}, f32[4,8,1440]{2,1,0:T(8,128)S(1)}, u32[]{:S(2)}, u32[]{:S(2)}) collective-permute-start(f32[4,8,1440]{2,1,0:T(8,128)} %get-tuple-element.19), channel_id=1, source_target_pairs={{8,0},{16,8},{24,16},{32,24},{40,32},{48,40},{56,48},{64,56},{72,6... | collective-permute-start | bytes 552968 | tf_op jit(solution)/shard_map/ppermute | solution.py:646
  9.6 1.3 %copy-start.5 = (f32[8,16,1440]{2,1,0:T(8,128)S(1)}, f32[8,16,1440]{2,1,0:T(8,128)}, u32[]{:S(2)}) copy-start(f32[8,16,1440]{2,1,0:T(8,128)} %clon_ref.3) | copy-start | bytes 2211844
  9.6 1.4 %copy-start.6 = (s32[8,16,1440]{2,1,0:T(8,128)S(1)}, s32[8,16,1440]{2,1,0:T(8,128)}, u32[]{:S(2)}) copy-start(s32[8,16,1440]{2,1,0:T(8,128)} %klon_ref.3) | copy-start | bytes 2211844
  15.3 7.2 %collective-permute-start.2 = (f32[2,8,1440]{2,1,0:T(8,128)S(1)}, f32[2,8,1440]{2,1,0:T(8,128)S(1)}, u32[]{:S(2)}, u32[]{:S(2)}) collective-permute-start(f32[2,8,1440]{2,1,0:T(8,128)S(1)} %get-tuple-element.25.up_ref.refs_2_), channel_id=1, source_target_pairs={{0,8},{8,16},{16,24},{24,32},{32,40},{40,48},{48,56},{56,64},{64,7... | collective-permute-start | bytes 276488 | tf_op jit(solution)/shard_map/ppermute | solution.py:646
  17.7 5.9 %collective-permute-start.3 = (f32[2,8,1440]{2,1,0:T(8,128)S(1)}, f32[2,8,1440]{2,1,0:T(8,128)S(1)}, u32[]{:S(2)}, u32[]{:S(2)}) collective-permute-start(f32[2,8,1440]{2,1,0:T(8,128)S(1)} %get-tuple-element.26.down_ref.refs_3_), channel_id=1, source_target_pairs={{8,0},{16,8},{24,16},{32,24},{40,32},{48,40},{56,48},{64,56},{72,6... | collective-permute-start | bytes 276488 | tf_op jit(solution)/shard_map/ppermute | solution.py:646
  25.3 6.8 %copy-start.19 = (s32[2000]{0:T(1024)S(1)}, s32[2000]{0:T(1024)}, u32[]{:S(2)}) copy-start(s32[2000]{0:T(1024)} %param.23) | copy-start | bytes 24004
  25.3 6.8 %copy-start.7 = (f32[16,4,16,16]{3,2,1,0:T(8,128)S(1)}, f32[16,4,16,16]{3,2,1,0:T(8,128)}, u32[]{:S(2)}) copy-start(f32[16,4,16,16]{3,2,1,0:T(8,128)} %inverse_ref.1) | copy-start | bytes 196612
  25.3 6.8 %copy-start.10 = (s32[16,1440]{1,0:T(8,128)S(1)}, s32[16,1440]{1,0:T(8,128)}, u32[]{:S(2)}) copy-start(s32[16,1440]{1,0:T(8,128)} %ids_ref.1) | copy-start | bytes 276484
  25.3 20.5 %all-to-all-start = ((f32[8,12,16,128]{3,2,1,0:T(8,128)}), f32[8,12,16,128]{3,2,1,0:T(8,128)S(1)}, u32[]{:S(2)}, u32[]{:S(2)}) async-start(f32[8,12,16,128]{3,2,1,0:T(8,128)} %edges.3), calls=%async_computation | async-start | bytes 1572864 | tf_op jit(solution)/shard_map/all_to_all | solution.py:683
  32.1 1.0 %copy-start.8 = (f32[16,3,16,16]{3,2,1,0:T(8,128)S(1)}, f32[16,3,16,16]{3,2,1,0:T(8,128)}, u32[]{:S(2)}) copy-start(f32[16,3,16,16]{3,2,1,0:T(8,128)} %lower_ref.1) | copy-start | bytes 147460
  33.1 1.0 %copy-start.9 = (f32[16,3,16,16]{3,2,1,0:T(8,128)S(1)}, f32[16,3,16,16]{3,2,1,0:T(8,128)}, u32[]{:S(2)}) copy-start(f32[16,3,16,16]{3,2,1,0:T(8,128)} %upper_ref.1) | copy-start | bytes 147460
  34.1 11.7 %copy-start = (f32[64,16,180]{2,1,0:T(8,128)S(1)}, f32[64,16,180]{2,1,0:T(8,128)}, u32[]{:S(2)}) copy-start(f32[64,16,180]{2,1,0:T(8,128)} %c_ref.1) | copy-start | bytes 2211844
  34.1 11.7 %copy-start.1 = (s32[64,16,180]{2,1,0:T(8,128)S(1)}, s32[64,16,180]{2,1,0:T(8,128)}, u32[]{:S(2)}) copy-start(s32[64,16,180]{2,1,0:T(8,128)} %k_ref.1) | copy-start | bytes 2211844
  38.8 0.9 copy-start.11
  39.7 0.8 copy-start.13
  45.8 1.0 %copy-start.14 = (bf16[16,64,192]{2,1,0:T(8,128)(2,1)S(1)}, bf16[16,64,192]{2,1,0:T(8,128)(2,1)}, u32[]{:S(2)}) copy-start(bf16[16,64,192]{2,1,0:T(8,128)(2,1)} %copy-done.13) | copy-start | bytes 1179652
  48.5 16.1 %copy-start.12 = (f32[1536,16]{1,0:T(8,128)S(1)}, f32[1536,16]{1,0:T(8,128)}, u32[]{:S(2)}) copy-start(f32[1536,16]{1,0:T(8,128)} %copy-done.11) | copy-start | bytes 294916
  48.5 16.1 %copy-start.16 = (f32[256,8]{1,0:T(8,128)S(1)}, f32[256,8]{1,0:T(8,128)}, u32[]{:S(2)}) copy-start(f32[256,8]{1,0:T(8,128)} %copy-done.15) | copy-start | bytes 24580
  48.5 16.1 %copy-start.18 = (f32[16,1536]{1,0:T(8,128)S(1)}, f32[16,1536]{1,0:T(8,128)}, u32[]{:S(2)}) copy-start(f32[16,1536]{1,0:T(8,128)} %copy-done.17) | copy-start | bytes 294916
  69.7 26.0 %all-to-all-start.2 = ((f32[256,1,128]{2,1,0:T(1,128)}), f32[256,1,128]{2,1,0:T(1,128)S(1)}, u32[]{:S(2)}, u32[]{:S(2)}) async-start(f32[256,1,128]{2,1,0:T(1,128)} %bitcast.5), calls=%async_computation.2 | async-start | bytes 262144 | tf_op jit(solution)/shard_map/all_to_all | solution.py:688
  (2 other events, 1.3 us)

commit v6 on v5

--- a/solution.py
+++ b/solution.py
@@ -438,7 +438,7 @@
         ),
         in_specs=[VMEM] * 5,
         out_specs=(VMEM,) * 5,
-        compiler_params=params(),
+        compiler_params=params(60),
         cost_estimate=cost(5),
         name="prep",
     )(inverse, lower, upper, owner_tiles, ids)

time: 97.2 us -> 96.4 us (level)
  local copies, waits for them, and re-layouts: 6.18 us -> 1.79 us
  Pallas kernels: 24.7 us -> 27 us
  waiting for transfers between devices: 17.9 us -> 20.1 us
    unnamed x40 -> x26, local copies, waits for them, and re-layouts: 6.17 us -> 1.19 us
    pallas_call x1, Pallas kernels: 4.69 us -> 6.98 us  [prep(): pl.pallas_call(functools.partial(prep_kernel, devices=devices, parts=part...]
    all_to_all x1, waiting for transfers between devices: 3.98 us -> 6.13 us  [local(): lax.all_to_all(sent, 'lev', split_axis=0, concat_axis=0, tiled=True)]
  transfers between devices with their start and end apart: 6 -> 6, of which waited for: 4 -> 4; matrix products, arithmetic and copies ran while one was open for 0% -> 1% of each run, Pallas kernels for 13% -> 16%
where the time goes in v6:
time: 96.4 us; the launch traced here: 96 us
  starting transfers between devices  30.2 us (31%)
  Pallas kernels  27 us (28%)
  waiting for transfers between devices  20.1 us (21%)
  blocking collectives  16.1 us (17%)
  local copies, waits for them, and re-layouts  1.79 us (2%)
    all_to_all x1, blocking collectives, local(): lax.all_to_all(columns.reshape(sent.shape), 'lev', split_axis=0, concat_a...  16.1 us
    all_to_all x1, starting transfers between devices, local(): lax.all_to_all(rows, ('lat', 'lev'), split_axis=0, concat_axis=0, tiled=T...  12.2 us
    all_to_all x1, waiting for transfers between devices, local(): lax.all_to_all(rows, ('lat', 'lev'), split_axis=0, concat_axis=0, tiled=T...  11.6 us
    ppermute x2, starting transfers between devices, neighbours(): lax.ppermute(up, 'lat', forward)  7.31 us
    pallas_call x1, Pallas kernels, prep(): pl.pallas_call(functools.partial(prep_kernel, devices=devices, parts=part...  6.98 us
    all_to_all x1, starting transfers between devices, local(): lax.all_to_all(sent, 'lev', split_axis=0, concat_axis=0, tiled=True)  6.78 us
    all_to_all x1, waiting for transfers between devices, local(): lax.all_to_all(sent, 'lev', split_axis=0, concat_axis=0, tiled=True)  6.13 us
    pallas_call x1, Pallas kernels, regions(): pl.pallas_call(functools.partial(region_kernel, levels=levels, scale=scal...  5.02 us
  transfers between devices with their start and end apart: 6, of which 4 were waited for; matrix products, arithmetic and copies ran while one was open for 1% of the time, Pallas kernels for 16%

profile of v6, /device:TPU:1, one launch (start us, length us, event | category | flops | bytes accessed | tf_op | source)
XLA Modules:
  0.0 96.0 jit_solution(7395533100882076330)
XLA Ops:
  0.7 2.0 %pack.1 = (f32[5,8,1440]{2,1,0:T(8,128)}, f32[4,8,1440]{2,1,0:T(8,128)}) custom-call(f32[8,16,1440]{2,1,0:T(8,128)} %a_ref.1, f32[8,16,1440]{2,1,0:T(8,128)} %clat_ref.3, s32[8,16,1440]{2,1,0:T(8,128)} %klat_ref.3), custom_call_target="tpu_custom_call" | custom-call | flops 2000000000 | bytes 2000000 | tf_op jit(solution)/shard_map/pack/pallas_call | solution.py:358
  2.7 4.9 %collective-permute-start = (f32[5,8,1440]{2,1,0:T(8,128)}, f32[5,8,1440]{2,1,0:T(8,128)S(1)}, u32[]{:S(2)}, u32[]{:S(2)}) collective-permute-start(f32[5,8,1440]{2,1,0:T(8,128)} %get-tuple-element.18), channel_id=1, source_target_pairs={{0,8},{8,16},{16,24},{24,32},{32,40},{40,48},{48,56},{56,64},{64,7... | collective-permute-start | bytes 691208 | tf_op jit(solution)/shard_map/ppermute | solution.py:646
  7.7 1.9 %collective-permute-start.1 = (f32[4,8,1440]{2,1,0:T(8,128)}, f32[4,8,1440]{2,1,0:T(8,128)S(1)}, u32[]{:S(2)}, u32[]{:S(2)}) collective-permute-start(f32[4,8,1440]{2,1,0:T(8,128)} %get-tuple-element.19), channel_id=1, source_target_pairs={{8,0},{16,8},{24,16},{32,24},{40,32},{48,40},{56,48},{64,56},{72,6... | collective-permute-start | bytes 552968 | tf_op jit(solution)/shard_map/ppermute | solution.py:646
  9.6 1.2 %first_lat.1 = (f32[8,16,1440]{2,1,0:T(8,128)S(1)}, f32[4,8,1440]{2,1,0:T(8,128)S(1)}, f32[7,8,1440]{2,1,0:T(8,128)S(1)}) custom-call(s32[1]{0:T(128)} %bitcast.last_ref, f32[8,16,1440]{2,1,0:T(8,128)S(1)} %copy-done.2, f32[8,16,1440]{2,1,0:T(8,128)S(1)} %copy-done.3, s32[8,16,1440]{2,1,0:T(8,128)S(1)} %copy-done.4), custom_call_target="tpu_custom_call" | custom-call | flops 2000000000 | bytes 2000000 | tf_op jit(solution)/shard_map/first_lat/pallas_call | solution.py:132
  11.0 2.6 %first_lon.1 = (f32[8,16,1440]{2,1,0:T(8,128)S(1)}, f32[4,6,8,1536]{3,2,1,0:T(8,128)S(1)}) custom-call(f32[8,16,1440]{2,1,0:T(8,128)S(1)} %get-tuple-element.21.rows_ref, f32[8,16,1440]{2,1,0:T(8,128)S(1)} %copy-done.5, s32[8,16,1440]{2,1,0:T(8,128)S(1)} %copy-done.6), custom_call_target="tpu_custom_call" | custom-call | flops 2000000000 | bytes 2000000 | tf_op jit(solution)/shard_map/first_lon/pallas_call | solution.py:170
  13.6 1.3 %collective-permute-done.1.above_ref = f32[4,8,1440]{2,1,0:T(8,128)S(1)} collective-permute-done((f32[4,8,1440]{2,1,0:T(8,128)}, f32[4,8,1440]{2,1,0:T(8,128)S(1)}, u32[]{:S(2)}, u32[]{:S(2)}) %collective-permute-start.1) | collective-permute-done | bytes 184352 | tf_op jit(solution)/shard_map/ppermute | solution.py:646
  14.9 0.4 edges.2
  15.3 2.4 %collective-permute-start.2 = (f32[2,8,1440]{2,1,0:T(8,128)S(1)}, f32[2,8,1440]{2,1,0:T(8,128)S(1)}, u32[]{:S(2)}, u32[]{:S(2)}) collective-permute-start(f32[2,8,1440]{2,1,0:T(8,128)S(1)} %get-tuple-element.25.up_ref.refs_2_), channel_id=1, source_target_pairs={{0,8},{8,16},{16,24},{24,32},{32,40},{40,48},{48,56},{56,64},{64,7... | collective-permute-start | bytes 276488 | tf_op jit(solution)/shard_map/ppermute | solution.py:646
  17.7 2.0 %collective-permute-start.3 = (f32[2,8,1440]{2,1,0:T(8,128)S(1)}, f32[2,8,1440]{2,1,0:T(8,128)S(1)}, u32[]{:S(2)}, u32[]{:S(2)}) collective-permute-start(f32[2,8,1440]{2,1,0:T(8,128)S(1)} %get-tuple-element.26.down_ref.refs_3_), channel_id=1, source_target_pairs={{8,0},{16,8},{24,16},{32,24},{40,32},{48,40},{56,48},{64,56},{72,6... | collective-permute-start | bytes 276488 | tf_op jit(solution)/shard_map/ppermute | solution.py:646
  19.7 2.9 %interior.1 = (f32[8,12,16,128]{3,2,1,0:T(8,128)S(1)}, f32[4,8,1440]{2,1,0:T(8,128)S(1)}) custom-call(s32[1]{0:T(128)} %bitcast.last_ref, f32[8,16,1440]{2,1,0:T(8,128)S(1)} %get-tuple-element.23.a_ref, f32[2,8,1440]{2,1,0:T(8,128)S(1)} %get-tuple-element.25.up_ref.refs_2_, f32[2,8,1440]{2,1,0:T(8,128)S(1)} %get-tuple-element.26.down_ref.refs_3_, ...), custom_call_target="tpu_custom_call" | custom-call | flops 4000000000 | bytes 4000000 | tf_op jit(solution)/shard_map/interior/pallas_call | solution.py:228
  22.6 1.1 %collective-permute-done.3.refs_1_ = f32[2,8,1440]{2,1,0:T(8,128)S(1)} collective-permute-done((f32[2,8,1440]{2,1,0:T(8,128)S(1)}, f32[2,8,1440]{2,1,0:T(8,128)S(1)}, u32[]{:S(2)}, u32[]{:S(2)}) %collective-permute-start.3) | collective-permute-done | bytes 92192 | tf_op jit(solution)/shard_map/ppermute | solution.py:646
  23.6 1.7 %edges.3 = f32[8,12,16,128]{3,2,1,0:T(8,128)} custom-call(f32[5,8,1440]{2,1,0:T(8,128)S(1)} %collective-permute-done.below_ref, f32[4,8,1440]{2,1,0:T(8,128)S(1)} %collective-permute-done.1.above_ref, f32[7,8,1440]{2,1,0:T(8,128)S(1)} %get-tuple-element.20.edge_ref, f32[4,6,8,1536]{3,2,1,0:T(8,128)S(1)} %get-tuple-element.22.lonc_ref, ...), custom_call_target="tpu_custom_call" | custom-call | flops 1000000000 | bytes 1000000 | tf_op jit(solution)/shard_map/edges/pallas_call | solution.py:321
  25.3 6.8 %all-to-all-start = ((f32[8,12,16,128]{3,2,1,0:T(8,128)}), f32[8,12,16,128]{3,2,1,0:T(8,128)S(1)}, u32[]{:S(2)}, u32[]{:S(2)}) async-start(f32[8,12,16,128]{3,2,1,0:T(8,128)} %edges.3), calls=%async_computation | async-start | bytes 1572864 | tf_op jit(solution)/shard_map/all_to_all | solution.py:683
  32.1 0.6 reshape.26.owner_ref
  32.7 7.0 %prep.1 = (bf16[16,64,192]{2,1,0:T(8,128)(2,1)}, s32[8,256]{1,0:T(8,128)}, f32[16,1536]{1,0:T(8,128)}, f32[1536,16]{1,0:T(8,128)}, f32[256,8]{1,0:T(8,128)}) custom-call(f32[16,4,16,16]{3,2,1,0:T(8,128)} %inverse_ref.1, f32[16,3,16,16]{3,2,1,0:T(8,128)} %lower_ref.1, f32[16,3,16,16]{3,2,1,0:T(8,128)} %upper_ref.1, s32[8,256]{1,0:T(8,128)} %reshape.26.owner_ref, ...), custom_call_target="tpu_custom_call" | custom-call | flops 5000000000 | bytes 5000000 | tf_op jit(solution)/shard_map/prep/pallas_call | solution.py:430
  39.7 6.1 %all-to-all-done = f32[8,12,16,128]{3,2,1,0:T(8,128)S(1)} async-done(((f32[8,12,16,128]{3,2,1,0:T(8,128)}), f32[8,12,16,128]{3,2,1,0:T(8,128)S(1)}, u32[]{:S(2)}, u32[]{:S(2)}) %all-to-all-start) | async-done | bytes 786464 | tf_op jit(solution)/shard_map/all_to_all | solution.py:683
  45.8 1.0 %copy-done.8 = bf16[16,64,192]{2,1,0:T(8,128)(2,1)S(1)} copy-done((bf16[16,64,192]{2,1,0:T(8,128)(2,1)S(1)}, bf16[16,64,192]{2,1,0:T(8,128)(2,1)}, u32[]{:S(2)}) %copy-start.8) | copy-done | bytes 393240
  46.9 1.6 %vertical.1 = f32[1536,128]{1,0:T(8,128)S(1)} custom-call(f32[1536,128]{1,0:T(8,128)S(1)} %bitcast.8, bf16[16,64,192]{2,1,0:T(8,128)(2,1)S(1)} %copy-done.8, f32[64,16,180]{2,1,0:T(8,128)S(1)} %copy-done, s32[64,16,180]{2,1,0:T(8,128)S(1)} %copy-done.1), custom_call_target="tpu_custom_call" | custom-call | flops 5000000000 | bytes 5000000 | tf_op jit(solution)/shard_map/vertical/pallas_call | solution.py:518
  48.5 16.1 %all_to_all.21.field_ref = f32[8,12,16,128]{3,2,1,0:T(8,128)S(1)} all-to-all(f32[8,12,16,128]{3,2,1,0:T(8,128)S(1)} %bitcast.10), channel_id=1, replica_groups=mesh['lat'=32,'lev'=8] {'lev'}, dimensions={0} | all-to-all | bytes 1572864 | tf_op jit(solution)/shard_map/all_to_all | solution.py:685
  64.7 5.0 %regions.1 = f32[256,128]{1,0:T(8,128)} custom-call(f32[1536,128]{1,0:T(8,128)S(1)} %bitcast.9, f32[16,1536]{1,0:T(8,128)S(1)} %copy-done.10, f32[1536,16]{1,0:T(8,128)S(1)} %copy-done.7, f32[256,8]{1,0:T(8,128)S(1)} %copy-done.9, s32[8,256]{1,0:T(8,128)S(1)} %copy-done.11), custom_call_target="tpu_custom_call" | custom-call | flops 6000000000 | bytes 6000000 | tf_op jit(solution)/shard_map/regions/pallas_call | solution.py:601
  69.7 12.2 %all-to-all-start.2 = ((f32[256,1,128]{2,1,0:T(1,128)}), f32[256,1,128]{2,1,0:T(1,128)S(1)}, u32[]{:S(2)}, u32[]{:S(2)}) async-start(f32[256,1,128]{2,1,0:T(1,128)} %bitcast.5), calls=%async_computation.2 | async-start | bytes 262144 | tf_op jit(solution)/shard_map/all_to_all | solution.py:688
  81.9 1.4 %rejoin.1 = f32[8,16,1440]{2,1,0:T(8,128)} custom-call(f32[8,12,16,128]{3,2,1,0:T(8,128)S(1)} %all_to_all.21.field_ref), custom_call_target="tpu_custom_call" | custom-call | flops 2000000000 | bytes 2000000 | tf_op jit(solution)/shard_map/rejoin/pallas_call | solution.py:546
  83.4 11.6 %all-to-all-done.2 = f32[256,1,128]{2,1,0:T(1,128)S(1)} async-done(((f32[256,1,128]{2,1,0:T(1,128)}), f32[256,1,128]{2,1,0:T(1,128)S(1)}, u32[]{:S(2)}, u32[]{:S(2)}) %all-to-all-start.2) | async-done | bytes 131104 | tf_op jit(solution)/shard_map/all_to_all | solution.py:688
  94.9 1.0 %owners.1 = f32[16,64]{1,0:T(8,128)} custom-call(f32[256,128]{1,0:T(8,128)S(1)} %bitcast.11), custom_call_target="tpu_custom_call" | custom-call | tf_op jit(solution)/shard_map/owners/pallas_call | solution.py:632
  (28 shorter events, 0.2 us)
Async XLA Ops:
  0.6 9.0 %copy-start.2 = (f32[8,16,1440]{2,1,0:T(8,128)S(1)}, f32[8,16,1440]{2,1,0:T(8,128)}, u32[]{:S(2)}) copy-start(f32[8,16,1440]{2,1,0:T(8,128)} %a_ref.1) | copy-start | bytes 2211844
  0.6 9.0 %copy-start.3 = (f32[8,16,1440]{2,1,0:T(8,128)S(1)}, f32[8,16,1440]{2,1,0:T(8,128)}, u32[]{:S(2)}) copy-start(f32[8,16,1440]{2,1,0:T(8,128)} %clat_ref.3) | copy-start | bytes 2211844
  0.6 9.0 %copy-start.4 = (s32[8,16,1440]{2,1,0:T(8,128)S(1)}, s32[8,16,1440]{2,1,0:T(8,128)}, u32[]{:S(2)}) copy-start(s32[8,16,1440]{2,1,0:T(8,128)} %klat_ref.3) | copy-start | bytes 2211844
  2.7 12.1 %collective-permute-start = (f32[5,8,1440]{2,1,0:T(8,128)}, f32[5,8,1440]{2,1,0:T(8,128)S(1)}, u32[]{:S(2)}, u32[]{:S(2)}) collective-permute-start(f32[5,8,1440]{2,1,0:T(8,128)} %get-tuple-element.18), channel_id=1, source_target_pairs={{0,8},{8,16},{16,24},{24,32},{32,40},{40,48},{48,56},{56,64},{64,7... | collective-permute-start | bytes 691208 | tf_op jit(solution)/shard_map/ppermute | solution.py:646
  7.7 7.2 %collective-permute-start.1 = (f32[4,8,1440]{2,1,0:T(8,128)}, f32[4,8,1440]{2,1,0:T(8,128)S(1)}, u32[]{:S(2)}, u32[]{:S(2)}) collective-permute-start(f32[4,8,1440]{2,1,0:T(8,128)} %get-tuple-element.19), channel_id=1, source_target_pairs={{8,0},{16,8},{24,16},{32,24},{40,32},{48,40},{56,48},{64,56},{72,6... | collective-permute-start | bytes 552968 | tf_op jit(solution)/shard_map/ppermute | solution.py:646
  9.6 1.3 %copy-start.5 = (f32[8,16,1440]{2,1,0:T(8,128)S(1)}, f32[8,16,1440]{2,1,0:T(8,128)}, u32[]{:S(2)}) copy-start(f32[8,16,1440]{2,1,0:T(8,128)} %clon_ref.3) | copy-start | bytes 2211844
  9.6 1.4 %copy-start.6 = (s32[8,16,1440]{2,1,0:T(8,128)S(1)}, s32[8,16,1440]{2,1,0:T(8,128)}, u32[]{:S(2)}) copy-start(s32[8,16,1440]{2,1,0:T(8,128)} %klon_ref.3) | copy-start | bytes 2211844
  15.3 7.2 %collective-permute-start.2 = (f32[2,8,1440]{2,1,0:T(8,128)S(1)}, f32[2,8,1440]{2,1,0:T(8,128)S(1)}, u32[]{:S(2)}, u32[]{:S(2)}) collective-permute-start(f32[2,8,1440]{2,1,0:T(8,128)S(1)} %get-tuple-element.25.up_ref.refs_2_), channel_id=1, source_target_pairs={{0,8},{8,16},{16,24},{24,32},{32,40},{40,48},{48,56},{56,64},{64,7... | collective-permute-start | bytes 276488 | tf_op jit(solution)/shard_map/ppermute | solution.py:646
  17.7 5.9 %collective-permute-start.3 = (f32[2,8,1440]{2,1,0:T(8,128)S(1)}, f32[2,8,1440]{2,1,0:T(8,128)S(1)}, u32[]{:S(2)}, u32[]{:S(2)}) collective-permute-start(f32[2,8,1440]{2,1,0:T(8,128)S(1)} %get-tuple-element.26.down_ref.refs_3_), channel_id=1, source_target_pairs={{8,0},{16,8},{24,16},{32,24},{40,32},{48,40},{56,48},{64,56},{72,6... | collective-permute-start | bytes 276488 | tf_op jit(solution)/shard_map/ppermute | solution.py:646
  25.3 6.8 %copy-start.12 = (s32[2000]{0:T(1024)S(1)}, s32[2000]{0:T(1024)}, u32[]{:S(2)}) copy-start(s32[2000]{0:T(1024)} %param.23) | copy-start | bytes 24004
  25.3 20.5 %all-to-all-start = ((f32[8,12,16,128]{3,2,1,0:T(8,128)}), f32[8,12,16,128]{3,2,1,0:T(8,128)S(1)}, u32[]{:S(2)}, u32[]{:S(2)}) async-start(f32[8,12,16,128]{3,2,1,0:T(8,128)} %edges.3), calls=%async_computation | async-start | bytes 1572864 | tf_op jit(solution)/shard_map/all_to_all | solution.py:683
  32.7 13.1 %copy-start = (f32[64,16,180]{2,1,0:T(8,128)S(1)}, f32[64,16,180]{2,1,0:T(8,128)}, u32[]{:S(2)}) copy-start(f32[64,16,180]{2,1,0:T(8,128)} %c_ref.1) | copy-start | bytes 2211844
  32.7 13.1 %copy-start.1 = (s32[64,16,180]{2,1,0:T(8,128)S(1)}, s32[64,16,180]{2,1,0:T(8,128)}, u32[]{:S(2)}) copy-start(s32[64,16,180]{2,1,0:T(8,128)} %k_ref.1) | copy-start | bytes 2211844
  45.8 1.0 %copy-start.8 = (bf16[16,64,192]{2,1,0:T(8,128)(2,1)S(1)}, bf16[16,64,192]{2,1,0:T(8,128)(2,1)}, u32[]{:S(2)}) copy-start(bf16[16,64,192]{2,1,0:T(8,128)(2,1)} %get-tuple-element.29.matrix_ref) | copy-start | bytes 1179652
  48.5 16.1 %copy-start.7 = (f32[1536,16]{1,0:T(8,128)S(1)}, f32[1536,16]{1,0:T(8,128)}, u32[]{:S(2)}) copy-start(f32[1536,16]{1,0:T(8,128)} %get-tuple-element.31.fine_ref) | copy-start | bytes 294916
  48.5 16.1 %copy-start.9 = (f32[256,8]{1,0:T(8,128)S(1)}, f32[256,8]{1,0:T(8,128)}, u32[]{:S(2)}) copy-start(f32[256,8]{1,0:T(8,128)} %get-tuple-element.32.device_ref) | copy-start | bytes 24580
  48.5 16.1 %copy-start.10 = (f32[16,1536]{1,0:T(8,128)S(1)}, f32[16,1536]{1,0:T(8,128)}, u32[]{:S(2)}) copy-start(f32[16,1536]{1,0:T(8,128)} %get-tuple-element.30.coarse_ref) | copy-start | bytes 294916
  48.5 16.1 %copy-start.11 = (s32[8,256]{1,0:T(8,128)S(1)}, s32[8,256]{1,0:T(8,128)}, u32[]{:S(2)}) copy-start(s32[8,256]{1,0:T(8,128)} %get-tuple-element.33.slot_ref) | copy-start | bytes 24580
  69.7 25.2 %all-to-all-start.2 = ((f32[256,1,128]{2,1,0:T(1,128)}), f32[256,1,128]{2,1,0:T(1,128)S(1)}, u32[]{:S(2)}, u32[]{:S(2)}) async-start(f32[256,1,128]{2,1,0:T(1,128)} %bitcast.5), calls=%async_computation.2 | async-start | bytes 262144 | tf_op jit(solution)/shard_map/all_to_all | solution.py:688

commit v7 on v6

--- a/solution.py
+++ b/solution.py
@@ -624,8 +624,9 @@
     spread = jnp.concatenate([jnp.where(mine, total[j : j + 1], 0.0) for j in range(groups)], axis=1)
     row = lax.broadcasted_iota(jnp.int32, (groups * lanes, width), 0)
     col = lax.broadcasted_iota(jnp.int32, (groups * lanes, width), 1)
-    fold = jnp.where(col == row // lanes * levels + row % levels, 1.0, 0.0)
-    out_ref[...] = jnp.dot(spread, fold, precision=lax.Precision.HIGHEST, preferred_element_type=F32)
+    fold = jnp.where(col == row // lanes * levels + row % levels, 1.0, 0.0).astype(BF16)
+    high, low = split(spread)
+    out_ref[...] = jnp.dot(high, fold, preferred_element_type=F32) + jnp.dot(low, fold, preferred_element_type=F32)
 
 
 def owners(rows, groups, levels):

time: 96.4 us -> 96.3 us (level)
  no operation moved by 1% of the time
where the time goes in v7:
time: 96.3 us; the launch traced here: 95.8 us
  starting transfers between devices  30.2 us (31%)
  Pallas kernels  26.8 us (28%)
  waiting for transfers between devices  20.1 us (21%)
  blocking collectives  16.1 us (17%)
  local copies, waits for them, and re-layouts  1.79 us (2%)
    all_to_all x1, blocking collectives, local(): lax.all_to_all(columns.reshape(sent.shape), 'lev', split_axis=0, concat_a...  16.1 us
    all_to_all x1, starting transfers between devices, local(): lax.all_to_all(rows, ('lat', 'lev'), split_axis=0, concat_axis=0, tiled=T...  12.2 us
    all_to_all x1, waiting for transfers between devices, local(): lax.all_to_all(rows, ('lat', 'lev'), split_axis=0, concat_axis=0, tiled=T...  11.6 us
    ppermute x2, starting transfers between devices, neighbours(): lax.ppermute(up, 'lat', forward)  7.31 us
    pallas_call x1, Pallas kernels, prep(): pl.pallas_call(functools.partial(prep_kernel, devices=devices, parts=part...  6.98 us
    all_to_all x1, starting transfers between devices, local(): lax.all_to_all(sent, 'lev', split_axis=0, concat_axis=0, tiled=True)  6.78 us
    all_to_all x1, waiting for transfers between devices, local(): lax.all_to_all(sent, 'lev', split_axis=0, concat_axis=0, tiled=True)  6.13 us
    pallas_call x1, Pallas kernels, regions(): pl.pallas_call(functools.partial(region_kernel, levels=levels, scale=scal...  5.02 us
  transfers between devices with their start and end apart: 6, of which 4 were waited for; matrix products, arithmetic and copies ran while one was open for 1% of the time, Pallas kernels for 16%

profile of v7, /device:TPU:1, one launch (start us, length us, event | category | flops | bytes accessed | tf_op | source)
XLA Modules:
  0.0 95.8 jit_solution(5900478026062813663)
XLA Ops:
  0.7 2.0 %pack.1 = (f32[5,8,1440]{2,1,0:T(8,128)}, f32[4,8,1440]{2,1,0:T(8,128)}) custom-call(f32[8,16,1440]{2,1,0:T(8,128)} %a_ref.1, f32[8,16,1440]{2,1,0:T(8,128)} %clat_ref.3, s32[8,16,1440]{2,1,0:T(8,128)} %klat_ref.3), custom_call_target="tpu_custom_call" | custom-call | flops 2000000000 | bytes 2000000 | tf_op jit(solution)/shard_map/pack/pallas_call | solution.py:358
  2.7 4.9 %collective-permute-start = (f32[5,8,1440]{2,1,0:T(8,128)}, f32[5,8,1440]{2,1,0:T(8,128)S(1)}, u32[]{:S(2)}, u32[]{:S(2)}) collective-permute-start(f32[5,8,1440]{2,1,0:T(8,128)} %get-tuple-element.18), channel_id=1, source_target_pairs={{0,8},{8,16},{16,24},{24,32},{32,40},{40,48},{48,56},{56,64},{64,7... | collective-permute-start | bytes 691208 | tf_op jit(solution)/shard_map/ppermute | solution.py:647
  7.7 1.9 %collective-permute-start.1 = (f32[4,8,1440]{2,1,0:T(8,128)}, f32[4,8,1440]{2,1,0:T(8,128)S(1)}, u32[]{:S(2)}, u32[]{:S(2)}) collective-permute-start(f32[4,8,1440]{2,1,0:T(8,128)} %get-tuple-element.19), channel_id=1, source_target_pairs={{8,0},{16,8},{24,16},{32,24},{40,32},{48,40},{56,48},{64,56},{72,6... | collective-permute-start | bytes 552968 | tf_op jit(solution)/shard_map/ppermute | solution.py:647
  9.6 1.2 %first_lat.1 = (f32[8,16,1440]{2,1,0:T(8,128)S(1)}, f32[4,8,1440]{2,1,0:T(8,128)S(1)}, f32[7,8,1440]{2,1,0:T(8,128)S(1)}) custom-call(s32[1]{0:T(128)} %bitcast.last_ref, f32[8,16,1440]{2,1,0:T(8,128)S(1)} %copy-done.2, f32[8,16,1440]{2,1,0:T(8,128)S(1)} %copy-done.3, s32[8,16,1440]{2,1,0:T(8,128)S(1)} %copy-done.4), custom_call_target="tpu_custom_call" | custom-call | flops 2000000000 | bytes 2000000 | tf_op jit(solution)/shard_map/first_lat/pallas_call | solution.py:132
  11.0 2.6 %first_lon.1 = (f32[8,16,1440]{2,1,0:T(8,128)S(1)}, f32[4,6,8,1536]{3,2,1,0:T(8,128)S(1)}) custom-call(f32[8,16,1440]{2,1,0:T(8,128)S(1)} %get-tuple-element.21.rows_ref, f32[8,16,1440]{2,1,0:T(8,128)S(1)} %copy-done.5, s32[8,16,1440]{2,1,0:T(8,128)S(1)} %copy-done.6), custom_call_target="tpu_custom_call" | custom-call | flops 2000000000 | bytes 2000000 | tf_op jit(solution)/shard_map/first_lon/pallas_call | solution.py:170
  13.6 1.3 %collective-permute-done.1.above_ref = f32[4,8,1440]{2,1,0:T(8,128)S(1)} collective-permute-done((f32[4,8,1440]{2,1,0:T(8,128)}, f32[4,8,1440]{2,1,0:T(8,128)S(1)}, u32[]{:S(2)}, u32[]{:S(2)}) %collective-permute-start.1) | collective-permute-done | bytes 184352 | tf_op jit(solution)/shard_map/ppermute | solution.py:647
  14.9 0.4 edges.2
  15.3 2.4 %collective-permute-start.2 = (f32[2,8,1440]{2,1,0:T(8,128)S(1)}, f32[2,8,1440]{2,1,0:T(8,128)S(1)}, u32[]{:S(2)}, u32[]{:S(2)}) collective-permute-start(f32[2,8,1440]{2,1,0:T(8,128)S(1)} %get-tuple-element.25.up_ref.refs_2_), channel_id=1, source_target_pairs={{0,8},{8,16},{16,24},{24,32},{32,40},{40,48},{48,56},{56,64},{64,7... | collective-permute-start | bytes 276488 | tf_op jit(solution)/shard_map/ppermute | solution.py:647
  17.7 2.0 %collective-permute-start.3 = (f32[2,8,1440]{2,1,0:T(8,128)S(1)}, f32[2,8,1440]{2,1,0:T(8,128)S(1)}, u32[]{:S(2)}, u32[]{:S(2)}) collective-permute-start(f32[2,8,1440]{2,1,0:T(8,128)S(1)} %get-tuple-element.26.down_ref.refs_3_), channel_id=1, source_target_pairs={{8,0},{16,8},{24,16},{32,24},{40,32},{48,40},{56,48},{64,56},{72,6... | collective-permute-start | bytes 276488 | tf_op jit(solution)/shard_map/ppermute | solution.py:647
  19.7 2.9 %interior.1 = (f32[8,12,16,128]{3,2,1,0:T(8,128)S(1)}, f32[4,8,1440]{2,1,0:T(8,128)S(1)}) custom-call(s32[1]{0:T(128)} %bitcast.last_ref, f32[8,16,1440]{2,1,0:T(8,128)S(1)} %get-tuple-element.23.a_ref, f32[2,8,1440]{2,1,0:T(8,128)S(1)} %get-tuple-element.25.up_ref.refs_2_, f32[2,8,1440]{2,1,0:T(8,128)S(1)} %get-tuple-element.26.down_ref.refs_3_, ...), custom_call_target="tpu_custom_call" | custom-call | flops 4000000000 | bytes 4000000 | tf_op jit(solution)/shard_map/interior/pallas_call | solution.py:228
  22.6 1.1 %collective-permute-done.3.refs_1_ = f32[2,8,1440]{2,1,0:T(8,128)S(1)} collective-permute-done((f32[2,8,1440]{2,1,0:T(8,128)S(1)}, f32[2,8,1440]{2,1,0:T(8,128)S(1)}, u32[]{:S(2)}, u32[]{:S(2)}) %collective-permute-start.3) | collective-permute-done | bytes 92192 | tf_op jit(solution)/shard_map/ppermute | solution.py:647
  23.6 1.7 %edges.3 = f32[8,12,16,128]{3,2,1,0:T(8,128)} custom-call(f32[5,8,1440]{2,1,0:T(8,128)S(1)} %collective-permute-done.below_ref, f32[4,8,1440]{2,1,0:T(8,128)S(1)} %collective-permute-done.1.above_ref, f32[7,8,1440]{2,1,0:T(8,128)S(1)} %get-tuple-element.20.edge_ref, f32[4,6,8,1536]{3,2,1,0:T(8,128)S(1)} %get-tuple-element.22.lonc_ref, ...), custom_call_target="tpu_custom_call" | custom-call | flops 1000000000 | bytes 1000000 | tf_op jit(solution)/shard_map/edges/pallas_call | solution.py:321
  25.3 6.8 %all-to-all-start = ((f32[8,12,16,128]{3,2,1,0:T(8,128)}), f32[8,12,16,128]{3,2,1,0:T(8,128)S(1)}, u32[]{:S(2)}, u32[]{:S(2)}) async-start(f32[8,12,16,128]{3,2,1,0:T(8,128)} %edges.3), calls=%async_computation | async-start | bytes 1572864 | tf_op jit(solution)/shard_map/all_to_all | solution.py:684
  32.1 0.6 reshape.26.owner_ref
  32.7 7.0 %prep.1 = (bf16[16,64,192]{2,1,0:T(8,128)(2,1)}, s32[8,256]{1,0:T(8,128)}, f32[16,1536]{1,0:T(8,128)}, f32[1536,16]{1,0:T(8,128)}, f32[256,8]{1,0:T(8,128)}) custom-call(f32[16,4,16,16]{3,2,1,0:T(8,128)} %inverse_ref.1, f32[16,3,16,16]{3,2,1,0:T(8,128)} %lower_ref.1, f32[16,3,16,16]{3,2,1,0:T(8,128)} %upper_ref.1, s32[8,256]{1,0:T(8,128)} %reshape.26.owner_ref, ...), custom_call_target="tpu_custom_call" | custom-call | flops 5000000000 | bytes 5000000 | tf_op jit(solution)/shard_map/prep/pallas_call | solution.py:430
  39.7 6.1 %all-to-all-done = f32[8,12,16,128]{3,2,1,0:T(8,128)S(1)} async-done(((f32[8,12,16,128]{3,2,1,0:T(8,128)}), f32[8,12,16,128]{3,2,1,0:T(8,128)S(1)}, u32[]{:S(2)}, u32[]{:S(2)}) %all-to-all-start) | async-done | bytes 786464 | tf_op jit(solution)/shard_map/all_to_all | solution.py:684
  45.8 1.0 %copy-done.8 = bf16[16,64,192]{2,1,0:T(8,128)(2,1)S(1)} copy-done((bf16[16,64,192]{2,1,0:T(8,128)(2,1)S(1)}, bf16[16,64,192]{2,1,0:T(8,128)(2,1)}, u32[]{:S(2)}) %copy-start.8) | copy-done | bytes 393240
  46.9 1.6 %vertical.1 = f32[1536,128]{1,0:T(8,128)S(1)} custom-call(f32[1536,128]{1,0:T(8,128)S(1)} %bitcast.8, bf16[16,64,192]{2,1,0:T(8,128)(2,1)S(1)} %copy-done.8, f32[64,16,180]{2,1,0:T(8,128)S(1)} %copy-done, s32[64,16,180]{2,1,0:T(8,128)S(1)} %copy-done.1), custom_call_target="tpu_custom_call" | custom-call | flops 5000000000 | bytes 5000000 | tf_op jit(solution)/shard_map/vertical/pallas_call | solution.py:518
  48.5 16.1 %all_to_all.21.field_ref = f32[8,12,16,128]{3,2,1,0:T(8,128)S(1)} all-to-all(f32[8,12,16,128]{3,2,1,0:T(8,128)S(1)} %bitcast.10), channel_id=1, replica_groups=mesh['lat'=32,'lev'=8] {'lev'}, dimensions={0} | all-to-all | bytes 1572864 | tf_op jit(solution)/shard_map/all_to_all | solution.py:686
  64.7 5.0 %regions.1 = f32[256,128]{1,0:T(8,128)} custom-call(f32[1536,128]{1,0:T(8,128)S(1)} %bitcast.9, f32[16,1536]{1,0:T(8,128)S(1)} %copy-done.10, f32[1536,16]{1,0:T(8,128)S(1)} %copy-done.7, f32[256,8]{1,0:T(8,128)S(1)} %copy-done.9, s32[8,256]{1,0:T(8,128)S(1)} %copy-done.11), custom_call_target="tpu_custom_call" | custom-call | flops 6000000000 | bytes 6000000 | tf_op jit(solution)/shard_map/regions/pallas_call | solution.py:601
  69.7 12.2 %all-to-all-start.2 = ((f32[256,1,128]{2,1,0:T(1,128)}), f32[256,1,128]{2,1,0:T(1,128)S(1)}, u32[]{:S(2)}, u32[]{:S(2)}) async-start(f32[256,1,128]{2,1,0:T(1,128)} %bitcast.5), calls=%async_computation.2 | async-start | bytes 262144 | tf_op jit(solution)/shard_map/all_to_all | solution.py:689
  81.9 1.4 %rejoin.1 = f32[8,16,1440]{2,1,0:T(8,128)} custom-call(f32[8,12,16,128]{3,2,1,0:T(8,128)S(1)} %all_to_all.21.field_ref), custom_call_target="tpu_custom_call" | custom-call | flops 2000000000 | bytes 2000000 | tf_op jit(solution)/shard_map/rejoin/pallas_call | solution.py:546
  83.4 11.6 %all-to-all-done.2 = f32[256,1,128]{2,1,0:T(1,128)S(1)} async-done(((f32[256,1,128]{2,1,0:T(1,128)}), f32[256,1,128]{2,1,0:T(1,128)S(1)}, u32[]{:S(2)}, u32[]{:S(2)}) %all-to-all-start.2) | async-done | bytes 131104 | tf_op jit(solution)/shard_map/all_to_all | solution.py:689
  94.9 0.9 owners.1
  (28 shorter events, 0.2 us)
Async XLA Ops:
  0.6 9.0 %copy-start.2 = (f32[8,16,1440]{2,1,0:T(8,128)S(1)}, f32[8,16,1440]{2,1,0:T(8,128)}, u32[]{:S(2)}) copy-start(f32[8,16,1440]{2,1,0:T(8,128)} %a_ref.1) | copy-start | bytes 2211844
  0.6 9.0 %copy-start.3 = (f32[8,16,1440]{2,1,0:T(8,128)S(1)}, f32[8,16,1440]{2,1,0:T(8,128)}, u32[]{:S(2)}) copy-start(f32[8,16,1440]{2,1,0:T(8,128)} %clat_ref.3) | copy-start | bytes 2211844
  0.6 9.0 %copy-start.4 = (s32[8,16,1440]{2,1,0:T(8,128)S(1)}, s32[8,16,1440]{2,1,0:T(8,128)}, u32[]{:S(2)}) copy-start(s32[8,16,1440]{2,1,0:T(8,128)} %klat_ref.3) | copy-start | bytes 2211844
  2.7 12.1 %collective-permute-start = (f32[5,8,1440]{2,1,0:T(8,128)}, f32[5,8,1440]{2,1,0:T(8,128)S(1)}, u32[]{:S(2)}, u32[]{:S(2)}) collective-permute-start(f32[5,8,1440]{2,1,0:T(8,128)} %get-tuple-element.18), channel_id=1, source_target_pairs={{0,8},{8,16},{16,24},{24,32},{32,40},{40,48},{48,56},{56,64},{64,7... | collective-permute-start | bytes 691208 | tf_op jit(solution)/shard_map/ppermute | solution.py:647
  7.7 7.2 %collective-permute-start.1 = (f32[4,8,1440]{2,1,0:T(8,128)}, f32[4,8,1440]{2,1,0:T(8,128)S(1)}, u32[]{:S(2)}, u32[]{:S(2)}) collective-permute-start(f32[4,8,1440]{2,1,0:T(8,128)} %get-tuple-element.19), channel_id=1, source_target_pairs={{8,0},{16,8},{24,16},{32,24},{40,32},{48,40},{56,48},{64,56},{72,6... | collective-permute-start | bytes 552968 | tf_op jit(solution)/shard_map/ppermute | solution.py:647
  9.6 1.3 %copy-start.5 = (f32[8,16,1440]{2,1,0:T(8,128)S(1)}, f32[8,16,1440]{2,1,0:T(8,128)}, u32[]{:S(2)}) copy-start(f32[8,16,1440]{2,1,0:T(8,128)} %clon_ref.3) | copy-start | bytes 2211844
  9.6 1.4 %copy-start.6 = (s32[8,16,1440]{2,1,0:T(8,128)S(1)}, s32[8,16,1440]{2,1,0:T(8,128)}, u32[]{:S(2)}) copy-start(s32[8,16,1440]{2,1,0:T(8,128)} %klon_ref.3) | copy-start | bytes 2211844
  15.3 7.2 %collective-permute-start.2 = (f32[2,8,1440]{2,1,0:T(8,128)S(1)}, f32[2,8,1440]{2,1,0:T(8,128)S(1)}, u32[]{:S(2)}, u32[]{:S(2)}) collective-permute-start(f32[2,8,1440]{2,1,0:T(8,128)S(1)} %get-tuple-element.25.up_ref.refs_2_), channel_id=1, source_target_pairs={{0,8},{8,16},{16,24},{24,32},{32,40},{40,48},{48,56},{56,64},{64,7... | collective-permute-start | bytes 276488 | tf_op jit(solution)/shard_map/ppermute | solution.py:647
  17.7 5.9 %collective-permute-start.3 = (f32[2,8,1440]{2,1,0:T(8,128)S(1)}, f32[2,8,1440]{2,1,0:T(8,128)S(1)}, u32[]{:S(2)}, u32[]{:S(2)}) collective-permute-start(f32[2,8,1440]{2,1,0:T(8,128)S(1)} %get-tuple-element.26.down_ref.refs_3_), channel_id=1, source_target_pairs={{8,0},{16,8},{24,16},{32,24},{40,32},{48,40},{56,48},{64,56},{72,6... | collective-permute-start | bytes 276488 | tf_op jit(solution)/shard_map/ppermute | solution.py:647
  25.3 6.8 %copy-start.12 = (s32[2000]{0:T(1024)S(1)}, s32[2000]{0:T(1024)}, u32[]{:S(2)}) copy-start(s32[2000]{0:T(1024)} %param.23) | copy-start | bytes 24004
  25.3 20.5 %all-to-all-start = ((f32[8,12,16,128]{3,2,1,0:T(8,128)}), f32[8,12,16,128]{3,2,1,0:T(8,128)S(1)}, u32[]{:S(2)}, u32[]{:S(2)}) async-start(f32[8,12,16,128]{3,2,1,0:T(8,128)} %edges.3), calls=%async_computation | async-start | bytes 1572864 | tf_op jit(solution)/shard_map/all_to_all | solution.py:684
  32.7 13.1 %copy-start = (f32[64,16,180]{2,1,0:T(8,128)S(1)}, f32[64,16,180]{2,1,0:T(8,128)}, u32[]{:S(2)}) copy-start(f32[64,16,180]{2,1,0:T(8,128)} %c_ref.1) | copy-start | bytes 2211844
  32.7 13.1 %copy-start.1 = (s32[64,16,180]{2,1,0:T(8,128)S(1)}, s32[64,16,180]{2,1,0:T(8,128)}, u32[]{:S(2)}) copy-start(s32[64,16,180]{2,1,0:T(8,128)} %k_ref.1) | copy-start | bytes 2211844
  45.8 1.0 %copy-start.8 = (bf16[16,64,192]{2,1,0:T(8,128)(2,1)S(1)}, bf16[16,64,192]{2,1,0:T(8,128)(2,1)}, u32[]{:S(2)}) copy-start(bf16[16,64,192]{2,1,0:T(8,128)(2,1)} %get-tuple-element.29.matrix_ref) | copy-start | bytes 1179652
  48.5 16.1 %copy-start.7 = (f32[1536,16]{1,0:T(8,128)S(1)}, f32[1536,16]{1,0:T(8,128)}, u32[]{:S(2)}) copy-start(f32[1536,16]{1,0:T(8,128)} %get-tuple-element.31.fine_ref) | copy-start | bytes 294916
  48.5 16.1 %copy-start.9 = (f32[256,8]{1,0:T(8,128)S(1)}, f32[256,8]{1,0:T(8,128)}, u32[]{:S(2)}) copy-start(f32[256,8]{1,0:T(8,128)} %get-tuple-element.32.device_ref) | copy-start | bytes 24580
  48.5 16.1 %copy-start.10 = (f32[16,1536]{1,0:T(8,128)S(1)}, f32[16,1536]{1,0:T(8,128)}, u32[]{:S(2)}) copy-start(f32[16,1536]{1,0:T(8,128)} %get-tuple-element.30.coarse_ref) | copy-start | bytes 294916
  48.5 16.1 %copy-start.11 = (s32[8,256]{1,0:T(8,128)S(1)}, s32[8,256]{1,0:T(8,128)}, u32[]{:S(2)}) copy-start(s32[8,256]{1,0:T(8,128)} %get-tuple-element.33.slot_ref) | copy-start | bytes 24580
  69.7 25.2 %all-to-all-start.2 = ((f32[256,1,128]{2,1,0:T(1,128)}), f32[256,1,128]{2,1,0:T(1,128)S(1)}, u32[]{:S(2)}, u32[]{:S(2)}) async-start(f32[256,1,128]{2,1,0:T(1,128)} %bitcast.5), calls=%async_computation.2 | async-start | bytes 262144 | tf_op jit(solution)/shard_map/all_to_all | solution.py:689
